TPU v7x, 32 devices: a whole 2x2x4 slice. The times are simulated.
32 devices in a mesh: dp: 4 (over x, core), seq: 4 (over z), heads: 2 (over y).
Axes of the slice: x: 2, y: 2, z: 4, core: 2. Of those that a mesh axis runs over, the one named last changes fastest.
Arguments:
- block_input: bfloat16 [2, 4, 1024, 1536], P(None, 'dp', 'seq'), may hold values from -6 to 6
- output_grad: bfloat16 [2, 4, 1024, 1536], P(None, 'dp', 'seq'), may hold values from -6 to 6
- input_gain: bfloat16 [1536], P(('dp', 'seq')), may hold values from 0.099609375 to 1.8984375
- gate_weight: bfloat16 [1536, 3072], P(('dp', 'seq'), 'heads'), may hold values from -0.15625 to 0.15625
- value_weight: bfloat16 [1536, 3072], P(('dp', 'seq'), 'heads'), may hold values from -0.15625 to 0.15625
- state_weight: bfloat16 [1536, 256], P(('dp', 'seq')), may hold values from -0.15625 to 0.15625
- step_weight: bfloat16 [1536, 48], P(('dp', 'seq'), 'heads'), may hold values from -0.15625 to 0.15625
- out_weight: bfloat16 [3072, 1536], P('heads', ('dp', 'seq')), may hold values from -0.109375 to 0.109375
- value_taps: float32 [5, 3072], P(None, 'heads'), may hold values from -0.6 to 0.6
- state_taps: float32 [5, 256], replicated, may hold values from -0.6 to 0.6
- step_bias: float32 [48], P('heads'), may hold values from -1 to 1
- log_decay: float32 [48], P('heads'), may hold values from -10 to -3, as said below
- skip_gain: float32 [48], P('heads'), may hold values from 0.5 to 1.5
- mixer_gain: float32 [3072], P('heads'), may hold values from 0.1 to 1.9
Outputs:
- block_output: bfloat16 [2, 4, 1024, 1536], P(None, 'dp', 'seq')
- grad_input: bfloat16 [2, 4, 1024, 1536], P(None, 'dp', 'seq')
- grad_input_gain: float32 [1536], P(('dp', 'seq'))
- grad_gate_weight: float32 [1536, 3072], P(('dp', 'seq'), 'heads')
- grad_value_weight: float32 [1536, 3072], P(('dp', 'seq'), 'heads')
- grad_state_weight: float32 [1536, 256], P(('dp', 'seq'))
- grad_step_weight: float32 [1536, 48], P(('dp', 'seq'), 'heads')
- grad_out_weight: float32 [3072, 1536], P('heads', ('dp', 'seq'))
- grad_value_taps: float32 [5, 3072], P(None, 'heads')
- grad_state_taps: float32 [5, 256], replicated
- grad_step_bias: float32 [48], P('heads')
- grad_log_decay: float32 [48], P('heads')
- grad_skip_gain: float32 [48], P('heads')
- grad_mixer_gain: float32 [3072], P('heads')
Inputs may be any that keep to these rules, and one draw needn't show every extreme that they name: `log_decay`: the log of each head's decay rate.
All inputs are finite; a program needn't handle non-finite values.
Results may differ from a plain program's by a relative error of at most 0.0028.
The roundings to bfloat16 on the way count: a program that leaves them out, or rounds other values in their place, can miss the bound.
Values may be sent and summed in bfloat16 or wider, within the bound.
No kernel may reach another device: no remote copies, remote signals or barrier semaphores. Data moves between devices by JAX's collectives and lax.ppermute only.
A program may use at most 192 MiB of HBM per device.

v0:
```python
import jax
import jax.numpy as jnp
from jax import lax
from jax.sharding import PartitionSpec as P

STATE = 128
CONV = 4
MB = 2
INNER = 3072


EPS = 1e-05
HIGH = lax.Precision.HIGHEST


def shifted(block, axis, distance):
    devices = range(lax.axis_size(axis))
    route = [(i - distance, i) for i in devices if i - distance in devices]
    return lax.ppermute(block, axis, route)


def entering(x, axis, combine, identity, reverse):
    peers, index = (lax.axis_size(axis), lax.axis_index(axis))
    everything = jax.tree.map(lambda part: lax.all_gather(part, axis), x)
    start = jax.tree.map(
        lambda part, zero: jnp.broadcast_to(jnp.asarray(zero, part.dtype), part.shape), x, identity
    )

    def step(k, before):
        at = peers - 1 - k if reverse else k
        reached = at > index if reverse else at < index
        new = combine(before, jax.tree.map(lambda part: part[at], everything))
        return jax.tree.map(lambda a, b: jnp.where(reached, a, b), new, before)

    return lax.fori_loop(0, peers, step, start)


def norm_rows(values, gain):
    return values * lax.rsqrt(jnp.mean(values * values, axis=-1, keepdims=True) + EPS) * gain


def conv_silu(extended, taps):
    length = extended.shape[1] - (CONV - 1)
    total = jnp.zeros((extended.shape[0], length, extended.shape[2]), jnp.float32) + taps[CONV]
    for offset in range(CONV):
        total = total + extended[:, offset : offset + length] * taps[offset]
    return jax.nn.silu(total)


def local_parts(
    values_ext, states_ext, step_pre, value_taps, state_taps, step_bias, log_decay, skip_gain
):
    values_conv = conv_silu(values_ext, value_taps)
    states_conv = conv_silu(states_ext, state_taps)
    batch, length, channels = values_conv.shape
    heads_here = step_pre.shape[-1]
    values = values_conv.reshape(batch, length, heads_here, channels // heads_here)
    input_mat = states_conv[..., :STATE]
    output_mat = states_conv[..., STATE:]
    stepsize = jax.nn.softplus(step_pre + step_bias)
    cumulative = jnp.cumsum(-stepsize * jnp.exp(log_decay), axis=1)
    gaps = cumulative[:, :, None, :] - cumulative[:, None, :, :]
    causal = (jnp.arange(length)[:, None] >= jnp.arange(length)[None, :])[None, :, :, None]
    decays = jnp.where(causal, jnp.exp(jnp.where(causal, gaps, 0.0)), 0.0)
    scores = jnp.einsum("btn,bsn->bts", output_mat, input_mat, precision=HIGH)
    weights = decays * scores[..., None] * stepsize[:, None, :, :]
    within = (
        jnp.einsum("btsh,bshp->bthp", weights, values, precision=HIGH) + skip_gain[:, None] * values
    )
    final = cumulative[:, -1]
    ending = jnp.exp(final[:, None, :] - cumulative) * stepsize
    local_state = jnp.einsum("bth,btn,bthp->bhnp", ending, input_mat, values, precision=HIGH)
    return (within, local_state, jnp.exp(final), cumulative, output_mat)


def carried_part(cumulative, output_mat, state_in):
    return jnp.exp(cumulative)[..., None] * jnp.einsum(
        "btn,bhnp->bthp", output_mat, state_in, precision=HIGH
    )


def whole_block(
    values_ext,
    states_ext,
    step_pre,
    value_taps,
    state_taps,
    step_bias,
    log_decay,
    skip_gain,
    state_in,
):
    within, local_state, span_decay, cumulative, output_mat = local_parts(
        values_ext, states_ext, step_pre, value_taps, state_taps, step_bias, log_decay, skip_gain
    )
    result = within + carried_part(cumulative, output_mat, state_in)
    return (result.reshape(result.shape[0], result.shape[1], -1), local_state, span_decay)


def compose(earlier, later):
    return (earlier[0] * later[0], later[0][..., None, None] * earlier[1] + later[1])


def shards(
    block_input,
    output_grad,
    input_gain,
    gate_weight,
    value_weight,
    state_weight,
    step_weight,
    out_weight,
    value_taps,
    state_taps,
    step_bias,
    log_decay,
    skip_gain,
    mixer_gain,
):
    margin = CONV - 1
    width = block_input.shape[-1]
    inner_here = gate_weight.shape[1]
    state_cols = state_weight.shape[1]
    heads_here = step_weight.shape[1]
    acc_gain = jnp.zeros((width,), jnp.float32)
    acc_gate = jnp.zeros((width, inner_here), jnp.float32)
    acc_value = jnp.zeros((width, inner_here), jnp.float32)
    acc_state = jnp.zeros((width, state_cols), jnp.float32)
    acc_step = jnp.zeros((width, heads_here), jnp.float32)
    acc_out = jnp.zeros((inner_here, width), jnp.float32)
    acc_value_taps = jnp.zeros_like(value_taps)
    acc_state_taps = jnp.zeros_like(state_taps)
    acc_step_bias = jnp.zeros_like(step_bias)
    acc_log_decay = jnp.zeros_like(log_decay)
    acc_skip = jnp.zeros_like(skip_gain)
    acc_mixer_gain = jnp.zeros_like(mixer_gain)
    outputs = []
    input_grads = []
    for micro_batch in range(MB):
        weights_now = (
            lax.all_gather(input_gain, ("dp", "seq"), axis=0, tiled=True),
            lax.all_gather(gate_weight, ("dp", "seq"), axis=0, tiled=True),
            lax.all_gather(value_weight, ("dp", "seq"), axis=0, tiled=True),
            lax.all_gather(state_weight, ("dp", "seq"), axis=0, tiled=True),
            lax.all_gather(step_weight, ("dp", "seq"), axis=0, tiled=True),
            lax.all_gather(out_weight, ("dp", "seq"), axis=1, tiled=True),
        )
        gain_full, gate_full, value_full, state_full, step_full, out_full = weights_now
        tokens = block_input[micro_batch].astype(jnp.float32)
        normed = norm_rows(tokens, gain_full.astype(jnp.float32)).astype(jnp.bfloat16)
        gate_lin = jnp.einsum("btd,di->bti", normed, gate_full, preferred_element_type=jnp.float32)
        values_pre = jnp.einsum(
            "btd,di->bti", normed, value_full, preferred_element_type=jnp.float32
        )
        states_pre = jnp.einsum(
            "btd,di->bti", normed, state_full, preferred_element_type=jnp.float32
        )
        step_pre = jnp.einsum("btd,di->bti", normed, step_full, preferred_element_type=jnp.float32)
        outgoing = jnp.concatenate([values_pre[:, -margin:], states_pre[:, -margin:]], axis=2)
        incoming = shifted(outgoing, "seq", 1)
        values_ext = jnp.concatenate([incoming[..., :inner_here], values_pre], axis=1)
        states_ext = jnp.concatenate([incoming[..., inner_here:], states_pre], axis=1)
        within, local_state, span_decay, cumulative, output_mat = local_parts(
            values_ext,
            states_ext,
            step_pre,
            value_taps,
            state_taps,
            step_bias,
            log_decay,
            skip_gain,
        )
        prefix = entering(
            (span_decay, local_state),
            "seq",
            compose,
            (jnp.ones_like(span_decay), jnp.zeros_like(local_state)),
            False,
        )
        state_in = prefix[1]
        mixer = (within + carried_part(cumulative, output_mat, state_in)).reshape(gate_lin.shape)
        silu_gate = jax.nn.silu(gate_lin)
        gated = mixer * silu_gate
        total_sq = lax.psum(jnp.sum(gated * gated, axis=-1), "heads")
        inverse = lax.rsqrt(total_sq / INNER + EPS)[..., None]
        out_normed = (gated * inverse * mixer_gain).astype(jnp.bfloat16)
        partial_out = jnp.einsum(
            "bti,id->btd", out_normed, out_full, preferred_element_type=jnp.float32
        )
        branch = lax.psum(partial_out, "heads")
        outputs.append((tokens + branch).astype(jnp.bfloat16))
        weights_back = (
            lax.all_gather(input_gain, ("dp", "seq"), axis=0, tiled=True),
            lax.all_gather(gate_weight, ("dp", "seq"), axis=0, tiled=True),
            lax.all_gather(value_weight, ("dp", "seq"), axis=0, tiled=True),
            lax.all_gather(state_weight, ("dp", "seq"), axis=0, tiled=True),
            lax.all_gather(step_weight, ("dp", "seq"), axis=0, tiled=True),
            lax.all_gather(out_weight, ("dp", "seq"), axis=1, tiled=True),
        )
        gain_full, gate_full, value_full, state_full, step_full, out_full = weights_back
        grad_out = output_grad[micro_batch]
        d_out_normed = jnp.einsum(
            "btd,id->bti", grad_out, out_full, preferred_element_type=jnp.float32
        )
        acc_out = acc_out + jnp.einsum(
            "bti,btd->id", out_normed, grad_out, preferred_element_type=jnp.float32
        )
        acc_mixer_gain = acc_mixer_gain + jnp.sum(d_out_normed * gated * inverse, axis=(0, 1))
        weighted = d_out_normed * mixer_gain
        dot_total = lax.psum(jnp.sum(weighted * gated, axis=-1), "heads")
        d_gated = inverse * weighted - gated * (inverse * inverse * inverse) * (
            dot_total[..., None] / INNER
        )
        d_mixer = d_gated * silu_gate
        sigmoid_gate = jax.nn.sigmoid(gate_lin)
        d_gate_lin = d_gated * mixer * sigmoid_gate * (1.0 + gate_lin * (1.0 - sigmoid_gate))
        carry_grad = jnp.einsum(
            "bth,btn,bthp->bhnp",
            jnp.exp(cumulative),
            output_mat,
            d_mixer.reshape(within.shape),
            precision=HIGH,
        )
        suffix = entering(
            (span_decay, carry_grad),
            "seq",
            compose,
            (jnp.ones_like(span_decay), jnp.zeros_like(carry_grad)),
            True,
        )
        later_grad = suffix[1]
        d_decay = jnp.sum(later_grad * state_in, axis=(2, 3))
        ignored, pullback = jax.vjp(
            whole_block,
            values_ext,
            states_ext,
            step_pre,
            value_taps,
            state_taps,
            step_bias,
            log_decay,
            skip_gain,
            state_in,
        )
        (
            d_values_ext,
            d_states_ext,
            d_step_pre,
            g_value_taps,
            g_state_taps,
            g_step_bias,
            g_log_decay,
            g_skip,
            unused_state,
        ) = pullback((d_mixer, later_grad, d_decay))
        rim_grads = jnp.concatenate([d_values_ext[:, :margin], d_states_ext[:, :margin]], axis=2)
        returned = shifted(rim_grads, "seq", -1)
        d_values_pre = d_values_ext[:, margin:].at[:, -margin:].add(returned[..., :inner_here])
        d_states_pre = d_states_ext[:, margin:].at[:, -margin:].add(returned[..., inner_here:])
        gate_low = d_gate_lin.astype(jnp.bfloat16)
        values_low = d_values_pre.astype(jnp.bfloat16)
        step_low = d_step_pre.astype(jnp.bfloat16)
        d_normed_part = (
            jnp.einsum("bti,di->btd", gate_low, gate_full, preferred_element_type=jnp.float32)
            + jnp.einsum("bti,di->btd", values_low, value_full, preferred_element_type=jnp.float32)
            + jnp.einsum("bti,di->btd", step_low, step_full, preferred_element_type=jnp.float32)
        )
        d_normed_sum, d_states_total, state_taps_total = lax.psum(
            (d_normed_part, d_states_pre, g_state_taps), "heads"
        )
        states_low = d_states_total.astype(jnp.bfloat16)
        d_normed = d_normed_sum + jnp.einsum(
            "bti,di->btd", states_low, state_full, preferred_element_type=jnp.float32
        )
        acc_gate = acc_gate + jnp.einsum(
            "btd,bti->di", normed, gate_low, preferred_element_type=jnp.float32
        )
        acc_value = acc_value + jnp.einsum(
            "btd,bti->di", normed, values_low, preferred_element_type=jnp.float32
        )
        acc_state = acc_state + jnp.einsum(
            "btd,bti->di", normed, states_low, preferred_element_type=jnp.float32
        )
        acc_step = acc_step + jnp.einsum(
            "btd,bti->di", normed, step_low, preferred_element_type=jnp.float32
        )
        scaling = lax.rsqrt(jnp.mean(tokens * tokens, axis=-1, keepdims=True) + EPS)
        acc_gain = acc_gain + jnp.sum(d_normed * tokens * scaling, axis=(0, 1))
        pushed = d_normed * gain_full.astype(jnp.float32)
        d_tokens = scaling * pushed - tokens * (scaling * scaling * scaling) * jnp.mean(
            pushed * tokens, axis=-1, keepdims=True
        )
        input_grads.append((grad_out.astype(jnp.float32) + d_tokens).astype(jnp.bfloat16))
        acc_value_taps = acc_value_taps + g_value_taps
        acc_state_taps = acc_state_taps + state_taps_total
        acc_step_bias = acc_step_bias + g_step_bias
        acc_log_decay = acc_log_decay + g_log_decay
        acc_skip = acc_skip + g_skip
    summed = (
        lax.psum_scatter(acc_gain, ("dp", "seq"), scatter_dimension=0, tiled=True),
        lax.psum_scatter(acc_gate, ("dp", "seq"), scatter_dimension=0, tiled=True),
        lax.psum_scatter(acc_value, ("dp", "seq"), scatter_dimension=0, tiled=True),
        lax.psum_scatter(acc_state, ("dp", "seq"), scatter_dimension=0, tiled=True),
        lax.psum_scatter(acc_step, ("dp", "seq"), scatter_dimension=0, tiled=True),
        lax.psum_scatter(acc_out, ("dp", "seq"), scatter_dimension=1, tiled=True),
    )
    smalls = lax.psum(
        (acc_value_taps, acc_state_taps, acc_step_bias, acc_log_decay, acc_skip, acc_mixer_gain),
        ("dp", "seq"),
    )
    return (
        jnp.stack(outputs),
        jnp.stack(input_grads),
        summed[0],
        summed[1],
        summed[2],
        summed[3],
        summed[4],
        summed[5],
        smalls[0],
        smalls[1],
        smalls[2],
        smalls[3],
        smalls[4],
        smalls[5],
    )


def solution(mesh):
    return jax.shard_map(
        shards,
        mesh=mesh,
        in_specs=(
            P(None, "dp", "seq", None),
            P(None, "dp", "seq", None),
            P(("dp", "seq")),
            P(("dp", "seq"), "heads"),
            P(("dp", "seq"), "heads"),
            P(("dp", "seq"), None),
            P(("dp", "seq"), "heads"),
            P("heads", ("dp", "seq")),
            P(None, "heads"),
            P(),
            P("heads"),
            P("heads"),
            P("heads"),
            P("heads"),
        ),
        out_specs=(
            P(None, "dp", "seq", None),
            P(None, "dp", "seq", None),
            P(("dp", "seq")),
            P(("dp", "seq"), "heads"),
            P(("dp", "seq"), "heads"),
            P(("dp", "seq"), None),
            P(("dp", "seq"), "heads"),
            P("heads", ("dp", "seq")),
            P(None, "heads"),
            P(),
            P("heads"),
            P("heads"),
            P("heads"),
            P("heads"),
        ),
        check_vma=False,
    )
```

profile of v0, /device:TPU:8, one launch (start us, length us, event | category | flops | bytes accessed | tf_op | source)
XLA Modules:
  0.0 1298.2 jit_solution(11607242005879796517)
XLA Ops:
  12.3 30.3 %all-reduce.42 = bf16[1536]{0:T(1024)(128)(2,1)S(1)} all-reduce(bf16[1536]{0:T(1024)(128)(2,1)S(1)} %dynamic-update-slice.12), channel_id=1, replica_groups=mesh['dp'=4,'seq'=4,'heads'=2] {'dp','seq'}, use_global_device_ids=true, to_apply=%add.42 | all-reduce | flops 1536 | bytes 6144
  42.6 34.3 %all-gather.4 = bf16[16,96,24]{1,2,0:T(8,128)(2,1)S(1)} all-gather(bf16[1,96,24]{1,2,0:T(8,128)(2,1)} %bitcast.985), channel_id=1, replica_groups=mesh['dp'=4,'seq'=4,'heads'=2] {'dp','seq'}, dimensions={0}, use_global_device_ids=true | all-gather | bytes 78336 | tf_op jit(solution)/shard_map/all_gather | solution.py:145
  83.6 44.4 %all_gather.34 = bf16[1536,256]{1,0:T(8,128)(2,1)S(1)} all-gather(bf16[96,256]{1,0:T(8,128)(2,1)S(1)} %copy-done.130), channel_id=1, replica_groups=mesh['dp'=4,'seq'=4,'heads'=2] {'dp','seq'}, dimensions={0}, use_global_device_ids=true | all-gather | bytes 835584 | tf_op jit(solution)/shard_map/all_gather | solution.py:144
  132.8 3.9 fusion.338
  136.8 3.7 collective-permute-start.1
  143.1 3.3 collective-permute-start
  148.9 5.8 fusion.145
  174.1 8.3 all_gather.81
  182.3 10.1 all_gather.36
  192.5 5.2 fusion.197
  199.9 20.6 %all-gather.19.cloned.1.call-done = f32[4,24,128,64]{2,3,1,0:T(8,128)} async-done(((f32[1,24,128,64]{2,3,1,0:T(8,128)}), f32[4,24,128,64]{2,3,1,0:T(8,128)}) %all-gather.19.cloned.1.call-update) | async-done | bytes 3145744 | tf_op jit(solution)/shard_map/all_gather | solution.py:24
  220.5 27.6 %while.64 = (s32[]{:T(128)}, f32[1,24,128,64]{3,2,1,0:T(8,128)}, s32[]{:T(128)}, f32[4,1,24]{2,1,0:T(1,128)}, f32[4,1,24,128,64]{3,4,2,0,1:T(8,128)}, /*index=5*/s32[]{:T(128)}, s32[]{:T(128)}) while((s32[]{:T(128)}, f32[1,24,128,64]{3,2,1,0:T(8,128)}, s32[]{:T(128)}, f32[4,1,24]{2,1,0:T(1,128)}, f32[4,1,24,128,64]{3,4,2,0,1:T(8,128)}, ...), condition=%wide.region_4.5_spmd.clone, body=%wide.region_3.4_spmd.clone.sunk | while | flops 786436 | bytes 5505425 | solution.py:35
  251.5 7.3 fusion.115
  260.5 23.5 %all-gather.21.cloned.1.call-done = f32[4,24,128,64]{2,3,1,0:T(8,128)} async-done(((f32[1,24,128,64]{2,3,1,0:T(8,128)}), f32[4,24,128,64]{2,3,1,0:T(8,128)}) %all-gather.21.cloned.1.call-update) | async-done | bytes 3145744 | tf_op jit(solution)/shard_map/all_gather | solution.py:24
  284.0 19.1 %while.65 = (s32[]{:T(128)}, f32[1,24,128,64]{3,2,1,0:T(8,128)S(1)}, s32[]{:T(128)}, f32[4,1,24]{2,1,0:T(1,128)}, f32[4,1,24,128,64]{3,4,2,0,1:T(8,128)}, /*index=5*/s32[]{:T(128)}, s32[]{:T(128)}) while((s32[]{:T(128)}, f32[1,24,128,64]{3,2,1,0:T(8,128)S(1)}, s32[]{:T(128)}, f32[4,1,24]{2,1,0:T(1,128)}, ...), condition=%wide.region_12.13_spmd.clone, body=%wide.region_11.12_spmd.clone.sunk | while | flops 786436 | bytes 5505425 | solution.py:35
  305.2 9.0 fusion.114
  314.2 3.5 copy.374
  317.7 22.7 %all-gather.15.cloned.1.call-done = bf16[1536,1536]{1,0:T(8,128)(2,1)} async-done(((bf16[96,1536]{1,0:T(8,128)(2,1)}), bf16[1536,1536]{1,0:T(8,128)(2,1)}) %all-gather.15.cloned.1.call-update) | async-done | bytes 4718608 | tf_op jit(solution)/shard_map/all_gather | solution.py:142
  340.4 6.2 multiply_reduce_fusion.18
  346.7 3.4 multiply_reduce_fusion.19
  350.1 4.9 all-reduce.47
  355.1 7.6 multiply_reduce_fusion.3
  362.8 4.9 all-reduce.46
  367.7 7.1 fusion.117
  376.7 3.1 fusion.163
  403.2 3.0 copy.417
  416.0 3.2 mul.1577
  419.2 3.1 copy.390
  422.3 3.2 mul.1648
  425.5 3.0 copy.418
  437.1 3.7 fusion.160
  440.8 7.7 convolution_bitcast_fusion.7
  448.6 6.2 convolution_bitcast_fusion.5
  454.8 4.3 multiply_convert_fusion.1
  459.2 5.4 fusion.363
  464.7 5.4 fusion.364
  470.1 7.1 fusion.365
  482.4 30.3 %while.67 = (s32[]{:T(128)}, f32[1,24,128,64]{3,2,1,0:T(8,128)}, s32[]{:T(128)}, f32[4,1,24]{2,1,0:T(1,128)}, f32[4,1,24,128,64]{3,4,2,0,1:T(8,128)}, /*index=5*/s32[]{:T(128)}, s32[]{:T(128)}, s32[]{:T(128)}, s32[]{:T(128)}) while((s32[]{:T(128)}, f32[1,24,128,64]{3,2,1,0:T(8,128)}, s32[]{:T(128)}, f32[4,1,24]{2,1,0:T(1,128)}, ...), condition=%wide.region_37.39_spmd.clone, body=%wide.region_36.38_spmd.clone.sunk | while | flops 786440 | bytes 5505487 | solution.py:35
  515.6 4.5 fusion.120
  520.1 23.9 %while.66 = (s32[]{:T(128)}, f32[1,24,128,64]{3,2,1,0:T(8,128)S(1)}, s32[]{:T(128)}, f32[4,1,24]{2,1,0:T(1,128)}, f32[4,1,24,128,64]{3,4,2,0,1:T(8,128)}, /*index=5*/s32[]{:T(128)}, s32[]{:T(128)}, s32[]{:T(128)}, s32[]{:T(128)}) while((s32[]{:T(128)}, f32[1,24,128,64]{3,2,1,0:T(8,128)S(1)}, s32[]{:T(128)}, ...), condition=%wide.region_19.20_spmd.clone, body=%wide.region_18.19_spmd.clone.sunk | while | flops 786440 | bytes 5505487 | solution.py:35
  546.3 4.4 fusion.127
  561.4 15.1 %fusion.37 = (f32[256,24]{0,1:T(8,128)}, f32[256,24]{0,1:T(8,128)}, f32[256,24]{0,1:T(8,128)}, f32[256,256]{1,0:T(8,128)}, f32[256,256]{1,0:T(8,128)}, /*index=5...) fusion(f32[256,256]{1,0:T(8,128)} %fusion.281, f32[256,24]{0,1:T(8,128)} %copy.385, f32[256,24]{0,1:T(8,128)} %copy.383, ...), kind=kOutput, calls=%fused_computation.62 | convolution fusion | flops 1254977536 | bytes 10797056 | tf_op jit(solution)/shard_map/transpose(jvp(btsh,bshp->bthp))/dot_general | solution.py:68
  590.0 3.8 reduce-window.56
  607.8 8.2 bitcast_add_fusion.5
  616.1 3.2 copy.386
  619.3 4.4 multiply_reduce_fusion.11
  623.8 9.0 bitcast_add_fusion.4
  632.8 3.1 copy.414
  636.0 3.9 multiply_reduce_fusion.7
  651.0 5.7 fusion.171
  656.8 5.9 fusion.181
  671.7 4.0 collective-permute-start.2
  685.2 4.6 convolution_add_fusion.7
  689.8 3.8 convolution_add_fusion.6
  702.3 17.2 %all-reduce.53 = (bf16[1,256,256]{2,1,0:T(8,128)(2,1)S(1)}, bf16[1,256,256]{2,1,0:T(8,128)(2,1)S(1)}, f32[5,256]{1,0:T(8,128)}) all-reduce(f32[1,256,256]{2,1,0:T(8,128)} %scatter-add.19, f32[1,256,256]{2,1,0:T(8,128)} %scatter-add.15, f32[5,256]{1,0:T(8,128)S(1)} %add_add_fusion.1), channel_id=1, replica_groups=mesh['dp'=4,'seq'=4,'heads'=2] {'heads'}, use_global_device_ids=true, to_apply=%region_50.52 | all-reduce | flops 132352 | bytes 796672 | tf_op jit(solution)/shard_map/psum | solution.py:268
  726.0 5.3 convolution_add_fusion
  734.1 5.2 convolution_add_fusion.2
  742.0 5.3 convolution_add_fusion.1
  751.0 129.0 %all-reduce.52.cloned.1.call-done = (f32[1,256,1536]{2,1,0:T(8,128)}, f32[1,256,1536]{2,1,0:T(8,128)}, f32[1,256,1536]{2,1,0:T(8,128)}, f32[1,256,1536]{2,1,0:T(8,128)}) async-done(((f32[1,256,1536]{2,1,0:T(8,128)}, f32[1,256,1536]{2,1,0:T(8,128)}, f32[1,256,1536]{2,1,0:T(8,128)}, f32[1,256,1536]{2,1,0:T(8,128)}), (f32[1,256,1536]{2,1,0:T(8,128)}, f32[1,256,1536]{2,1,0:T(8,128)}, f32[1,256,1536]{2,1,0:T(8,128)}, ...) | async-done | bytes 6291472 | tf_op jit(solution)/shard_map/psum | solution.py:190
  884.3 60.4 %all-reduce.44 = (f32[1536]{0:T(1024)S(1)}, f32[5,1536]{1,0:T(8,128)}, f32[5,256]{1,0:T(8,128)}, f32[24]{0:T(128)}, f32[24]{0:T(128)}, /*index=5*/f32[24]{0:T(128)}, f32[1536]{0:T(1024)}) all-reduce(f32[1536]{0:T(1024)S(1)} %add.649, f32[5,1536]{1,0:T(8,128)S(1)} %add_add_fusion, ...), channel_id=6, replica_groups=mesh['dp'=4,'seq'=4,'heads'=2] {'dp','seq'}, use_global_device_ids=true, to_apply=%region_54.56.clone | all-reduce | flops 12104 | bytes 96832
  945.3 3.5 fusion.192
  951.4 108.1 %reduce-scatter.14.cloned.1.call-done = f32[1536,96]{0,1:T(8,128)} async-done(((f32[1536,1536]{0,1:T(8,128)}), f32[1536,96]{0,1:T(8,128)}) %reduce-scatter.14.cloned.1.call-update) | async-done | bytes 589840 | tf_op jit(solution)/shard_map/reduce_scatter | solution.py:305
  1059.4 115.7 %reduce-scatter.8.cloned.1.call-done = f32[96,1536]{1,0:T(8,128)} async-done(((f32[1536,1536]{1,0:T(8,128)}), f32[96,1536]{1,0:T(8,128)}) %reduce-scatter.8.cloned.1.call-update) | async-done | bytes 589840 | tf_op jit(solution)/shard_map/reduce_scatter | solution.py:301
  1175.1 116.4 %reduce-scatter.10.cloned.1.call-done = f32[96,1536]{1,0:T(8,128)} async-done(((f32[1536,1536]{1,0:T(8,128)}), f32[96,1536]{1,0:T(8,128)}) %reduce-scatter.10.cloned.1.call-update) | async-done | bytes 589840 | tf_op jit(solution)/shard_map/reduce_scatter | solution.py:302
  (730 shorter events, 301.0 us)
Async XLA Ops:
  7.2 72.2 %copy-start.3 = (bf16[2,1,256,1536]{3,2,1,0:T(8,128)(2,1)S(1)}, bf16[2,1,256,1536]{3,2,1,0:T(8,128)(2,1)}, u32[]{:S(2)}) copy-start(bf16[2,1,256,1536]{3,2,1,0:T(8,128)(2,1)} %param.31) | copy-start | bytes 4718596
  7.2 72.2 %copy-start.206 = (f32[24]{0:T(128)S(1)}, f32[24]{0:T(128)}, u32[]{:S(2)}) copy-start(f32[24]{0:T(128)} %param.41) | copy-start | bytes 292
  7.2 125.6 %all-gather.13.cloned.1.call-start = ((), (), s32[]{:S(2)}) async-start(), calls=%async_computation.5 | async-start | bytes 5013504 | tf_op jit(solution)/shard_map/all_gather | solution.py:143
  7.9 184.5 %all-gather.17.cloned.1.call-start = ((), (), s32[]{:S(2)}) async-start(), calls=%async_computation.7 | async-start | bytes 5013504 | tf_op jit(solution)/shard_map/all_gather | solution.py:146
  8.7 211.8 %all-gather.19.cloned.1.call-start = ((), (), s32[]{:S(2)}) async-start(), calls=%async_computation.12 | async-start | bytes 3932160 | tf_op jit(solution)/shard_map/all_gather | solution.py:24
  9.4 122.5 %copy-start.193 = (f32[24]{0:T(128)}, f32[24]{0:T(128)S(1)}, u32[]{:S(2)}) copy-start(f32[24]{0:T(128)S(1)} %exp.161) | copy-start | bytes 292
  79.4 61.1 %copy-start.126 = (f32[256]{0:T(256)}, f32[256]{0:T(256)S(1)}, u32[]{:S(2)}) copy-start(f32[256]{0:T(256)S(1)} %get-tuple-element.954) | copy-start | bytes 3076
  79.4 261.0 %copy-start.123 = (f32[256]{0:T(256)}, f32[256]{0:T(256)S(1)}, u32[]{:S(2)}) copy-start(f32[256]{0:T(256)S(1)} %get-tuple-element.935) | copy-start | bytes 3076
  80.5 51.4 %copy-start.82 = (f32[256,24]{1,0:T(8,128)}, f32[256,24]{1,0:T(8,128)S(1)}, u32[]{:S(2)}) copy-start(f32[256,24]{1,0:T(8,128)S(1)} %get-tuple-element.944) | copy-start | bytes 73732
  82.6 49.3 %copy-start.83 = (f32[256,24]{1,0:T(8,128)}, f32[256,24]{1,0:T(8,128)S(1)}, u32[]{:S(2)}) copy-start(f32[256,24]{1,0:T(8,128)S(1)} %get-tuple-element.945) | copy-start | bytes 73732
  131.9 24.9 %copy-start.160 = (f32[1,256]{1,0:T(1,128)}, f32[1,256]{1,0:T(1,128)S(1)}, u32[]{:S(2)}) copy-start(f32[1,256]{1,0:T(1,128)S(1)} %get-tuple-element.922) | copy-start | bytes 3076
  132.8 7.7 copy-start.203
  136.8 12.1 copy-start.11
  136.8 9.6 copy-start.159
  136.8 10.5 collective-permute-start.1
  143.1 5.8 collective-permute-start
  146.5 8.2 copy-start.114
  146.6 8.2 copy-start.116
  146.6 8.2 copy-start.118
  146.6 8.2 copy-start.120
  147.3 7.5 copy-start.102
  160.4 123.6 %all-gather.21.cloned.1.call-start = ((), (), s32[]{:S(2)}) async-start(), calls=%async_computation.13 | async-start | bytes 3932160 | tf_op jit(solution)/shard_map/all_gather | solution.py:24
  164.7 9.3 copy-start.201
  164.8 175.7 %all-gather.15.cloned.1.call-start = ((), (), s32[]{:S(2)}) async-start(), calls=%async_computation.6 | async-start | bytes 5013504 | tf_op jit(solution)/shard_map/all_gather | solution.py:142
  165.4 317.1 %all-gather.25.cloned.1.call-start = ((), (), s32[]{:S(2)}) async-start(), calls=%async_computation.15 | async-start | bytes 3932160 | tf_op jit(solution)/shard_map/all_gather | solution.py:24
  192.4 112.7 %copy-start.122 = (pred[256,256]{1,0:T(8,128)(4,1)}, pred[256,256]{1,0:T(8,128)(4,1)S(1)}, u32[]{:S(2)}) copy-start(pred[256,256]{1,0:T(8,128)(4,1)S(1)} %iota_compare_fusion) | copy-start | bytes 196612
  251.5 7.4 copy-start.45
  303.1 145.3 %copy-start.2 = (f32[1,24,128,64]{3,2,1,0:T(8,128)}, f32[1,24,128,64]{3,2,1,0:T(8,128)S(1)}, u32[]{:S(2)}) copy-start(f32[1,24,128,64]{3,2,1,0:T(8,128)S(1)} %get-tuple-element.519) | copy-start | bytes 2359300
  305.1 9.0 copy-start.46
  314.2 26.3 %copy-start.4 = (bf16[2,1,256,1536]{3,2,1,0:T(8,128)(2,1)S(1)}, bf16[2,1,256,1536]{3,2,1,0:T(8,128)(2,1)}, u32[]{:S(2)}) copy-start(bf16[2,1,256,1536]{3,2,1,0:T(8,128)(2,1)} %param.31) | copy-start | bytes 4718596
  317.7 29.0 %copy-start.127 = (f32[256]{0:T(256)S(1)}, f32[256]{0:T(256)}, u32[]{:S(2)}) copy-start(f32[256]{0:T(256)} %copy-done.126) | copy-start | bytes 3076
  346.7 8.4 copy-start.95
  355.0 12.6 copy-start.133
  355.0 12.6 copy-start.168
  355.1 12.6 copy-start.137
  355.1 12.6 copy-start.170
  355.1 12.6 copy-start.32
  376.7 10.9 copy-start.92
  379.9 140.2 %all-gather.23.cloned.1.call-start = ((), (), s32[]{:S(2)}) async-start(), calls=%async_computation.14 | async-start | bytes 3932160 | tf_op jit(solution)/shard_map/all_gather | solution.py:24
  440.8 7.7 copy-start.47
  440.8 14.0 %copy-start.48 = (f32[256,1536]{1,0:T(8,128)S(1)}, f32[256,1536]{1,0:T(8,128)}, u32[]{:S(2)}) copy-start(f32[256,1536]{1,0:T(8,128)} %fusion.197) | copy-start | bytes 4718596
  459.2 290.3 %reduce-scatter.16.cloned.1.call-start = ((), (), s32[]{:S(2)}) async-start(), calls=%async_computation.16 | async-start | bytes 835584
  464.7 12.5 slice-start
  576.5 7.5 copy-start.158
  576.5 8.3 copy-start.157
  576.5 9.0 copy-start.196
  576.5 9.0 copy-start.197
  586.3 21.6 %copy-start.39 = (f32[256,1536]{0,1:T(8,128)S(1)}, f32[256,1536]{0,1:T(8,128)}, u32[]{:S(2)}) copy-start(f32[256,1536]{0,1:T(8,128)} %copy.376) | copy-start | bytes 4718596
  607.8 8.3 copy-start.109
  623.8 9.0 copy-start.111
  666.7 213.3 %all-reduce.52.cloned.1.call-start = ((), (), s32[]{:S(2)}) async-start(), calls=%async_computation.17 | async-start | bytes 12582912 | tf_op jit(solution)/shard_map/psum | solution.py:190
  671.0 8.1 copy-start.71
  671.0 9.2 copy-start.31
  671.3 8.9 copy-start.29
  671.7 8.5 collective-permute-start.2
  677.0 5.9 collective-permute-start.3
  696.8 254.6 %reduce-scatter.12.cloned.1.call-start = ((), (), s32[]{:S(2)}) async-start(), calls=%async_computation.10 | async-start | bytes 1671168 | tf_op jit(solution)/shard_map/reduce_scatter | solution.py:303
  698.8 20.8 %copy-start.129 = (f32[256]{0:T(256)S(1)}, f32[256]{0:T(256)}, u32[]{:S(2)}) copy-start(f32[256]{0:T(256)} %copy-done.126) | copy-start | bytes 3076
  701.0 19.1 %copy-start.125 = (f32[256]{0:T(256)S(1)}, f32[256]{0:T(256)}, u32[]{:S(2)}) copy-start(f32[256]{0:T(256)} %copy-done.123) | copy-start | bytes 3076
  721.8 337.7 %reduce-scatter.14.cloned.1.call-start = ((), (), s32[]{:S(2)}) async-start(), calls=%async_computation.11 | async-start | bytes 10027008 | tf_op jit(solution)/shard_map/reduce_scatter | solution.py:305
  731.3 443.8 %reduce-scatter.8.cloned.1.call-start = ((), (), s32[]{:S(2)}) async-start(), calls=%async_computation.8 | async-start | bytes 10027008 | tf_op jit(solution)/shard_map/reduce_scatter | solution.py:301
  739.4 552.1 %reduce-scatter.10.cloned.1.call-start = ((), (), s32[]{:S(2)}) async-start(), calls=%async_computation.9 | async-start | bytes 10027008 | tf_op jit(solution)/shard_map/reduce_scatter | solution.py:302
  882.4 62.9 %copy-start.180 = (f32[256]{0:T(256)S(1)}, f32[256]{0:T(256)}, u32[]{:S(2)}) copy-start(f32[256]{0:T(256)} %get-tuple-element.934) | copy-start | bytes 3076
  882.4 62.9 %copy-start.181 = (f32[256]{0:T(256)S(1)}, f32[256]{0:T(256)}, u32[]{:S(2)}) copy-start(f32[256]{0:T(256)} %get-tuple-element.955) | copy-start | bytes 3076
  (164 other events, 519.8 us)
Sparse Core Ops, SparseCore 0:
  10.3 55.3 all-gather.12
  68.0 58.9 all-gather.16
  160.5 59.8 all-gather.18
  221.9 62.0 all-gather.20
  286.2 54.2 all-gather.14
  380.0 59.7 all-gather.24
  459.3 59.7 all-gather.22
  666.8 56.3 reduce-scatter.15
  726.5 153.4 all-reduce.51
  884.1 59.3 reduce-scatter.11
  948.7 110.6 reduce-scatter.13
  1064.0 111.0 reduce-scatter.7
  1180.3 111.0 reduce-scatter.9
where the time goes:
time: 1310 us; the launch traced here: 1300 us
  waiting for transfers between devices  541 us (41%)
  blocking collectives  215 us (16%)
  matrix products  197 us (15%)
  local copies, waits for them, and re-layouts  187 us (14%)
  other arithmetic  125 us (10%)
  between operations  18.2 us (1%)
  starting transfers between devices  13.8 us (1%)
    psum x1, waiting for transfers between devices, shards(): branch = lax.psum(partial_out, 'heads')  129 us
    reduce_scatter x1, waiting for transfers between devices, shards(): lax.psum_scatter(acc_value, ('dp', 'seq'), scatter_dimension=0, tiled=True)  116 us
    reduce_scatter x1, waiting for transfers between devices, shards(): lax.psum_scatter(acc_gate, ('dp', 'seq'), scatter_dimension=0, tiled=True)  116 us
    reduce_scatter x1, waiting for transfers between devices, shards(): lax.psum_scatter(acc_out, ('dp', 'seq'), scatter_dimension=1, tiled=True)  108 us
    unnamed x2, blocking collectives  90.7 us
    dynamic_slice x32, local copies, waits for them, and re-layouts, step(): new = combine(before, jax.tree.map(lambda part: part[at], everything))  59.6 us
    dot_general x6, matrix products, local_parts(): jnp.einsum('btsh,bshp->bthp', weights, values, precision=HIGH)  55.8 us
    all_gather x1, blocking collectives, shards(): lax.all_gather(state_weight, ('dp', 'seq'), axis=0, tiled=True)  44.4 us
  transfers between devices with their start and end apart: 17, of which 9 were waited for; matrix products, arithmetic and copies ran while one was open for 25% of the time, Pallas kernels for 0%

commit v1 on v0

--- a/solution.py
+++ b/solution.py
@@ -1,6 +1,8 @@
 import jax
 import jax.numpy as jnp
 from jax import lax
+from jax.experimental import pallas as pl
+from jax.experimental.pallas import tpu as pltpu
 from jax.sharding import PartitionSpec as P
 
 STATE = 128
@@ -326,19 +328,646 @@
     )
 
 
+BF = jnp.bfloat16
+F32 = jnp.float32
+CHUNK = 256
+VMEM = 40 * 1024 * 1024
+
+
+def halves(x):
+    top = x.astype(BF)
+    return top, (x - top.astype(F32)).astype(BF)
+
+
+def mm(a, b):
+    return lax.dot_general(a, b, (((1,), (0,)), ((), ())), preferred_element_type=F32)
+
+
+def mm_nt(a, b):
+    return lax.dot_general(a, b, (((1,), (1,)), ((), ())), preferred_element_type=F32)
+
+
+def mm3(a, b):
+    wide = mm(a[0], jnp.concatenate([b[0], b[1]], axis=1))
+    n = b[0].shape[1]
+    return wide[:, :n] + wide[:, n:] + mm(a[1], b[0])
+
+
+def mm3_nt(a, b):
+    return mm_nt(a[0], b[0]) + mm_nt(a[0], b[1]) + mm_nt(a[1], b[0])
+
+
+def softplus(x):
+    return jnp.maximum(x, 0.0) + jnp.log1p(jnp.exp(-jnp.abs(x)))
+
+
+def taps_applied(extended, taps):
+    total = taps[CONV : CONV + 1, :]
+    for k in range(CONV):
+        total = total + extended[5 + k : 5 + k + CHUNK] * taps[k : k + 1, :]
+    return total
+
+
+def step_terms(step_ref, bias_ref, log_decay_ref):
+    shifted_pre = step_ref[...] + bias_ref[...]
+    step = softplus(shifted_pre)
+    rates = jnp.exp(log_decay_ref[...])
+    rows = lax.broadcasted_iota(jnp.int32, (CHUNK, CHUNK), 0)
+    cols = lax.broadcasted_iota(jnp.int32, (CHUNK, CHUNK), 1)
+    lower = jnp.where(rows >= cols, 1.0, 0.0).astype(F32)
+    cum = jnp.dot(lower, -step * rates, precision=HIGH, preferred_element_type=F32)
+    return shifted_pre, step, rates, cum
+
+
+def by_pair(q, p):
+    left = lax.broadcasted_iota(jnp.int32, (1, 128), 1) < 64
+    return jnp.where(left, q[:, 2 * p : 2 * p + 1], q[:, 2 * p + 1 : 2 * p + 2])
+
+
+def forward_kernel(
+    vpre, spre, spre_step, vtaps, staps, bias, log_decay, skip, mixer, starts, state, vtail, stail
+):
+    @pl.when(pl.program_id(0) == 0)
+    def _():
+        state[...] = jnp.zeros_like(state)
+        vtail[...] = jnp.zeros_like(vtail)
+        stail[...] = jnp.zeros_like(stail)
+
+    vx, sx = vpre[...], spre[...]
+    values = jax.nn.silu(taps_applied(jnp.concatenate([vtail[...], vx], axis=0), vtaps[...]))
+    states = jax.nn.silu(taps_applied(jnp.concatenate([stail[...], sx], axis=0), staps[...]))
+    vtail[...] = vx[CHUNK - 8 :]
+    stail[...] = sx[CHUNK - 8 :]
+    b, c = states[:, :STATE], states[:, STATE:]
+    shifted_pre, step, rates, cum = step_terms(spre_step, bias, log_decay)
+    cum_t = cum.T
+    final = cum[CHUNK - 1 :, :]
+    grown, ending, whole = jnp.exp(cum), jnp.exp(final - cum), jnp.exp(final)
+    b2, c2, bt2 = halves(b), halves(c), halves(b.T)
+    scores = mm3_nt(c2, b2)
+    rows = lax.broadcasted_iota(jnp.int32, (CHUNK, CHUNK), 0)
+    cols = lax.broadcasted_iota(jnp.int32, (CHUNK, CHUNK), 1)
+    barred = jnp.where(rows >= cols, 0.0, -1e30).astype(F32)
+    left = lax.broadcasted_iota(jnp.int32, (1, 128), 1) < 64
+    starts[0] = state[...]
+    for p in range(vx.shape[1] // 128):
+        lanes = slice(128 * p, 128 * p + 128)
+        v = values[:, lanes]
+        weighted = v * by_pair(step, p)
+        w2 = halves(weighted)
+        both = jnp.concatenate([w2[0], w2[1]], axis=1)
+        parts = []
+        for h in (2 * p, 2 * p + 1):
+            mix = halves(jnp.exp(cum[:, h : h + 1] - cum_t[h : h + 1, :] + barred) * scores)
+            wide = mm(mix[0], both)
+            parts.append(wide[:, :128] + wide[:, 128:] + mm(mix[1], w2[0]))
+        held = state[:, lanes]
+        carried = by_pair(grown, p) * mm3(c2, halves(held))
+        mixer[:, lanes] = jnp.where(left, parts[0], parts[1]) + carried + skip[:, lanes] * v
+        state[:, lanes] = held * by_pair(whole, p) + mm3(bt2, halves(weighted * by_pair(ending, p)))
+
+
+def forward_scan(vpre, spre, step_pre, vtaps, staps, bias, log_decay, skip):
+    tokens, width = vpre.shape
+    chunks = tokens // CHUNK
+    row = lambda n: pl.BlockSpec((CHUNK, n), lambda i: (i, 0))
+    fixed = lambda x: pl.BlockSpec(x.shape, lambda i: (0, 0))
+    return pl.pallas_call(
+        forward_kernel,
+        grid=(chunks,),
+        in_specs=[row(width), row(2 * STATE), row(128)]
+        + [fixed(x) for x in (vtaps, staps, bias, log_decay, skip)],
+        out_specs=[row(width), pl.BlockSpec((1, STATE, width), lambda i: (i, 0, 0))],
+        out_shape=[
+            jax.ShapeDtypeStruct((tokens, width), F32),
+            jax.ShapeDtypeStruct((chunks, STATE, width), F32),
+        ],
+        scratch_shapes=[
+            pltpu.VMEM((STATE, width), F32),
+            pltpu.VMEM((8, width), F32),
+            pltpu.VMEM((8, 2 * STATE), F32),
+        ],
+        compiler_params=pltpu.CompilerParams(vmem_limit_bytes=VMEM),
+        cost_estimate=pl.CostEstimate(
+            flops=chunks * 12 * 4 * CHUNK * CHUNK * 256,
+            bytes_accessed=tokens * width * 8,
+            transcendentals=chunks * 12 * CHUNK * CHUNK,
+        ),
+        name="scan_forward",
+    )(vpre, spre, step_pre, vtaps, staps, bias, log_decay, skip)
+
+
+def silu_slope(total):
+    s = jax.nn.sigmoid(total)
+    return s * (1.0 + total * (1.0 - s))
+
+
+def taps_back(d_total, later, taps):
+    extended = jnp.concatenate([d_total, later], axis=0)
+    result = 0.0
+    for k in range(CONV):
+        result = result + extended[3 - k : 3 - k + CHUNK] * taps[k : k + 1, :]
+    return result
+
+
+def taps_grads(d_total, extended):
+    rows = [
+        jnp.sum(d_total * extended[5 + k : 5 + k + CHUNK], axis=0, keepdims=True)
+        for k in range(CONV)
+    ]
+    return rows + [jnp.sum(d_total, axis=0, keepdims=True)]
+
+
+def backward_kernel(
+    vpre, vbefore, spre, sbefore, spre_step, vtaps, staps, bias, log_decay, skip, chooser,
+    mixer, d_mixer, starts,
+    values_low, d_spre, step_low, value_sums, state_sums, step_sums,
+    later_grad, later_state, vhead, shead, products, d_values,
+):
+    place = pl.program_id(0)
+
+    @pl.when(place == 0)
+    def _():
+        for ref in (later_grad, later_state, vhead, shead, value_sums, state_sums, step_sums):
+            ref[...] = jnp.zeros_like(ref)
+
+    first = place == pl.num_programs(0) - 1
+    vx, sx = vpre[...], spre[...]
+    vext = jnp.concatenate([jnp.where(first, 0.0, vbefore[...]), vx], axis=0)
+    sext = jnp.concatenate([jnp.where(first, 0.0, sbefore[...]), sx], axis=0)
+    vtotal, stotal = taps_applied(vext, vtaps[...]), taps_applied(sext, staps[...])
+    values, states = jax.nn.silu(vtotal), jax.nn.silu(stotal)
+    b, c = states[:, :STATE], states[:, STATE:]
+    shifted_pre, step, rates, cum = step_terms(spre_step, bias, log_decay)
+    cum_t = cum.T
+    final = cum[CHUNK - 1 :, :]
+    grown, ending, whole = jnp.exp(cum), jnp.exp(final - cum), jnp.exp(final)
+    b2, c2, ct2 = halves(b), halves(c), halves(c.T)
+    scores_t = mm3_nt(b2, c2)
+    rows = lax.broadcasted_iota(jnp.int32, (CHUNK, CHUNK), 0)
+    cols = lax.broadcasted_iota(jnp.int32, (CHUNK, CHUNK), 1)
+    barred = jnp.where(cols >= rows, 0.0, -1e30).astype(F32)
+    left = lax.broadcasted_iota(jnp.int32, (1, 128), 1) < 64
+    zero = jnp.zeros((CHUNK, 128), BF)
+    d_scores_t = jnp.zeros((CHUNK, CHUNK), F32)
+    d_b = jnp.zeros((CHUNK, STATE), F32)
+    d_c = jnp.zeros((CHUNK, STATE), F32)
+    skip_rows = []
+    final_rows = []
+    pairs = vx.shape[1] // 128
+    for p in range(pairs):
+        lanes = slice(128 * p, 128 * p + 128)
+        v, dy = values[:, lanes], d_mixer[:, lanes]
+        weighted = v * by_pair(step, p)
+        w2, d2 = halves(weighted), halves(dy)
+        both = jnp.concatenate([d2[0], d2[1]], axis=1)
+        w_rest = pltpu.roll(weighted - w2[0].astype(F32), 64, 1).astype(BF)
+        d_top = pltpu.roll(d2[0].astype(F32), 64, 1).astype(BF)
+        parts = []
+        for h, mine in ((2 * p, left), (2 * p + 1, ~left)):
+            decay = jnp.exp(cum_t[h : h + 1, :] - cum[:, h : h + 1] + barred)
+            mix = halves(decay * scores_t)
+            wide = mm(mix[0], both)
+            parts.append(wide[:, :128] + wide[:, 128:] + mm(mix[1], d2[0]))
+            one = jnp.concatenate(
+                [jnp.where(mine, w2[0], w_rest), jnp.where(mine, w2[0], zero)], axis=1
+            )
+            other = jnp.concatenate(
+                [jnp.where(mine, d2[0], d_top), jnp.where(mine, d2[1], zero)], axis=1
+            )
+            d_scores_t = d_scores_t + mm_nt(one, other) * decay
+        held, after = starts[0, :, lanes], later_grad[:, lanes]
+        after2 = halves(after)
+        ends = by_pair(ending, p)
+        d_weighted = jnp.where(left, parts[0], parts[1]) + ends * mm3(b2, after2)
+        gain = skip[:, lanes]
+        products[:, lanes] = dy * (mixer[:, lanes] - gain * v)
+        products[:, 128 * (pairs + p) : 128 * (pairs + p) + 128] = v * d_weighted
+        d_values[:, lanes] = by_pair(step, p) * d_weighted + gain * dy
+        skip_rows.append(jnp.sum(v * dy, axis=0, keepdims=True))
+        final_rows.append(jnp.sum(after * later_state[:, lanes], axis=0, keepdims=True))
+        faded = halves(by_pair(grown, p) * dy)
+        d_c = d_c + mm3_nt(faded, halves(held))
+        d_b = d_b + mm3_nt(halves(weighted * ends), after2)
+        later_grad[:, lanes] = after * by_pair(whole, p) + mm3(ct2, faded)
+    later_state[...] = starts[0]
+    d2 = halves(d_scores_t)
+    dt2 = halves(d_scores_t.T)
+    d_b = d_b + mm3(d2, c2)
+    d_c = d_c + mm3(dt2, b2)
+    width = 128 * pairs
+    pick = chooser[...]
+
+    def by_head(x):
+        top, rest = halves(x)
+        return mm(top, pick) + mm(rest, pick)
+
+    reached = by_head(products[:, :width])
+    pulled = by_head(products[:, width:])
+    at_end = by_head(jnp.broadcast_to(jnp.concatenate(final_rows, axis=1), (8, width)))[:1]
+    rows128 = lax.broadcasted_iota(jnp.int32, (CHUNK, 128), 0)
+    d_cum = reached - step * pulled + jnp.where(rows128 == CHUNK - 1, at_end, 0.0)
+    upper = jnp.where(cols >= rows, 1.0, 0.0).astype(F32)
+    d_rate = jnp.dot(upper, d_cum, precision=HIGH, preferred_element_type=F32)
+    d_step = pulled - rates * d_rate
+    d_shifted = d_step * jax.nn.sigmoid(shifted_pre)
+    step_low[...] = d_shifted.astype(BF)
+    step_sums[0:1, :] += jnp.sum(d_shifted, axis=0, keepdims=True)
+    step_sums[1:2, :] -= jnp.sum(d_rate * step, axis=0, keepdims=True) * rates
+    d_vtotal = d_values[...] * silu_slope(vtotal)
+    values_low[...] = taps_back(d_vtotal, vhead[...], vtaps[...]).astype(BF)
+    value_sums[...] += jnp.concatenate(
+        taps_grads(d_vtotal, vext)
+        + [jnp.concatenate(skip_rows, axis=1), jnp.zeros((2, width), F32)],
+        axis=0,
+    )
+    vhead[...] = d_vtotal[:8]
+    d_stotal = jnp.concatenate([d_b, d_c], axis=1) * silu_slope(stotal)
+    d_spre[...] = taps_back(d_stotal, shead[...], staps[...])
+    state_sums[...] += jnp.concatenate(
+        taps_grads(d_stotal, sext) + [jnp.zeros((3, 2 * STATE), F32)], axis=0
+    )
+    shead[...] = d_stotal[:8]
+
+
+def backward_scan(
+    vpre, spre, step_pre, vtaps, staps, bias, log_decay, skip, mixer, d_mixer, starts
+):
+    tokens, width = vpre.shape
+    chunks = tokens // CHUNK
+    heads = jnp.arange(width)[:, None] // 64
+    chooser = (heads == jnp.arange(128)[None, :]).astype(BF)
+    row = lambda n: pl.BlockSpec((CHUNK, n), lambda i: (chunks - 1 - i, 0))
+    before = lambda n: pl.BlockSpec(
+        (8, n), lambda i: (jnp.maximum((chunks - 1 - i) * (CHUNK // 8) - 1, 0), 0)
+    )
+    fixed = lambda x: pl.BlockSpec(x.shape, lambda i: (0, 0))
+    summed = lambda n: pl.BlockSpec((8, n), lambda i: (0, 0))
+    return pl.pallas_call(
+        backward_kernel,
+        grid=(chunks,),
+        in_specs=[row(width), before(width), row(2 * STATE), before(2 * STATE), row(128)]
+        + [fixed(x) for x in (vtaps, staps, bias, log_decay, skip, chooser)]
+        + [row(width), row(width), pl.BlockSpec((1, STATE, width), lambda i: (chunks - 1 - i, 0, 0))],
+        out_specs=[
+            row(width), row(2 * STATE), row(128), summed(width), summed(2 * STATE), summed(128),
+        ],
+        out_shape=[
+            jax.ShapeDtypeStruct((tokens, width), BF),
+            jax.ShapeDtypeStruct((tokens, 2 * STATE), F32),
+            jax.ShapeDtypeStruct((tokens, 128), BF),
+            jax.ShapeDtypeStruct((8, width), F32),
+            jax.ShapeDtypeStruct((8, 2 * STATE), F32),
+            jax.ShapeDtypeStruct((8, 128), F32),
+        ],
+        scratch_shapes=[
+            pltpu.VMEM((STATE, width), F32),
+            pltpu.VMEM((STATE, width), F32),
+            pltpu.VMEM((8, width), F32),
+            pltpu.VMEM((8, 2 * STATE), F32),
+            pltpu.VMEM((CHUNK, 2 * width), F32),
+            pltpu.VMEM((CHUNK, width), F32),
+        ],
+        compiler_params=pltpu.CompilerParams(vmem_limit_bytes=VMEM),
+        cost_estimate=pl.CostEstimate(
+            flops=chunks * 12 * 8 * CHUNK * CHUNK * 256,
+            bytes_accessed=tokens * width * 16,
+            transcendentals=chunks * 12 * CHUNK * CHUNK,
+        ),
+        name="scan_backward",
+    )(vpre, vpre, spre, spre, step_pre, vtaps, staps, bias, log_decay, skip, chooser, mixer, d_mixer, starts)
+
+
+def place(arrays, piece, targets, rows):
+    count = sum(x.shape[0] // piece for x in arrays)
+    assert count == len(targets)
+    width, dtype = arrays[0].shape[1], arrays[0].dtype
+
+    def kernel(at, *refs):
+        sources, out, done = refs[: len(arrays)], refs[len(arrays)], refs[len(arrays) + 1]
+        copies = []
+        for source in sources:
+            for j in range(source.shape[0] // piece):
+                k = len(copies)
+                start = pl.multiple_of(at[k], piece)
+                copies.append(
+                    pltpu.make_async_copy(
+                        source.at[pl.ds(j * piece, piece)], out.at[pl.ds(start, piece)], done.at[k]
+                    )
+                )
+        for copy in copies:
+            copy.start()
+        for copy in copies:
+            copy.wait()
+
+    return pl.pallas_call(
+        kernel,
+        grid_spec=pltpu.PrefetchScalarGridSpec(
+            num_scalar_prefetch=1,
+            grid=(1,),
+            in_specs=[pl.BlockSpec(memory_space=pl.ANY)] * len(arrays),
+            out_specs=pl.BlockSpec(memory_space=pltpu.VMEM),
+            scratch_shapes=[pltpu.SemaphoreType.DMA((count,))],
+        ),
+        out_shape=jax.ShapeDtypeStruct((rows, width), dtype),
+        compiler_params=pltpu.CompilerParams(vmem_limit_bytes=16 * 1024 * 1024),
+        cost_estimate=pl.CostEstimate(
+            flops=0, bytes_accessed=2 * rows * width * dtype.itemsize, transcendentals=0
+        ),
+        name="place",
+    )(jnp.stack([jnp.asarray(t, jnp.int32) for t in targets]), *arrays)
+
+
+def swap(x, axis, bit=1):
+    return lax.ppermute(x, axis, [(i, i ^ bit) for i in range(lax.axis_size(axis))])
+
+
+def turned(x, axis, distance):
+    n = lax.axis_size(axis)
+    return lax.ppermute(x, axis, [(i, (i + distance) % n) for i in range(n)])
+
+
+def at(x, index, axis):
+    return lax.dynamic_index_in_dim(x, index, axis, keepdims=False)
+
+
+def part(x, index, size, axis):
+    return lax.dynamic_slice_in_dim(x, index * size, size, axis)
+
+
+def ordered(flag, mine, other, axis):
+    first = jnp.where(flag == 0, mine, other)
+    second = jnp.where(flag == 0, other, mine)
+    return jnp.concatenate([first, second], axis=axis)
+
+
+def whole_sequences(
+    block_input, output_grad, input_gain, gate_weight, value_weight, state_weight, step_weight,
+    out_weight, value_taps, state_taps, step_bias, log_decay, skip_gain, mixer_gain,
+):
+    xi, ci, zi, yi = (lax.axis_index(n) for n in ("x", "core", "seq", "heads"))
+    nz = lax.axis_size("seq")
+    nx = lax.axis_size("x")
+    d_model = block_input.shape[-1]
+    group = block_input.shape[2]
+    sub = group // 4
+    tokens = group * nz
+    own = sub * nz
+    rows = gate_weight.shape[0]
+    cols = gate_weight.shape[1] // 2
+    heads = step_weight.shape[1] // 2
+    slot = 2 * (zi // 2) + ci
+
+    def tokens_in(x):
+        rounds = []
+        for r in range(nz):
+            j = zi ^ r
+            start = yi * (2 * sub) + (j % 2) * sub
+            piece = lax.dynamic_slice(x, (j // 2, 0, start, 0), (1, 1, sub, d_model))
+            route = [
+                (c * nz + z, ((z ^ r) % 2) * nz + 2 * ((z ^ r) // 2) + c)
+                for c in range(2)
+                for z in range(nz)
+            ]
+            rounds.append(lax.ppermute(piece.reshape(sub, d_model), ("core", "seq"), route))
+        return place(rounds, sub, [(slot ^ r) * sub for r in range(nz)], own)
+
+    def tokens_back(x):
+        mine, other = [], []
+        for r in range(nz):
+            piece = part(x, slot ^ r, sub, 0)
+            route = [
+                (((z ^ r) % 2) * nz + 2 * ((z ^ r) // 2) + c, c * nz + z)
+                for c in range(2)
+                for z in range(nz)
+            ]
+            mine.append(lax.ppermute(piece, ("core", "seq"), route))
+            other.append(swap(mine[-1], "heads"))
+        targets = [
+            (((zi ^ r) // 2) * 4 + 2 * y + (zi ^ r) % 2) * sub
+            for y in (yi, 1 - yi)
+            for r in range(nz)
+        ]
+        return place(mine + other, sub, targets, 2 * group).reshape(block_input.shape)
+
+    def spread(x):
+        by_y = swap(x, "heads")
+        by_core = swap(x, "core")
+        by_both = swap(by_y, "core")
+        targets = [
+            (4 * k + 2 * y + c) * sub
+            for y, c in ((yi, ci), (1 - yi, ci), (yi, 1 - ci), (1 - yi, 1 - ci))
+            for k in range(nz)
+        ]
+        return place([x, by_y, by_core, by_both], sub, targets, tokens), by_core
+
+    def reduced(x, link=BF):
+        split = x.reshape(nz, 2, 2, sub, x.shape[-1])
+        summed = at(split, ci, 2) + swap(at(split, 1 - ci, 2), "core")
+        sent = swap(at(summed, 1 - yi, 1).astype(link), "heads").astype(F32)
+        return (at(summed, yi, 1) + sent).reshape(own, x.shape[-1])
+
+    def gathered(weight):
+        width = weight.shape[1] // 2
+        received = swap(part(weight, 1 - ci, width, 1), "core")
+        block = ordered(ci, part(weight, ci, width, 1), received, 0)
+        right = turned(block, "seq", 1)
+        left = turned(block, "seq", -1)
+        across = swap(block, "x")
+        far = turned(right, "seq", 1)
+        blocks = [block, right, left, far, across]
+        blocks += [swap(right, "x"), swap(left, "x"), swap(far, "x")]
+        targets = [
+            ((x * 2 + c) * nz + z % nz) * rows
+            for x in (xi, 1 - xi)
+            for z in (zi, zi + nz - 1, zi + 1, zi + 2)
+            for c in range(2)
+        ]
+        return place(blocks, rows, targets, d_model)
+
+    def scattered(grad):
+        half = d_model // 2
+        summed = part(grad, xi, half, 0) + swap(
+            part(grad, 1 - xi, half, 0).astype(BF), "x"
+        ).astype(F32)
+        summed = summed.reshape(2, nz, rows, grad.shape[1])
+        total = at(summed, zi, 1)
+        for d in range(1, nz):
+            sent = at(summed, (zi + d) % nz, 1).astype(BF)
+            total = total + turned(sent, "seq", d).astype(F32)
+        return total
+
+    def to_core(total):
+        received = swap(at(total, 1 - ci, 0), "core")
+        return at(total, ci, 0), received
+
+    gain = ordered(ci, input_gain[None], swap(input_gain[None], "core"), 0)
+    near = [gain] + [turned(gain, "seq", d) for d in range(1, nz)]
+    by_z = jnp.stack(near)[(zi - jnp.arange(nz)) % nz]
+    gain = ordered(xi, by_z[None], swap(by_z[None], "x"), 0)
+    gain = jnp.transpose(gain, (0, 2, 1, 3)).reshape(1, d_model).astype(F32)
+
+    kept = tokens_in(block_input)
+    x_own = kept.astype(F32)
+    scaling = lax.rsqrt(jnp.mean(x_own * x_own, axis=-1, keepdims=True) + EPS)
+    normed_own = (x_own * scaling * gain).astype(BF)
+    normed, normed_core = spread(normed_own)
+
+    pad = 128 - heads
+    first = jnp.concatenate(
+        [
+            jnp.concatenate(
+                [
+                    value_weight[:, cols * k : cols * k + cols],
+                    state_weight[:, STATE * k : STATE * k + STATE],
+                    step_weight[:, heads * k : heads * k + heads],
+                    jnp.zeros((rows, pad), BF),
+                ],
+                axis=1,
+            )
+            for k in range(2)
+        ],
+        axis=1,
+    )
+    first_full = gathered(first)
+    gate_full = gathered(gate_weight)
+    og_own = tokens_in(output_grad)
+    og, og_core = spread(og_own)
+    out_full = gathered(out_weight.T)
+
+    project = lambda a, b: jnp.dot(a, b, preferred_element_type=F32)
+    weights_in = (first_full[:, :cols], first_full[:, cols : cols + STATE], first_full[:, cols + STATE :])
+    values_pre = project(normed, weights_in[0])
+    states_half = project(normed, weights_in[1])
+    step_pre = project(normed, weights_in[2])
+    states_pre = ordered(ci, states_half, swap(states_half, "core"), 1)
+
+    vtaps = part(value_taps, ci, cols, 1)
+    lanes = lambda v: jnp.pad(part(v, ci, heads, 0), (0, pad))[None]
+    bias, decays = lanes(step_bias), lanes(log_decay)
+    skip = jnp.repeat(part(skip_gain, ci, heads, 0), cols // heads)[None]
+    gain_mixer = part(mixer_gain, ci, cols, 0)[None]
+    mixer, starts = forward_scan(
+        values_pre, states_pre, step_pre, vtaps, state_taps, bias, decays, skip
+    )
+    gate_lin = project(normed, gate_full)
+    d_out = project(og, out_full)
+    sigmoid_gate = jax.nn.sigmoid(gate_lin)
+    silu_gate = gate_lin * sigmoid_gate
+    gated = mixer * silu_gate
+    weighted = d_out * gain_mixer
+    sums = jnp.stack([jnp.sum(gated * gated, axis=1), jnp.sum(weighted * gated, axis=1)])
+    sums = sums + swap(sums, "core")
+    sums = sums + swap(sums, "heads")
+    inverse = lax.rsqrt(sums[0] / INNER + EPS)[:, None]
+    out_normed = (gated * inverse * gain_mixer).astype(BF)
+    d_gated = inverse * weighted - gated * (inverse * inverse * inverse) * (sums[1][:, None] / INNER)
+    d_mixer = d_gated * silu_gate
+    gate_low = (d_gated * mixer * sigmoid_gate * (1.0 + gate_lin * (1.0 - sigmoid_gate))).astype(BF)
+    g_mixer_gain = jnp.sum(d_out * gated * inverse, axis=0)
+
+    transposed = lambda a, b: lax.dot_general(
+        a, b, (((0,), (0,)), ((), ())), preferred_element_type=F32
+    )
+    back = lambda a, b: lax.dot_general(a, b, (((1,), (1,)), ((), ())), preferred_element_type=F32)
+    g_out = scattered(transposed(og, out_normed))
+    g_gate = scattered(transposed(normed, gate_low))
+    branch = reduced(back(out_normed, out_full))
+    block_output = tokens_back((x_own + branch).astype(BF))
+
+    values_low, d_states, step_low, value_sums, state_sums, step_sums = backward_scan(
+        values_pre, states_pre, step_pre, vtaps, state_taps, bias, decays, skip, mixer, d_mixer, starts
+    )
+    states_own = reduced(d_states, F32).astype(BF)
+    g_value = scattered(transposed(normed, values_low))
+    d_normed = reduced(
+        back(gate_low, gate_full) + back(values_low, weights_in[0]) + back(step_low, weights_in[2])
+    )
+    states_weights = ordered(ci, weights_in[1], swap(weights_in[1], "core"), 1)
+    d_normed = d_normed + back(states_own, states_weights)
+    states_both = jnp.concatenate([states_own, swap(states_own, "core")], axis=0)
+    normed_both = jnp.concatenate([normed_own, normed_core], axis=0)
+    g_small = scattered(
+        jnp.concatenate(
+            [
+                transposed(normed_both, part(states_both, ci, STATE, 1)),
+                transposed(normed, step_low),
+            ],
+            axis=1,
+        )
+    )
+
+    pushed = d_normed * gain
+    d_tokens = scaling * pushed - x_own * (scaling * scaling * scaling) * jnp.mean(
+        pushed * x_own, axis=-1, keepdims=True
+    )
+    grad_input = tokens_back((og_own.astype(F32) + d_tokens).astype(BF))
+    g_input_gain = jnp.sum(d_normed * x_own * scaling, axis=0)
+
+    per_core = jnp.concatenate(
+        [value_sums[:6], g_mixer_gain[None], jnp.pad(step_sums[:2].reshape(1, -1), ((0, 0), (0, cols - 256)))],
+        axis=0,
+    ).reshape(-1, 256)
+    shared = jnp.concatenate([state_sums, g_input_gain.reshape(-1, 256)], axis=0)
+    n_core = per_core.shape[0]
+    pack = jnp.concatenate([per_core, shared], axis=0)
+    pack = pack + swap(pack, "x")
+    pack = pack + swap(pack, "seq", 1)
+    pack = pack + swap(pack, "seq", 2)
+    other = swap(pack, "core")
+    shared = pack[n_core:] + other[n_core:]
+    shared = shared + swap(shared, "heads")
+    both = ordered(ci, pack[:n_core].reshape(1, 8, cols), other[:n_core].reshape(1, 8, cols), 0)
+    by_channel = jnp.transpose(both, (1, 0, 2)).reshape(8, 2 * cols)
+    per_head = both[:, 7, :256].reshape(2, 2, 128)[:, :, :heads]
+    input_gain_all = shared[8:].reshape(nx, 2, nz, rows)
+    my_gain = at(at(at(input_gain_all, xi, 0), ci, 0), zi, 0)
+
+    widths = lambda total: ordered(ci, *to_core(total), 1)
+    small_mine, small_other = to_core(g_small)
+    g_state = ordered(ci, small_mine[:, :STATE], small_other[:, :STATE], 1)
+    g_state = g_state + swap(g_state, "heads")
+    g_step = ordered(ci, small_mine[:, STATE : STATE + heads], small_other[:, STATE : STATE + heads], 1)
+    return (
+        block_output,
+        grad_input,
+        my_gain,
+        widths(g_gate),
+        widths(g_value),
+        g_state,
+        g_step,
+        widths(g_out).T,
+        by_channel[:5],
+        shared[:5],
+        per_head[:, 0].reshape(-1),
+        per_head[:, 1].reshape(-1),
+        jnp.sum(by_channel[5].reshape(2 * heads, -1), axis=1),
+        by_channel[6],
+    )
+
+
 def solution(mesh):
+    sizes = dict(mesh.shape)
+    if sizes["seq"] == 2 * MB and sizes["dp"] == 4 and sizes["heads"] == 2:
+        devices = mesh.devices.reshape(sizes["dp"] // 2, 2, sizes["seq"], sizes["heads"])
+        mesh = jax.sharding.Mesh(devices, ("x", "core", "seq", "heads"))
+        body, dp = whole_sequences, ("x", "core")
+    else:
+        body, dp = shards, ("dp",)
+    tokens = P(None, dp, "seq", None)
+    both = (*dp, "seq")
     return jax.shard_map(
-        shards,
+        body,
         mesh=mesh,
         in_specs=(
-            P(None, "dp", "seq", None),
-            P(None, "dp", "seq", None),
-            P(("dp", "seq")),
-            P(("dp", "seq"), "heads"),
-            P(("dp", "seq"), "heads"),
-            P(("dp", "seq"), None),
-            P(("dp", "seq"), "heads"),
-            P("heads", ("dp", "seq")),
+            tokens,
+            tokens,
+            P(both),
+            P(both, "heads"),
+            P(both, "heads"),
+            P(both, None),
+            P(both, "heads"),
+            P("heads", both),
             P(None, "heads"),
             P(),
             P("heads"),
@@ -347,14 +976,14 @@
             P("heads"),
         ),
         out_specs=(
-            P(None, "dp", "seq", None),
-            P(None, "dp", "seq", None),
-            P(("dp", "seq")),
-            P(("dp", "seq"), "heads"),
-            P(("dp", "seq"), "heads"),
-            P(("dp", "seq"), None),
-            P(("dp", "seq"), "heads"),
-            P("heads", ("dp", "seq")),
+            tokens,
+            tokens,
+            P(both),
+            P(both, "heads"),
+            P(both, "heads"),
+            P(both, None),
+            P(both, "heads"),
+            P("heads", both),
             P(None, "heads"),
             P(),
             P("heads"),

time: 1310 us -> 598 us (0.46)
  waiting for transfers between devices: 541 us -> 257 us
  blocking collectives: 215 us -> 0 us
  matrix products: 197 us -> 49.3 us
  local copies, waits for them, and re-layouts: 187 us -> 66.2 us
  other arithmetic: 125 us -> 34.8 us
  starting transfers between devices: 13.8 us -> 103 us
  Pallas kernels: 0 us -> 79.7 us
  between operations: 18.2 us -> 2.75 us
    reduce_scatter x4 -> x0, waiting for transfers between devices: 340 us -> none  [the longest x1 116 us: shards(): lax.psum_scatter(acc_value, ('dp', 'seq'), scatter_dimension=0, tiled=True)]
    ppermute x4 -> x96, waiting for transfers between devices: 2.94 us -> 257 us  [the longest x56 134 us: swap(): lax.ppermute(x, axis, [(i, i ^ bit) for i in range(lax.axis_size(axis))])]
    dot_general x52 -> x15, matrix products: 194 us -> 49.3 us  [the longest x5 18.4 us: whole_sequences(): lax.dot_general(a, b, (((1,), (1,)), ((), ())), preferred_element_type=F32)]
    psum x1 -> x0, waiting for transfers between devices: 129 us -> none  [shards(): branch = lax.psum(partial_out, 'heads')]
    all_gather x4 -> x0, blocking collectives: 97.1 us -> none  [the longest x1 44.4 us: shards(): lax.all_gather(state_weight, ('dp', 'seq'), axis=0, tiled=True)]
    unnamed x2 -> x0, blocking collectives: 90.7 us -> none
    ppermute x4 -> x96, starting transfers between devices: 13 us -> 103 us  [the longest x56 38.9 us: swap(): lax.ppermute(x, axis, [(i, i ^ bit) for i in range(lax.axis_size(axis))])]
    pallas_call x0 -> x11, Pallas kernels: none -> 79.7 us  [the longest x1 33 us: backward_scan(): pl.pallas_call(backward_kernel, grid=(chunks,), in_specs=[row(width), bef...]
  transfers between devices with their start and end apart: 17 -> 96, of which waited for: 9 -> 42; matrix products, arithmetic and copies ran while one was open for 25% -> 15% of each run, Pallas kernels for 0% -> 7%
where the time goes in v1:
time: 598 us; the launch traced here: 593 us
  waiting for transfers between devices  257 us (43%)
  starting transfers between devices  103 us (17%)
  Pallas kernels  79.7 us (13%)
  local copies, waits for them, and re-layouts  66.2 us (11%)
  matrix products  49.3 us (8%)
  other arithmetic  34.8 us (6%)
    ppermute x56, waiting for transfers between devices, swap(): lax.ppermute(x, axis, [(i, i ^ bit) for i in range(lax.axis_size(axis))])  134 us
    ppermute x24, waiting for transfers between devices, turned(): return lax.ppermute(x, axis, [(i, (i + distance) % n) for i in range(n)])  74.4 us
    ppermute x56, starting transfers between devices, swap(): lax.ppermute(x, axis, [(i, i ^ bit) for i in range(lax.axis_size(axis))])  38.9 us
    ppermute x24, starting transfers between devices, turned(): return lax.ppermute(x, axis, [(i, (i + distance) % n) for i in range(n)])  37.5 us
    pallas_call x1, Pallas kernels, backward_scan(): pl.pallas_call(backward_kernel, grid=(chunks,), in_specs=[row(width), bef...  33 us
    pallas_call x9, Pallas kernels, place(): pl.pallas_call(kernel, grid_spec=pltpu.PrefetchScalarGridSpec(num_scalar_...  31.7 us
    ppermute x8, waiting for transfers between devices, tokens_in(): lax.ppermute(piece.reshape(sub, d_model), ('core', 'seq'), route)  31.4 us
    unnamed x208, local copies, waits for them, and re-layouts  23.3 us
  transfers between devices with their start and end apart: 96, of which 42 were waited for; matrix products, arithmetic and copies ran while one was open for 15% of the time, Pallas kernels for 7%

profile of v1, /device:TPU:8, one launch (start us, length us, event | category | flops | bytes accessed | tf_op | source)
XLA Modules:
  0.0 592.8 jit_solution(14209463352676806579)
XLA Ops:
  24.0 2.7 collective-permute-start.3
  27.9 2.8 collective-permute-start.29
  32.8 8.9 %collective-permute-done.2.refs_2_ = bf16[64,1536]{1,0:T(8,128)(2,1)S(1)} collective-permute-done((bf16[64,1536]{1,0:T(8,128)(2,1)}, bf16[64,1536]{1,0:T(8,128)(2,1)S(1)}, u32[]{:S(2)}, u32[]{:S(2)}) %collective-permute-start.2) | collective-permute-done | bytes 196640 | tf_op jit(solution)/shard_map/ppermute | solution.py:732
  41.8 4.6 collective-permute-done.3.refs_3_
  49.8 7.7 %collective-permute-start.37 = (bf16[192,768]{1,0:T(8,128)(2,1)S(1)}, bf16[192,768]{1,0:T(8,128)(2,1)S(1)}, u32[]{:S(2)}, u32[]{:S(2)}) collective-permute-start(bf16[192,768]{1,0:T(8,128)(2,1)S(1)} %pad_maximum_fusion.5.refs_0_), channel_id=1, source_target_pairs={{0,2},{2,4},{4,6},{6,0},{1,3},{3,5},{5,7},{7,1},{8,10},{10,12},{12... | collective-permute-start | bytes 884744 | tf_op jit(solution)/shard_map/ppermute | solution.py:687
  60.2 16.9 %collective-permute-done.32.refs_3_ = bf16[64,1536]{1,0:T(8,128)(2,1)S(1)} collective-permute-done((bf16[64,1536]{1,0:T(8,128)(2,1)S(1)}, bf16[64,1536]{1,0:T(8,128)(2,1)S(1)}, u32[]{:S(2)}, u32[]{:S(2)}) %collective-permute-start.32) | collective-permute-done | bytes 196640 | tf_op jit(solution)/shard_map/ppermute | solution.py:732
  78.7 2.5 collective-permute-start.13
  84.3 3.0 collective-permute-done.38.refs_2_
  91.8 5.7 collective-permute-done.13.refs_1_
  99.0 5.2 collective-permute-done.14.refs_2_
  108.0 4.3 collective-permute-done.24.refs_3_
  125.6 11.8 %collective-permute-done.42.refs_6_ = bf16[192,768]{1,0:T(8,128)(2,1)S(1)} collective-permute-done((bf16[192,768]{1,0:T(8,128)(2,1)S(1)}, bf16[192,768]{1,0:T(8,128)(2,1)S(1)}, u32[]{:S(2)}, u32[]{:S(2)}) %collective-permute-start.42) | collective-permute-done | bytes 294944 | tf_op jit(solution)/shard_map/ppermute | solution.py:682
  142.9 5.7 collective-permute-done.28.refs_7_
  150.8 4.1 collective-permute-done.43.refs_7_
  164.6 4.0 place.12
  168.7 4.0 place.15
  173.4 4.0 place.11
  180.6 5.0 place.10
  188.0 2.6 fusion.3.vpre.vbefore
  190.6 3.0 place.14
  193.6 4.3 fusion.88
  198.6 15.1 %scan_forward.1 = (f32[1024,768]{1,0:T(8,128)S(1)}, f32[4,128,768]{2,1,0:T(8,128)S(1)}) custom-call(f32[1024,768]{1,0:T(8,128)S(1)} %fusion.3.vpre.vbefore, f32[1024,256]{1,0:T(8,128)S(1)} %pad_maximum_fusion.spre.sbefore, f32[1024,128]{1,0:T(8,128)S(1)} %fusion.43.spre_step, f32[5,768]{1,0:T(8,128)S(1)} %constant_dynamic-slice_fusion.14.vtaps, ...), custom_call_target="tpu_custom_call" | custom-call | flops 3221225472 | bytes 6291456 | tf_op jit(solution)/shard_map/scan_forward/pallas_call | solution.py:435
  213.8 5.2 multiply_reduce_fusion.2
  224.1 7.9 %fusion.81 = f32[1536,768]{1,0:T(8,128)} fusion(bf16[1024,1536]{1,0:T(8,128)(2,1)} %copy-done.6, f32[1024,768]{1,0:T(8,128)} %get-tuple-element.92, f32[1024]{0:T(1024)S(1)} %bitcast.304, f32[768]{0:T(1024)S(1)} %dynamic_slice.250), kind=kOutput, calls=%fused_computation.232 | convolution fusion | flops 2418278400 | bytes 11017216 | tf_op jit(solution)/shard_map/dot_general | solution.py:869
  232.0 3.8 fusion.20
  236.3 33.0 %scan_backward.1 = (bf16[1024,768]{1,0:T(8,128)(2,1)S(1)}, f32[1024,256]{1,0:T(8,128)S(1)}, bf16[1024,128]{1,0:T(8,128)(2,1)S(1)}, f32[8,768]{1,0:T(8,128)S(1)},...) custom-call(f32[1024,768]{1,0:T(8,128)S(1)} %copy-done.61, f32[1024,768]{1,0:T(8,128)S(1)} %copy-done.61, ...), custom_call_target="tpu_custom_call" | custom-call | flops 6442450944 | bytes 12582912 | tf_op jit(solution)/shard_map/scan_backward/pallas_call | solution.py:606
  269.3 4.6 fusion.1
  274.0 4.3 fusion.91
  278.3 4.7 fusion.89
  283.1 2.7 fusion.90
  285.8 2.7 fusion.82
  288.4 5.6 add_add_fusion
  294.0 3.1 constant_dynamic-slice_fusion.6
  297.2 2.9 dynamic-slice_convert_fusion
  300.6 2.8 dynamic-slice_convert_fusion.1
  306.6 3.2 constant_dynamic-slice_fusion.12
  313.8 5.1 collective-permute-done.59
  320.7 3.9 copy.159
  334.4 20.0 %collective-permute-done.79 = bf16[768,768]{1,0:T(8,128)(2,1)} collective-permute-done((bf16[768,768]{1,0:T(8,128)(2,1)}, bf16[768,768]{1,0:T(8,128)(2,1)}, u32[]{:S(2)}, u32[]{:S(2)}) %collective-permute-start.79) | collective-permute-done | bytes 1179680 | tf_op jit(solution)/shard_map/ppermute | solution.py:682
  357.1 22.6 %collective-permute-done.74 = bf16[768,768]{1,0:T(8,128)(2,1)} collective-permute-done((bf16[768,768]{1,0:T(8,128)(2,1)}, bf16[768,768]{1,0:T(8,128)(2,1)}, u32[]{:S(2)}, u32[]{:S(2)}) %collective-permute-start.74) | collective-permute-done | bytes 1179680 | tf_op jit(solution)/shard_map/ppermute | solution.py:682
  381.4 6.3 %collective-permute-done.85 = bf16[768,256]{0,1:T(8,128)(2,1)S(1)} collective-permute-done((bf16[768,256]{0,1:T(8,128)(2,1)S(1)}, bf16[768,256]{0,1:T(8,128)(2,1)S(1)}, u32[]{:S(2)}, u32[]{:S(2)}) %collective-permute-start.85) | collective-permute-done | bytes 393248 | tf_op jit(solution)/shard_map/ppermute | solution.py:682
  393.0 11.7 %collective-permute-done.86 = bf16[2,96,256]{2,1,0:T(8,128)(2,1)S(1)} collective-permute-done((bf16[2,96,256]{2,1,0:T(8,128)(2,1)S(1)}, bf16[2,96,256]{2,1,0:T(8,128)(2,1)S(1)}, u32[]{:S(2)}, u32[]{:S(2)}) %collective-permute-start.86) | collective-permute-done | bytes 98336 | tf_op jit(solution)/shard_map/ppermute | solution.py:687
  407.2 2.6 collective-permute-start.81
  412.0 13.9 %collective-permute-done.94 = bf16[2,96,768]{2,1,0:T(8,128)(2,1)S(1)} collective-permute-done((bf16[2,96,768]{2,1,0:T(8,128)(2,1)}, bf16[2,96,768]{2,1,0:T(8,128)(2,1)S(1)}, u32[]{:S(2)}, u32[]{:S(2)}) %collective-permute-start.94) | collective-permute-done | bytes 294944 | tf_op jit(solution)/shard_map/ppermute | solution.py:687
  430.0 3.8 collective-permute-done.81
  433.8 3.3 collective-permute-start.76
  437.1 15.9 %collective-permute-done.82 = bf16[2,96,768]{2,1,0:T(8,128)(2,1)S(1)} collective-permute-done((bf16[2,96,768]{2,1,0:T(8,128)(2,1)}, bf16[2,96,768]{2,1,0:T(8,128)(2,1)S(1)}, u32[]{:S(2)}, u32[]{:S(2)}) %collective-permute-start.82) | collective-permute-done | bytes 294944 | tf_op jit(solution)/shard_map/ppermute | solution.py:687
  456.4 6.0 %collective-permute-done.77 = bf16[2,96,768]{2,1,0:T(8,128)(2,1)S(1)} collective-permute-done((bf16[2,96,768]{2,1,0:T(8,128)(2,1)S(1)}, bf16[2,96,768]{2,1,0:T(8,128)(2,1)S(1)}, u32[]{:S(2)}, u32[]{:S(2)}) %collective-permute-start.77) | collective-permute-done | bytes 294944 | tf_op jit(solution)/shard_map/ppermute | solution.py:687
  464.3 4.6 collective-permute-done.90
  474.5 2.6 bitcast_add_fusion
  484.5 13.2 %collective-permute-done.57 = bf16[4,64,1536]{2,1,0:T(8,128)(2,1)S(1)} collective-permute-done((bf16[4,64,1536]{2,1,0:T(8,128)(2,1)S(1)}, bf16[4,64,1536]{2,1,0:T(8,128)(2,1)S(1)}, u32[]{:S(2)}, u32[]{:S(2)}) %collective-permute-start.57) | collective-permute-done | bytes 786464 | tf_op jit(solution)/shard_map/ppermute | solution.py:682
  499.4 14.8 %collective-permute-done.47 = bf16[4,64,1536]{2,1,0:T(8,128)(2,1)} collective-permute-done((bf16[4,64,1536]{2,1,0:T(8,128)(2,1)}, bf16[4,64,1536]{2,1,0:T(8,128)(2,1)}, u32[]{:S(2)}, u32[]{:S(2)}) %collective-permute-start.47) | collective-permute-done | bytes 786464 | tf_op jit(solution)/shard_map/ppermute | solution.py:682
  522.2 3.2 collective-permute-start.63
  528.4 3.4 collective-permute-done.73
  534.0 2.8 collective-permute-start.50
  538.7 3.8 collective-permute-start.51
  542.5 10.0 %collective-permute-done.64.refs_3_ = bf16[64,1536]{1,0:T(8,128)(2,1)S(1)} collective-permute-done((bf16[64,1536]{1,0:T(8,128)(2,1)S(1)}, bf16[64,1536]{1,0:T(8,128)(2,1)S(1)}, u32[]{:S(2)}, u32[]{:S(2)}) %collective-permute-start.64) | collective-permute-done | bytes 196640 | tf_op jit(solution)/shard_map/ppermute | solution.py:744
  556.6 3.9 collective-permute-done.51.refs_3_
  564.8 3.9 collective-permute-done.67.refs_6_
  573.4 3.8 place.17
  577.2 4.2 collective-permute-done.53.refs_5_
  581.4 4.2 collective-permute-done.54.refs_6_
  585.6 3.2 collective-permute-done.55.refs_7_
  588.7 3.8 place.16
  (499 shorter events, 175.1 us)
Async XLA Ops:
  2.5 21.6 %collective-permute-start.21 = (bf16[96,768]{1,0:T(8,128)(2,1)}, bf16[96,768]{1,0:T(8,128)(2,1)}, u32[]{:S(2)}, u32[]{:S(2)}) collective-permute-start(bf16[96,768]{1,0:T(8,128)(2,1)} %constant_dynamic-slice_fusion.13), channel_id=1, source_target_pairs={{0,8},{8,0},{1,9},{9,1},{2,10},{10,2},{3,11},{11,3},{4,12},{12,4},... | collective-permute-start | bytes 442376 | tf_op jit(solution)/shard_map/ppermute | solution.py:682
  3.4 23.4 %collective-permute-start.36 = (bf16[96,768]{1,0:T(8,128)(2,1)S(1)}, bf16[96,768]{1,0:T(8,128)(2,1)}, u32[]{:S(2)}, u32[]{:S(2)}) collective-permute-start(bf16[96,768]{1,0:T(8,128)(2,1)S(1)} %dynamic-slice_bitcast_fusion.13), channel_id=1, source_target_pairs={{0,8},{8,0},{1,9},{9,1},{2,10},{10,2},{3,11},{11,3},{4,12},{12,4},... | collective-permute-start | bytes 442376 | tf_op jit(solution)/shard_map/ppermute | solution.py:682
  23.9 17.8 %collective-permute-start.2 = (bf16[64,1536]{1,0:T(8,128)(2,1)}, bf16[64,1536]{1,0:T(8,128)(2,1)S(1)}, u32[]{:S(2)}, u32[]{:S(2)}) collective-permute-start(bf16[64,1536]{1,0:T(8,128)(2,1)} %get-tuple-element.118), channel_id=1, source_target_pairs={{0,4},{2,12},{4,0},{6,8},{8,6},{10,14},{12,2},{14,10},{1,5},{3,13}... | collective-permute-start | bytes 589832 | tf_op jit(solution)/shard_map/ppermute | solution.py:732
  24.0 22.3 %collective-permute-start.3 = (bf16[64,1536]{1,0:T(8,128)(2,1)}, bf16[64,1536]{1,0:T(8,128)(2,1)S(1)}, u32[]{:S(2)}, u32[]{:S(2)}) collective-permute-start(bf16[64,1536]{1,0:T(8,128)(2,1)} %get-tuple-element.115), channel_id=1, source_target_pairs={{0,12},{2,4},{4,8},{6,0},{8,14},{10,6},{12,10},{14,2},{1,13},{3,5}... | collective-permute-start | bytes 589832 | tf_op jit(solution)/shard_map/ppermute | solution.py:732
  27.9 20.3 %collective-permute-start.29 = (bf16[64,1536]{1,0:T(8,128)(2,1)}, bf16[64,1536]{1,0:T(8,128)(2,1)S(1)}, u32[]{:S(2)}, u32[]{:S(2)}) collective-permute-start(bf16[64,1536]{1,0:T(8,128)(2,1)} %get-tuple-element.113), channel_id=1, source_target_pairs={{0,0},{2,8},{4,4},{6,12},{8,2},{10,10},{12,6},{14,14},{1,1},{3,9},... | collective-permute-start | bytes 589832 | tf_op jit(solution)/shard_map/ppermute | solution.py:732
  30.7 19.0 %collective-permute-start.30 = (bf16[64,1536]{1,0:T(8,128)(2,1)S(1)}, bf16[64,1536]{1,0:T(8,128)(2,1)S(1)}, u32[]{:S(2)}, u32[]{:S(2)}) collective-permute-start(bf16[64,1536]{1,0:T(8,128)(2,1)S(1)} %copy-done.87), channel_id=1, source_target_pairs={{0,8},{2,0},{4,12},{6,4},{8,10},{10,2},{12,14},{14,6},{1,9},{3,1},... | collective-permute-start | bytes 589832 | tf_op jit(solution)/shard_map/ppermute | solution.py:732
  31.0 27.4 %collective-permute-start.31 = (bf16[64,1536]{1,0:T(8,128)(2,1)S(1)}, bf16[64,1536]{1,0:T(8,128)(2,1)S(1)}, u32[]{:S(2)}, u32[]{:S(2)}) collective-permute-start(bf16[64,1536]{1,0:T(8,128)(2,1)S(1)} %get-tuple-element.114), channel_id=1, source_target_pairs={{0,4},{2,12},{4,0},{6,8},{8,6},{10,14},{12,2},{14,10},{1,5},{3,13}... | collective-permute-start | bytes 589832 | tf_op jit(solution)/shard_map/ppermute | solution.py:732
  41.8 35.3 %collective-permute-start.22 = (bf16[192,768]{1,0:T(8,128)(2,1)S(1)}, bf16[192,768]{1,0:T(8,128)(2,1)S(1)}, u32[]{:S(2)}, u32[]{:S(2)}) collective-permute-start(bf16[192,768]{1,0:T(8,128)(2,1)S(1)} %pad_maximum_fusion.4.refs_0_), channel_id=1, source_target_pairs={{0,2},{2,4},{4,6},{6,0},{1,3},{3,5},{5,7},{7,1},{8,10},{10,12},{12... | collective-permute-start | bytes 884744 | tf_op jit(solution)/shard_map/ppermute | solution.py:687
  46.3 32.3 %collective-permute-start.23 = (bf16[192,768]{1,0:T(8,128)(2,1)S(1)}, bf16[192,768]{1,0:T(8,128)(2,1)S(1)}, u32[]{:S(2)}, u32[]{:S(2)}) collective-permute-start(bf16[192,768]{1,0:T(8,128)(2,1)S(1)} %pad_maximum_fusion.4.refs_0_), channel_id=1, source_target_pairs={{0,6},{2,0},{4,2},{6,4},{1,7},{3,1},{5,3},{7,5},{8,14},{10,8},{12,... | collective-permute-start | bytes 884744 | tf_op jit(solution)/shard_map/ppermute | solution.py:687
  48.2 33.0 %collective-permute-start.25 = (bf16[192,768]{1,0:T(8,128)(2,1)S(1)}, bf16[192,768]{1,0:T(8,128)(2,1)S(1)}, u32[]{:S(2)}, u32[]{:S(2)}) collective-permute-start(bf16[192,768]{1,0:T(8,128)(2,1)S(1)} %pad_maximum_fusion.4.refs_0_), channel_id=1, source_target_pairs={{0,16},{16,0},{1,17},{17,1},{2,18},{18,2},{3,19},{19,3},{4,20},{20... | collective-permute-start | bytes 884744 | tf_op jit(solution)/shard_map/ppermute | solution.py:682
  49.8 33.7 %collective-permute-start.37 = (bf16[192,768]{1,0:T(8,128)(2,1)S(1)}, bf16[192,768]{1,0:T(8,128)(2,1)S(1)}, u32[]{:S(2)}, u32[]{:S(2)}) collective-permute-start(bf16[192,768]{1,0:T(8,128)(2,1)S(1)} %pad_maximum_fusion.5.refs_0_), channel_id=1, source_target_pairs={{0,2},{2,4},{4,6},{6,0},{1,3},{3,5},{5,7},{7,1},{8,10},{10,12},{12... | collective-permute-start | bytes 884744 | tf_op jit(solution)/shard_map/ppermute | solution.py:687
  58.4 18.7 %collective-permute-start.32 = (bf16[64,1536]{1,0:T(8,128)(2,1)S(1)}, bf16[64,1536]{1,0:T(8,128)(2,1)S(1)}, u32[]{:S(2)}, u32[]{:S(2)}) collective-permute-start(bf16[64,1536]{1,0:T(8,128)(2,1)S(1)} %get-tuple-element.111), channel_id=1, source_target_pairs={{0,12},{2,4},{4,8},{6,0},{8,14},{10,6},{12,10},{14,2},{1,13},{3,5}... | collective-permute-start | bytes 589832 | tf_op jit(solution)/shard_map/ppermute | solution.py:732
  78.7 18.8 %collective-permute-start.13 = (bf16[192,1024]{1,0:T(8,128)(2,1)S(1)}, bf16[192,1024]{1,0:T(8,128)(2,1)S(1)}, u32[]{:S(2)}, u32[]{:S(2)}) collective-permute-start(bf16[192,1024]{1,0:T(8,128)(2,1)S(1)} %pad_maximum_fusion.3.refs_0_), channel_id=1, source_target_pairs={{0,2},{2,4},{4,6},{6,0},{1,3},{3,5},{5,7},{7,1},{8,10},{10,12},{12... | collective-permute-start | bytes 1179656 | tf_op jit(solution)/shard_map/ppermute | solution.py:687
  81.9 22.4 %collective-permute-start.14 = (bf16[192,1024]{1,0:T(8,128)(2,1)S(1)}, bf16[192,1024]{1,0:T(8,128)(2,1)}, u32[]{:S(2)}, u32[]{:S(2)}) collective-permute-start(bf16[192,1024]{1,0:T(8,128)(2,1)S(1)} %pad_maximum_fusion.3.refs_0_), channel_id=1, source_target_pairs={{0,6},{2,0},{4,2},{6,4},{1,7},{3,1},{5,3},{7,5},{8,14},{10,8},{12,... | collective-permute-start | bytes 1179656 | tf_op jit(solution)/shard_map/ppermute | solution.py:687
  83.5 22.2 %collective-permute-start.16 = (bf16[192,1024]{1,0:T(8,128)(2,1)S(1)}, bf16[192,1024]{1,0:T(8,128)(2,1)S(1)}, u32[]{:S(2)}, u32[]{:S(2)}) collective-permute-start(bf16[192,1024]{1,0:T(8,128)(2,1)S(1)} %pad_maximum_fusion.3.refs_0_), channel_id=1, source_target_pairs={{0,16},{16,0},{1,17},{17,1},{2,18},{18,2},{3,19},{19,3},{4,20},{20... | collective-permute-start | bytes 1179656 | tf_op jit(solution)/shard_map/ppermute | solution.py:682
  87.3 50.8 %collective-permute-start.9 = (bf16[256,1536]{1,0:T(8,128)(2,1)S(1)}, bf16[256,1536]{1,0:T(8,128)(2,1)S(1)}, u32[]{:S(2)}, u32[]{:S(2)}) collective-permute-start(bf16[256,1536]{1,0:T(8,128)(2,1)S(1)} %fusion.7.refs_0_), channel_id=1, source_target_pairs={{0,1},{1,0},{2,3},{3,2},{4,5},{5,4},{6,7},{7,6},{8,9},{9,8},{10,11... | collective-permute-start | bytes 2359304 | tf_op jit(solution)/shard_map/ppermute | solution.py:682
  89.6 22.7 %collective-permute-start.24 = (bf16[192,768]{1,0:T(8,128)(2,1)S(1)}, bf16[192,768]{1,0:T(8,128)(2,1)S(1)}, u32[]{:S(2)}, u32[]{:S(2)}) collective-permute-start(bf16[192,768]{1,0:T(8,128)(2,1)S(1)} %collective-permute-done.22.refs_1_), channel_id=1, source_target_pairs={{0,2},{2,4},{4,6},{6,0},{1,3},{3,5},{5,7},{7,1},{8,10},{10,12},{12... | collective-permute-start | bytes 884744 | tf_op jit(solution)/shard_map/ppermute | solution.py:687
  97.5 15.2 %collective-permute-start.26 = (bf16[192,768]{1,0:T(8,128)(2,1)S(1)}, bf16[192,768]{1,0:T(8,128)(2,1)S(1)}, u32[]{:S(2)}, u32[]{:S(2)}) collective-permute-start(bf16[192,768]{1,0:T(8,128)(2,1)S(1)} %collective-permute-done.22.refs_1_), channel_id=1, source_target_pairs={{0,16},{16,0},{1,17},{17,1},{2,18},{18,2},{3,19},{19,3},{4,20},{20... | collective-permute-start | bytes 884744 | tf_op jit(solution)/shard_map/ppermute | solution.py:682
  112.3 26.4 %collective-permute-start.15 = (bf16[192,1024]{1,0:T(8,128)(2,1)S(1)}, bf16[192,1024]{1,0:T(8,128)(2,1)}, u32[]{:S(2)}, u32[]{:S(2)}) collective-permute-start(bf16[192,1024]{1,0:T(8,128)(2,1)S(1)} %collective-permute-done.13.refs_1_), channel_id=1, source_target_pairs={{0,2},{2,4},{4,6},{6,0},{1,3},{3,5},{5,7},{7,1},{8,10},{10,12},{12... | collective-permute-start | bytes 1179656 | tf_op jit(solution)/shard_map/ppermute | solution.py:687
  115.7 25.2 %collective-permute-start.17 = (bf16[192,1024]{1,0:T(8,128)(2,1)S(1)}, bf16[192,1024]{1,0:T(8,128)(2,1)S(1)}, u32[]{:S(2)}, u32[]{:S(2)}) collective-permute-start(bf16[192,1024]{1,0:T(8,128)(2,1)S(1)} %collective-permute-done.13.refs_1_), channel_id=1, source_target_pairs={{0,16},{16,0},{1,17},{17,1},{2,18},{18,2},{3,19},{19,3},{4,20},{20... | collective-permute-start | bytes 1179656 | tf_op jit(solution)/shard_map/ppermute | solution.py:682
  118.6 18.8 %collective-permute-start.42 = (bf16[192,768]{1,0:T(8,128)(2,1)S(1)}, bf16[192,768]{1,0:T(8,128)(2,1)S(1)}, u32[]{:S(2)}, u32[]{:S(2)}) collective-permute-start(bf16[192,768]{1,0:T(8,128)(2,1)S(1)} %collective-permute-done.38.refs_2_), channel_id=1, source_target_pairs={{0,16},{16,0},{1,17},{17,1},{2,18},{18,2},{3,19},{19,3},{4,20},{20... | collective-permute-start | bytes 884744 | tf_op jit(solution)/shard_map/ppermute | solution.py:682
  124.0 48.8 %collective-permute-start.33 = (bf16[256,1536]{1,0:T(8,128)(2,1)}, bf16[256,1536]{1,0:T(8,128)(2,1)}, u32[]{:S(2)}, u32[]{:S(2)}) collective-permute-start(bf16[256,1536]{1,0:T(8,128)(2,1)} %place.13.refs_0_), channel_id=1, source_target_pairs={{0,1},{1,0},{2,3},{3,2},{4,5},{5,4},{6,7},{7,6},{8,9},{9,8},{10,11... | collective-permute-start | bytes 2359304 | tf_op jit(solution)/shard_map/ppermute | solution.py:682
  138.1 40.4 %collective-permute-start.10 = (bf16[256,1536]{1,0:T(8,128)(2,1)S(1)}, bf16[256,1536]{1,0:T(8,128)(2,1)S(1)}, u32[]{:S(2)}, u32[]{:S(2)}) collective-permute-start(bf16[256,1536]{1,0:T(8,128)(2,1)S(1)} %fusion.7.refs_0_), channel_id=1, source_target_pairs={{0,8},{8,0},{1,9},{9,1},{2,10},{10,2},{3,11},{11,3},{4,12},{12,4},... | collective-permute-start | bytes 2359304 | tf_op jit(solution)/shard_map/ppermute | solution.py:682
  138.1 41.4 %collective-permute-start.11 = (bf16[256,1536]{1,0:T(8,128)(2,1)S(1)}, bf16[256,1536]{1,0:T(8,128)(2,1)}, u32[]{:S(2)}, u32[]{:S(2)}) collective-permute-start(bf16[256,1536]{1,0:T(8,128)(2,1)S(1)} %collective-permute-done.9.refs_1_), channel_id=1, source_target_pairs={{0,8},{8,0},{1,9},{9,1},{2,10},{10,2},{3,11},{11,3},{4,12},{12,4},... | collective-permute-start | bytes 2359304 | tf_op jit(solution)/shard_map/ppermute | solution.py:682
  141.7 13.2 %collective-permute-start.43 = (bf16[192,768]{1,0:T(8,128)(2,1)S(1)}, bf16[192,768]{1,0:T(8,128)(2,1)S(1)}, u32[]{:S(2)}, u32[]{:S(2)}) collective-permute-start(bf16[192,768]{1,0:T(8,128)(2,1)S(1)} %collective-permute-done.39.refs_3_), channel_id=1, source_target_pairs={{0,16},{16,0},{1,17},{17,1},{2,18},{18,2},{3,19},{19,3},{4,20},{20... | collective-permute-start | bytes 884744 | tf_op jit(solution)/shard_map/ppermute | solution.py:682
  149.3 23.5 %collective-permute-start.18 = (bf16[192,1024]{1,0:T(8,128)(2,1)}, bf16[192,1024]{1,0:T(8,128)(2,1)}, u32[]{:S(2)}, u32[]{:S(2)}) collective-permute-start(bf16[192,1024]{1,0:T(8,128)(2,1)} %collective-permute-done.14.refs_2_), channel_id=1, source_target_pairs={{0,16},{16,0},{1,17},{17,1},{2,18},{18,2},{3,19},{19,3},{4,20},{20... | collective-permute-start | bytes 1179656 | tf_op jit(solution)/shard_map/ppermute | solution.py:682
  155.6 17.8 %collective-permute-start.19 = (bf16[192,1024]{1,0:T(8,128)(2,1)}, bf16[192,1024]{1,0:T(8,128)(2,1)}, u32[]{:S(2)}, u32[]{:S(2)}) collective-permute-start(bf16[192,1024]{1,0:T(8,128)(2,1)} %collective-permute-done.15.refs_3_), channel_id=1, source_target_pairs={{0,16},{16,0},{1,17},{17,1},{2,18},{18,2},{3,19},{19,3},{4,20},{20... | collective-permute-start | bytes 1179656 | tf_op jit(solution)/shard_map/ppermute | solution.py:682
  172.8 17.8 %collective-permute-start.34 = (bf16[256,1536]{1,0:T(8,128)(2,1)}, bf16[256,1536]{1,0:T(8,128)(2,1)S(1)}, u32[]{:S(2)}, u32[]{:S(2)}) collective-permute-start(bf16[256,1536]{1,0:T(8,128)(2,1)} %place.13.refs_0_), channel_id=1, source_target_pairs={{0,8},{8,0},{1,9},{9,1},{2,10},{10,2},{3,11},{11,3},{4,12},{12,4},... | collective-permute-start | bytes 2359304 | tf_op jit(solution)/shard_map/ppermute | solution.py:682
  172.9 17.7 %collective-permute-start.35 = (bf16[256,1536]{1,0:T(8,128)(2,1)}, bf16[256,1536]{1,0:T(8,128)(2,1)S(1)}, u32[]{:S(2)}, u32[]{:S(2)}) collective-permute-start(bf16[256,1536]{1,0:T(8,128)(2,1)} %collective-permute-done.33.refs_1_), channel_id=1, source_target_pairs={{0,8},{8,0},{1,9},{9,1},{2,10},{10,2},{3,11},{11,3},{4,12},{12,4},... | collective-permute-start | bytes 2359304 | tf_op jit(solution)/shard_map/ppermute | solution.py:682
  178.4 43.4 %collective-permute-start.60 = (bf16[1536,128]{1,0:T(8,128)(2,1)}, bf16[1536,128]{1,0:T(8,128)(2,1)}, u32[]{:S(2)}, u32[]{:S(2)}) collective-permute-start(bf16[1536,128]{1,0:T(8,128)(2,1)} %slice.128), channel_id=1, source_target_pairs={{0,8},{8,0},{1,9},{9,1},{2,10},{10,2},{3,11},{11,3},{4,12},{12,4},... | collective-permute-start | bytes 1179656 | tf_op jit(solution)/shard_map/ppermute | solution.py:682
  300.1 29.1 %collective-permute-start.91 = (bf16[768,768]{1,0:T(8,128)(2,1)}, bf16[768,768]{1,0:T(8,128)(2,1)}, u32[]{:S(2)}, u32[]{:S(2)}) collective-permute-start(bf16[768,768]{1,0:T(8,128)(2,1)} %dynamic-slice_convert_fusion), channel_id=1, source_target_pairs={{0,16},{16,0},{1,17},{17,1},{2,18},{18,2},{3,19},{19,3},{4,20},{20... | collective-permute-start | bytes 3538952 | tf_op jit(solution)/shard_map/ppermute | solution.py:682
  303.4 51.0 %collective-permute-start.79 = (bf16[768,768]{1,0:T(8,128)(2,1)}, bf16[768,768]{1,0:T(8,128)(2,1)}, u32[]{:S(2)}, u32[]{:S(2)}) collective-permute-start(bf16[768,768]{1,0:T(8,128)(2,1)} %dynamic-slice_convert_fusion.1), channel_id=1, source_target_pairs={{0,16},{16,0},{1,17},{17,1},{2,18},{18,2},{3,19},{19,3},{4,20},{20... | collective-permute-start | bytes 3538952 | tf_op jit(solution)/shard_map/ppermute | solution.py:682
  306.0 73.7 %collective-permute-start.74 = (bf16[768,768]{1,0:T(8,128)(2,1)}, bf16[768,768]{1,0:T(8,128)(2,1)}, u32[]{:S(2)}, u32[]{:S(2)}) collective-permute-start(bf16[768,768]{1,0:T(8,128)(2,1)} %dynamic-slice_convert_fusion.2), channel_id=1, source_target_pairs={{0,16},{16,0},{1,17},{17,1},{2,18},{18,2},{3,19},{19,3},{4,20},{20... | collective-permute-start | bytes 3538952 | tf_op jit(solution)/shard_map/ppermute | solution.py:682
  327.7 60.0 %collective-permute-start.85 = (bf16[768,256]{0,1:T(8,128)(2,1)S(1)}, bf16[768,256]{0,1:T(8,128)(2,1)S(1)}, u32[]{:S(2)}, u32[]{:S(2)}) collective-permute-start(bf16[768,256]{0,1:T(8,128)(2,1)S(1)} %fusion.24), channel_id=1, source_target_pairs={{0,16},{16,0},{1,17},{17,1},{2,18},{18,2},{3,19},{19,3},{4,20},{20... | collective-permute-start | bytes 1179656 | tf_op jit(solution)/shard_map/ppermute | solution.py:682
  332.5 77.3 %collective-permute-start.92 = (bf16[2,96,768]{2,1,0:T(8,128)(2,1)}, bf16[2,96,768]{2,1,0:T(8,128)(2,1)}, u32[]{:S(2)}, u32[]{:S(2)}) collective-permute-start(bf16[2,96,768]{2,1,0:T(8,128)(2,1)} %get-tuple-element.102), channel_id=1, source_target_pairs={{0,2},{2,4},{4,6},{6,0},{1,3},{3,5},{5,7},{7,1},{8,10},{10,12},{12... | collective-permute-start | bytes 884744 | tf_op jit(solution)/shard_map/ppermute | solution.py:687
  333.6 78.4 %collective-permute-start.93 = (bf16[2,96,768]{2,1,0:T(8,128)(2,1)}, bf16[2,96,768]{2,1,0:T(8,128)(2,1)}, u32[]{:S(2)}, u32[]{:S(2)}) collective-permute-start(bf16[2,96,768]{2,1,0:T(8,128)(2,1)} %get-tuple-element.103), channel_id=1, source_target_pairs={{0,4},{2,6},{4,0},{6,2},{1,5},{3,7},{5,1},{7,3},{8,12},{10,14},{12... | collective-permute-start | bytes 884744 | tf_op jit(solution)/shard_map/ppermute | solution.py:687
  390.1 14.6 %collective-permute-start.86 = (bf16[2,96,256]{2,1,0:T(8,128)(2,1)S(1)}, bf16[2,96,256]{2,1,0:T(8,128)(2,1)S(1)}, u32[]{:S(2)}, u32[]{:S(2)}) collective-permute-start(bf16[2,96,256]{2,1,0:T(8,128)(2,1)S(1)} %get-tuple-element.127), channel_id=1, source_target_pairs={{0,2},{2,4},{4,6},{6,0},{1,3},{3,5},{5,7},{7,1},{8,10},{10,12},{12... | collective-permute-start | bytes 294920 | tf_op jit(solution)/shard_map/ppermute | solution.py:687
  391.2 15.2 %collective-permute-start.87 = (bf16[2,96,256]{2,1,0:T(8,128)(2,1)S(1)}, bf16[2,96,256]{2,1,0:T(8,128)(2,1)S(1)}, u32[]{:S(2)}, u32[]{:S(2)}) collective-permute-start(bf16[2,96,256]{2,1,0:T(8,128)(2,1)S(1)} %get-tuple-element.129), channel_id=1, source_target_pairs={{0,4},{2,6},{4,0},{6,2},{1,5},{3,7},{5,1},{7,3},{8,12},{10,14},{12... | collective-permute-start | bytes 294920 | tf_op jit(solution)/shard_map/ppermute | solution.py:687
  392.0 15.2 %collective-permute-start.88 = (bf16[2,96,256]{2,1,0:T(8,128)(2,1)S(1)}, bf16[2,96,256]{2,1,0:T(8,128)(2,1)S(1)}, u32[]{:S(2)}, u32[]{:S(2)}) collective-permute-start(bf16[2,96,256]{2,1,0:T(8,128)(2,1)S(1)} %get-tuple-element.128), channel_id=1, source_target_pairs={{0,6},{2,0},{4,2},{6,4},{1,7},{3,1},{5,3},{7,5},{8,14},{10,8},{12,... | collective-permute-start | bytes 294920 | tf_op jit(solution)/shard_map/ppermute | solution.py:687
  404.7 21.2 %collective-permute-start.94 = (bf16[2,96,768]{2,1,0:T(8,128)(2,1)}, bf16[2,96,768]{2,1,0:T(8,128)(2,1)S(1)}, u32[]{:S(2)}, u32[]{:S(2)}) collective-permute-start(bf16[2,96,768]{2,1,0:T(8,128)(2,1)} %get-tuple-element.104), channel_id=1, source_target_pairs={{0,6},{2,0},{4,2},{6,4},{1,7},{3,1},{5,3},{7,5},{8,14},{10,8},{12,... | collective-permute-start | bytes 884744 | tf_op jit(solution)/shard_map/ppermute | solution.py:687
  406.4 21.2 %collective-permute-start.80 = (bf16[2,96,768]{2,1,0:T(8,128)(2,1)}, bf16[2,96,768]{2,1,0:T(8,128)(2,1)S(1)}, u32[]{:S(2)}, u32[]{:S(2)}) collective-permute-start(bf16[2,96,768]{2,1,0:T(8,128)(2,1)} %get-tuple-element.105), channel_id=1, source_target_pairs={{0,2},{2,4},{4,6},{6,0},{1,3},{3,5},{5,7},{7,1},{8,10},{10,12},{12... | collective-permute-start | bytes 884744 | tf_op jit(solution)/shard_map/ppermute | solution.py:687
  407.2 26.6 %collective-permute-start.81 = (bf16[2,96,768]{2,1,0:T(8,128)(2,1)}, bf16[2,96,768]{2,1,0:T(8,128)(2,1)S(1)}, u32[]{:S(2)}, u32[]{:S(2)}) collective-permute-start(bf16[2,96,768]{2,1,0:T(8,128)(2,1)} %get-tuple-element.106), channel_id=1, source_target_pairs={{0,4},{2,6},{4,0},{6,2},{1,5},{3,7},{5,1},{7,3},{8,12},{10,14},{12... | collective-permute-start | bytes 884744 | tf_op jit(solution)/shard_map/ppermute | solution.py:687
  409.8 43.1 %collective-permute-start.82 = (bf16[2,96,768]{2,1,0:T(8,128)(2,1)}, bf16[2,96,768]{2,1,0:T(8,128)(2,1)S(1)}, u32[]{:S(2)}, u32[]{:S(2)}) collective-permute-start(bf16[2,96,768]{2,1,0:T(8,128)(2,1)} %get-tuple-element.107), channel_id=1, source_target_pairs={{0,6},{2,0},{4,2},{6,4},{1,7},{3,1},{5,3},{7,5},{8,14},{10,8},{12,... | collective-permute-start | bytes 884744 | tf_op jit(solution)/shard_map/ppermute | solution.py:687
  411.9 62.5 %collective-permute-start.56 = (f32[4,2,64,1536]{3,2,0,1:T(8,128)}, f32[4,2,64,1536]{3,2,0,1:T(8,128)}, u32[]{:S(2)}, u32[]{:S(2)}) collective-permute-start(f32[4,2,64,1536]{3,2,0,1:T(8,128)} %bitcast.271), channel_id=1, source_target_pairs={{0,8},{8,0},{1,9},{9,1},{2,10},{10,2},{3,11},{11,3},{4,12},{12,4},... | collective-permute-start | bytes 9437192 | tf_op jit(solution)/shard_map/ppermute | solution.py:682
  425.9 51.6 %collective-permute-start.46 = (f32[4,2,64,1536]{3,2,0,1:T(8,128)}, f32[4,2,64,1536]{3,2,0,1:T(8,128)}, u32[]{:S(2)}, u32[]{:S(2)}) collective-permute-start(f32[4,2,64,1536]{3,2,0,1:T(8,128)} %bitcast.272), channel_id=1, source_target_pairs={{0,8},{8,0},{1,9},{9,1},{2,10},{10,2},{3,11},{11,3},{4,12},{12,4},... | collective-permute-start | bytes 9437192 | tf_op jit(solution)/shard_map/ppermute | solution.py:682
  427.6 28.3 %collective-permute-start.75 = (bf16[2,96,768]{2,1,0:T(8,128)(2,1)S(1)}, bf16[2,96,768]{2,1,0:T(8,128)(2,1)S(1)}, u32[]{:S(2)}, u32[]{:S(2)}) collective-permute-start(bf16[2,96,768]{2,1,0:T(8,128)(2,1)S(1)} %get-tuple-element.108), channel_id=1, source_target_pairs={{0,2},{2,4},{4,6},{6,0},{1,3},{3,5},{5,7},{7,1},{8,10},{10,12},{12... | collective-permute-start | bytes 884744 | tf_op jit(solution)/shard_map/ppermute | solution.py:687
  433.8 22.5 %collective-permute-start.76 = (bf16[2,96,768]{2,1,0:T(8,128)(2,1)S(1)}, bf16[2,96,768]{2,1,0:T(8,128)(2,1)S(1)}, u32[]{:S(2)}, u32[]{:S(2)}) collective-permute-start(bf16[2,96,768]{2,1,0:T(8,128)(2,1)S(1)} %get-tuple-element.109), channel_id=1, source_target_pairs={{0,4},{2,6},{4,0},{6,2},{1,5},{3,7},{5,1},{7,3},{8,12},{10,14},{12... | collective-permute-start | bytes 884744 | tf_op jit(solution)/shard_map/ppermute | solution.py:687
  456.3 13.2 %collective-permute-start.95 = (f32[96,768]{1,0:T(8,128)}, f32[96,768]{1,0:T(8,128)}, u32[]{:S(2)}, u32[]{:S(2)}) collective-permute-start(f32[96,768]{1,0:T(8,128)} %dynamic-slice_bitcast_fusion.1), channel_id=1, source_target_pairs={{0,8},{8,0},{1,9},{9,1},{2,10},{10,2},{3,11},{11,3},{4,12},{12,4},... | collective-permute-start | bytes 884744 | tf_op jit(solution)/shard_map/ppermute | solution.py:682
  477.2 20.4 %collective-permute-start.57 = (bf16[4,64,1536]{2,1,0:T(8,128)(2,1)S(1)}, bf16[4,64,1536]{2,1,0:T(8,128)(2,1)S(1)}, u32[]{:S(2)}, u32[]{:S(2)}) collective-permute-start(bf16[4,64,1536]{2,1,0:T(8,128)(2,1)S(1)} %fusion.22), channel_id=1, source_target_pairs={{0,1},{1,0},{2,3},{3,2},{4,5},{5,4},{6,7},{7,6},{8,9},{9,8},{10,11... | collective-permute-start | bytes 2359304 | tf_op jit(solution)/shard_map/ppermute | solution.py:682
  482.7 31.5 %collective-permute-start.47 = (bf16[4,64,1536]{2,1,0:T(8,128)(2,1)}, bf16[4,64,1536]{2,1,0:T(8,128)(2,1)}, u32[]{:S(2)}, u32[]{:S(2)}) collective-permute-start(bf16[4,64,1536]{2,1,0:T(8,128)(2,1)} %fusion.21), channel_id=1, source_target_pairs={{0,1},{1,0},{2,3},{3,2},{4,5},{5,4},{6,7},{7,6},{8,9},{9,8},{10,11... | collective-permute-start | bytes 2359304 | tf_op jit(solution)/shard_map/ppermute | solution.py:682
  498.7 17.4 %collective-permute-start.69 = (f32[38,256]{1,0:T(8,128)S(1)}, f32[38,256]{1,0:T(8,128)S(1)}, u32[]{:S(2)}, u32[]{:S(2)}) collective-permute-start(f32[38,256]{1,0:T(8,128)S(1)} %constant_dynamic-update-slice_fusion), channel_id=1, source_target_pairs={{0,16},{16,0},{1,17},{17,1},{2,18},{18,2},{3,19},{19,3},{4,20},{20... | collective-permute-start | bytes 116744 | tf_op jit(solution)/shard_map/ppermute | solution.py:682
  520.2 13.6 %collective-permute-start.61 = (bf16[64,1536]{1,0:T(8,128)(2,1)S(1)}, bf16[64,1536]{1,0:T(8,128)(2,1)S(1)}, u32[]{:S(2)}, u32[]{:S(2)}) collective-permute-start(bf16[64,1536]{1,0:T(8,128)(2,1)S(1)} %get-tuple-element.133), channel_id=1, source_target_pairs={{0,0},{8,2},{4,4},{12,6},{2,8},{10,10},{6,12},{14,14},{1,1},{9,3},... | collective-permute-start | bytes 589832 | tf_op jit(solution)/shard_map/ppermute | solution.py:744
  522.2 16.5 %collective-permute-start.63 = (bf16[64,1536]{1,0:T(8,128)(2,1)S(1)}, bf16[64,1536]{1,0:T(8,128)(2,1)S(1)}, u32[]{:S(2)}, u32[]{:S(2)}) collective-permute-start(bf16[64,1536]{1,0:T(8,128)(2,1)S(1)} %get-tuple-element.131), channel_id=1, source_target_pairs={{4,0},{12,2},{0,4},{8,6},{6,8},{14,10},{2,12},{10,14},{5,1},{13,3}... | collective-permute-start | bytes 589832 | tf_op jit(solution)/shard_map/ppermute | solution.py:744
  525.5 27.0 %collective-permute-start.64 = (bf16[64,1536]{1,0:T(8,128)(2,1)S(1)}, bf16[64,1536]{1,0:T(8,128)(2,1)S(1)}, u32[]{:S(2)}, u32[]{:S(2)}) collective-permute-start(bf16[64,1536]{1,0:T(8,128)(2,1)S(1)} %get-tuple-element.130), channel_id=1, source_target_pairs={{12,0},{4,2},{8,4},{0,6},{14,8},{6,10},{10,12},{2,14},{13,1},{5,3}... | collective-permute-start | bytes 589832 | tf_op jit(solution)/shard_map/ppermute | solution.py:744
  531.8 21.0 %collective-permute-start.48 = (bf16[64,1536]{1,0:T(8,128)(2,1)S(1)}, bf16[64,1536]{1,0:T(8,128)(2,1)S(1)}, u32[]{:S(2)}, u32[]{:S(2)}) collective-permute-start(bf16[64,1536]{1,0:T(8,128)(2,1)S(1)} %get-tuple-element.139), channel_id=1, source_target_pairs={{0,0},{8,2},{4,4},{12,6},{2,8},{10,10},{6,12},{14,14},{1,1},{9,3},... | collective-permute-start | bytes 589832 | tf_op jit(solution)/shard_map/ppermute | solution.py:744
  533.9 20.7 %collective-permute-start.49 = (bf16[64,1536]{1,0:T(8,128)(2,1)S(1)}, bf16[64,1536]{1,0:T(8,128)(2,1)S(1)}, u32[]{:S(2)}, u32[]{:S(2)}) collective-permute-start(bf16[64,1536]{1,0:T(8,128)(2,1)S(1)} %get-tuple-element.138), channel_id=1, source_target_pairs={{8,0},{0,2},{12,4},{4,6},{10,8},{2,10},{14,12},{6,14},{9,1},{1,3},... | collective-permute-start | bytes 589832 | tf_op jit(solution)/shard_map/ppermute | solution.py:744
  534.0 21.8 %collective-permute-start.50 = (bf16[64,1536]{1,0:T(8,128)(2,1)}, bf16[64,1536]{1,0:T(8,128)(2,1)S(1)}, u32[]{:S(2)}, u32[]{:S(2)}) collective-permute-start(bf16[64,1536]{1,0:T(8,128)(2,1)} %get-tuple-element.137), channel_id=1, source_target_pairs={{4,0},{12,2},{0,4},{8,6},{6,8},{14,10},{2,12},{10,14},{5,1},{13,3}... | collective-permute-start | bytes 589832 | tf_op jit(solution)/shard_map/ppermute | solution.py:744
  538.7 21.7 %collective-permute-start.51 = (bf16[64,1536]{1,0:T(8,128)(2,1)S(1)}, bf16[64,1536]{1,0:T(8,128)(2,1)S(1)}, u32[]{:S(2)}, u32[]{:S(2)}) collective-permute-start(bf16[64,1536]{1,0:T(8,128)(2,1)S(1)} %get-tuple-element.136), channel_id=1, source_target_pairs={{12,0},{4,2},{8,4},{0,6},{14,8},{6,10},{10,12},{2,14},{13,1},{5,3}... | collective-permute-start | bytes 589832 | tf_op jit(solution)/shard_map/ppermute | solution.py:744
  554.5 14.2 %collective-permute-start.67 = (bf16[64,1536]{1,0:T(8,128)(2,1)S(1)}, bf16[64,1536]{1,0:T(8,128)(2,1)S(1)}, u32[]{:S(2)}, u32[]{:S(2)}) collective-permute-start(bf16[64,1536]{1,0:T(8,128)(2,1)S(1)} %collective-permute-done.63.refs_2_), channel_id=1, source_target_pairs={{0,1},{1,0},{2,3},{3,2},{4,5},{5,4},{6,7},{7,6},{8,9},{9,8},{10,11... | collective-permute-start | bytes 589832 | tf_op jit(solution)/shard_map/ppermute | solution.py:682
  555.8 17.5 %collective-permute-start.68 = (bf16[64,1536]{1,0:T(8,128)(2,1)S(1)}, bf16[64,1536]{1,0:T(8,128)(2,1)S(1)}, u32[]{:S(2)}, u32[]{:S(2)}) collective-permute-start(bf16[64,1536]{1,0:T(8,128)(2,1)S(1)} %collective-permute-done.64.refs_3_), channel_id=1, source_target_pairs={{0,1},{1,0},{2,3},{3,2},{4,5},{5,4},{6,7},{7,6},{8,9},{9,8},{10,11... | collective-permute-start | bytes 589832 | tf_op jit(solution)/shard_map/ppermute | solution.py:682
  560.5 16.7 %collective-permute-start.52 = (bf16[64,1536]{1,0:T(8,128)(2,1)S(1)}, bf16[64,1536]{1,0:T(8,128)(2,1)S(1)}, u32[]{:S(2)}, u32[]{:S(2)}) collective-permute-start(bf16[64,1536]{1,0:T(8,128)(2,1)S(1)} %collective-permute-done.48.refs_0_), channel_id=1, source_target_pairs={{0,1},{1,0},{2,3},{3,2},{4,5},{5,4},{6,7},{7,6},{8,9},{9,8},{10,11... | collective-permute-start | bytes 589832 | tf_op jit(solution)/shard_map/ppermute | solution.py:682
  560.8 20.6 %collective-permute-start.53 = (bf16[64,1536]{1,0:T(8,128)(2,1)S(1)}, bf16[64,1536]{1,0:T(8,128)(2,1)S(1)}, u32[]{:S(2)}, u32[]{:S(2)}) collective-permute-start(bf16[64,1536]{1,0:T(8,128)(2,1)S(1)} %collective-permute-done.49.refs_1_), channel_id=1, source_target_pairs={{0,1},{1,0},{2,3},{3,2},{4,5},{5,4},{6,7},{7,6},{8,9},{9,8},{10,11... | collective-permute-start | bytes 589832 | tf_op jit(solution)/shard_map/ppermute | solution.py:682
  564.5 21.1 %collective-permute-start.54 = (bf16[64,1536]{1,0:T(8,128)(2,1)S(1)}, bf16[64,1536]{1,0:T(8,128)(2,1)S(1)}, u32[]{:S(2)}, u32[]{:S(2)}) collective-permute-start(bf16[64,1536]{1,0:T(8,128)(2,1)S(1)} %collective-permute-done.50.refs_2_), channel_id=1, source_target_pairs={{0,1},{1,0},{2,3},{3,2},{4,5},{5,4},{6,7},{7,6},{8,9},{9,8},{10,11... | collective-permute-start | bytes 589832 | tf_op jit(solution)/shard_map/ppermute | solution.py:682
  568.7 20.0 %collective-permute-start.55 = (bf16[64,1536]{1,0:T(8,128)(2,1)S(1)}, bf16[64,1536]{1,0:T(8,128)(2,1)S(1)}, u32[]{:S(2)}, u32[]{:S(2)}) collective-permute-start(bf16[64,1536]{1,0:T(8,128)(2,1)S(1)} %collective-permute-done.51.refs_3_), channel_id=1, source_target_pairs={{0,1},{1,0},{2,3},{3,2},{4,5},{5,4},{6,7},{7,6},{8,9},{9,8},{10,11... | collective-permute-start | bytes 589832 | tf_op jit(solution)/shard_map/ppermute | solution.py:682
  (134 other events, 2081.9 us)

commit v2 on v1

--- a/solution.py
+++ b/solution.py
@@ -1,3 +1,5 @@
+import functools
+
 import jax
 import jax.numpy as jnp
 from jax import lax
@@ -330,7 +332,7 @@
 
 BF = jnp.bfloat16
 F32 = jnp.float32
-CHUNK = 256
+CHUNK = 128
 VMEM = 40 * 1024 * 1024
 
 
@@ -347,14 +349,23 @@
     return lax.dot_general(a, b, (((1,), (1,)), ((), ())), preferred_element_type=F32)
 
 
-def mm3(a, b):
-    wide = mm(a[0], jnp.concatenate([b[0], b[1]], axis=1))
-    n = b[0].shape[1]
-    return wide[:, :n] + wide[:, n:] + mm(a[1], b[0])
-
-
-def mm3_nt(a, b):
-    return mm_nt(a[0], b[0]) + mm_nt(a[0], b[1]) + mm_nt(a[1], b[0])
+def beside(pair):
+    return jnp.concatenate(pair, axis=1)
+
+
+def right_side(b):
+    top, rest = b
+    return jnp.concatenate([beside((top, rest)), beside((top, jnp.zeros_like(top)))], axis=0)
+
+
+def right_side_nt(b):
+    top, rest = b
+    return jnp.concatenate([beside((top, top)), beside((rest, jnp.zeros_like(top)))], axis=0)
+
+
+def folded(wide):
+    n = wide.shape[1] // 2
+    return wide[:, :n] + wide[:, n:]
 
 
 def softplus(x):
@@ -368,13 +379,15 @@
     return total
 
 
+def square(which):
+    return lax.broadcasted_iota(jnp.int32, (CHUNK, CHUNK), which)
+
+
 def step_terms(step_ref, bias_ref, log_decay_ref):
     shifted_pre = step_ref[...] + bias_ref[...]
     step = softplus(shifted_pre)
     rates = jnp.exp(log_decay_ref[...])
-    rows = lax.broadcasted_iota(jnp.int32, (CHUNK, CHUNK), 0)
-    cols = lax.broadcasted_iota(jnp.int32, (CHUNK, CHUNK), 1)
-    lower = jnp.where(rows >= cols, 1.0, 0.0).astype(F32)
+    lower = jnp.where(square(0) >= square(1), 1.0, 0.0).astype(F32)
     cum = jnp.dot(lower, -step * rates, precision=HIGH, preferred_element_type=F32)
     return shifted_pre, step, rates, cum
 
@@ -385,7 +398,8 @@
 
 
 def forward_kernel(
-    vpre, spre, spre_step, vtaps, staps, bias, log_decay, skip, mixer, starts, state, vtail, stail
+    vpre, spre, spre_step, vtaps, staps, bias, log_decay, skip,
+    mixer, starts, vtotal, stotal, state, vtail, stail,
 ):
     @pl.when(pl.program_id(0) == 0)
     def _():
@@ -393,38 +407,39 @@
         vtail[...] = jnp.zeros_like(vtail)
         stail[...] = jnp.zeros_like(stail)
 
-    vx, sx = vpre[...], spre[...]
-    values = jax.nn.silu(taps_applied(jnp.concatenate([vtail[...], vx], axis=0), vtaps[...]))
-    states = jax.nn.silu(taps_applied(jnp.concatenate([stail[...], sx], axis=0), staps[...]))
-    vtail[...] = vx[CHUNK - 8 :]
+    sx = spre[...]
+    total = taps_applied(jnp.concatenate([stail[...], sx], axis=0), staps[...])
+    stotal[...] = total
+    states = jax.nn.silu(total)
     stail[...] = sx[CHUNK - 8 :]
     b, c = states[:, :STATE], states[:, STATE:]
     shifted_pre, step, rates, cum = step_terms(spre_step, bias, log_decay)
     cum_t = cum.T
     final = cum[CHUNK - 1 :, :]
     grown, ending, whole = jnp.exp(cum), jnp.exp(final - cum), jnp.exp(final)
-    b2, c2, bt2 = halves(b), halves(c), halves(b.T)
-    scores = mm3_nt(c2, b2)
-    rows = lax.broadcasted_iota(jnp.int32, (CHUNK, CHUNK), 0)
-    cols = lax.broadcasted_iota(jnp.int32, (CHUNK, CHUNK), 1)
-    barred = jnp.where(rows >= cols, 0.0, -1e30).astype(F32)
+    c_left, bt_left = beside(halves(c)), beside(halves(b.T))
+    scores = folded(mm_nt(c_left, right_side_nt(halves(b))))
+    scores = jnp.where(square(0) >= square(1), scores, 0.0)
     left = lax.broadcasted_iota(jnp.int32, (1, 128), 1) < 64
     starts[0] = state[...]
-    for p in range(vx.shape[1] // 128):
+    for p in range(vpre.shape[1] // 128):
         lanes = slice(128 * p, 128 * p + 128)
-        v = values[:, lanes]
+        vx = vpre[:, lanes]
+        total = taps_applied(jnp.concatenate([vtail[:, lanes], vx], axis=0), vtaps[:, lanes])
+        vtotal[:, lanes] = total
+        vtail[:, lanes] = vx[CHUNK - 8 :]
+        v = jax.nn.silu(total)
         weighted = v * by_pair(step, p)
-        w2 = halves(weighted)
-        both = jnp.concatenate([w2[0], w2[1]], axis=1)
+        right = right_side(halves(weighted))
         parts = []
         for h in (2 * p, 2 * p + 1):
-            mix = halves(jnp.exp(cum[:, h : h + 1] - cum_t[h : h + 1, :] + barred) * scores)
-            wide = mm(mix[0], both)
-            parts.append(wide[:, :128] + wide[:, 128:] + mm(mix[1], w2[0]))
+            decay = jnp.exp(jnp.minimum(cum[:, h : h + 1] - cum_t[h : h + 1, :], 0.0))
+            parts.append(folded(mm(beside(halves(decay * scores)), right)))
         held = state[:, lanes]
-        carried = by_pair(grown, p) * mm3(c2, halves(held))
+        carried = by_pair(grown, p) * folded(mm(c_left, right_side(halves(held))))
         mixer[:, lanes] = jnp.where(left, parts[0], parts[1]) + carried + skip[:, lanes] * v
-        state[:, lanes] = held * by_pair(whole, p) + mm3(bt2, halves(weighted * by_pair(ending, p)))
+        entering_here = right_side(halves(weighted * by_pair(ending, p)))
+        state[:, lanes] = held * by_pair(whole, p) + folded(mm(bt_left, entering_here))
 
 
 def forward_scan(vpre, spre, step_pre, vtaps, staps, bias, log_decay, skip):
@@ -437,10 +452,14 @@
         grid=(chunks,),
         in_specs=[row(width), row(2 * STATE), row(128)]
         + [fixed(x) for x in (vtaps, staps, bias, log_decay, skip)],
-        out_specs=[row(width), pl.BlockSpec((1, STATE, width), lambda i: (i, 0, 0))],
+        out_specs=[
+            row(width), pl.BlockSpec((1, STATE, width), lambda i: (i, 0, 0)), row(width), row(2 * STATE)
+        ],
         out_shape=[
             jax.ShapeDtypeStruct((tokens, width), F32),
             jax.ShapeDtypeStruct((chunks, STATE, width), F32),
+            jax.ShapeDtypeStruct((tokens, width), F32),
+            jax.ShapeDtypeStruct((tokens, 2 * STATE), F32),
         ],
         scratch_shapes=[
             pltpu.VMEM((STATE, width), F32),
@@ -449,164 +468,131 @@
         ],
         compiler_params=pltpu.CompilerParams(vmem_limit_bytes=VMEM),
         cost_estimate=pl.CostEstimate(
-            flops=chunks * 12 * 4 * CHUNK * CHUNK * 256,
-            bytes_accessed=tokens * width * 8,
-            transcendentals=chunks * 12 * CHUNK * CHUNK,
+            flops=tokens * width * 16 * 256,
+            bytes_accessed=tokens * width * 20,
+            transcendentals=tokens * width * 3,
         ),
         name="scan_forward",
     )(vpre, spre, step_pre, vtaps, staps, bias, log_decay, skip)
 
 
-def silu_slope(total):
-    s = jax.nn.sigmoid(total)
-    return s * (1.0 + total * (1.0 - s))
-
-
-def taps_back(d_total, later, taps):
+def taps_back(d_total, later, x, taps):
     extended = jnp.concatenate([d_total, later], axis=0)
-    result = 0.0
+    d_x, rows = 0.0, []
     for k in range(CONV):
-        result = result + extended[3 - k : 3 - k + CHUNK] * taps[k : k + 1, :]
-    return result
-
-
-def taps_grads(d_total, extended):
-    rows = [
-        jnp.sum(d_total * extended[5 + k : 5 + k + CHUNK], axis=0, keepdims=True)
-        for k in range(CONV)
-    ]
-    return rows + [jnp.sum(d_total, axis=0, keepdims=True)]
+        moved = extended[3 - k : 3 - k + CHUNK]
+        d_x = d_x + moved * taps[k : k + 1, :]
+        rows.append(jnp.sum(moved * x, axis=0, keepdims=True))
+    return d_x, rows + [jnp.sum(d_total, axis=0, keepdims=True)]
 
 
 def backward_kernel(
-    vpre, vbefore, spre, sbefore, spre_step, vtaps, staps, bias, log_decay, skip, chooser,
+    vpre, vtotal, spre, stotal, spre_step, vtaps, staps, bias, log_decay, skip, chooser,
     mixer, d_mixer, starts,
     values_low, d_spre, step_low, value_sums, state_sums, step_sums,
-    later_grad, later_state, vhead, shead, products, d_values,
+    later_grad, later_state, vhead, shead,
 ):
-    place = pl.program_id(0)
-
-    @pl.when(place == 0)
+    @pl.when(pl.program_id(0) == 0)
     def _():
         for ref in (later_grad, later_state, vhead, shead, value_sums, state_sums, step_sums):
             ref[...] = jnp.zeros_like(ref)
 
-    first = place == pl.num_programs(0) - 1
-    vx, sx = vpre[...], spre[...]
-    vext = jnp.concatenate([jnp.where(first, 0.0, vbefore[...]), vx], axis=0)
-    sext = jnp.concatenate([jnp.where(first, 0.0, sbefore[...]), sx], axis=0)
-    vtotal, stotal = taps_applied(vext, vtaps[...]), taps_applied(sext, staps[...])
-    values, states = jax.nn.silu(vtotal), jax.nn.silu(stotal)
+    stot = stotal[...]
+    s_sigmoid = jax.nn.sigmoid(stot)
+    states = stot * s_sigmoid
     b, c = states[:, :STATE], states[:, STATE:]
     shifted_pre, step, rates, cum = step_terms(spre_step, bias, log_decay)
     cum_t = cum.T
     final = cum[CHUNK - 1 :, :]
     grown, ending, whole = jnp.exp(cum), jnp.exp(final - cum), jnp.exp(final)
-    b2, c2, ct2 = halves(b), halves(c), halves(c.T)
-    scores_t = mm3_nt(b2, c2)
-    rows = lax.broadcasted_iota(jnp.int32, (CHUNK, CHUNK), 0)
-    cols = lax.broadcasted_iota(jnp.int32, (CHUNK, CHUNK), 1)
-    barred = jnp.where(cols >= rows, 0.0, -1e30).astype(F32)
+    b2, c2 = halves(b), halves(c)
+    b_left, ct_left = beside(b2), beside(halves(c.T))
+    causal = square(1) >= square(0)
+    scores_t = jnp.where(causal, folded(mm_nt(b_left, right_side_nt(c2))), 0.0)
     left = lax.broadcasted_iota(jnp.int32, (1, 128), 1) < 64
     zero = jnp.zeros((CHUNK, 128), BF)
     d_scores_t = jnp.zeros((CHUNK, CHUNK), F32)
     d_b = jnp.zeros((CHUNK, STATE), F32)
     d_c = jnp.zeros((CHUNK, STATE), F32)
-    skip_rows = []
-    final_rows = []
-    pairs = vx.shape[1] // 128
-    for p in range(pairs):
+    reached = jnp.zeros((CHUNK, 128), F32)
+    pulled = jnp.zeros((CHUNK, 128), F32)
+    at_end = jnp.zeros((8, 128), F32)
+    for p in range(vpre.shape[1] // 128):
         lanes = slice(128 * p, 128 * p + 128)
-        v, dy = values[:, lanes], d_mixer[:, lanes]
-        weighted = v * by_pair(step, p)
+        pick = chooser[256 * p : 256 * p + 256, :]
+        total, dy = vtotal[:, lanes], d_mixer[:, lanes]
+        sigmoid = jax.nn.sigmoid(total)
+        v = total * sigmoid
+        steps = by_pair(step, p)
+        weighted = v * steps
         w2, d2 = halves(weighted), halves(dy)
-        both = jnp.concatenate([d2[0], d2[1]], axis=1)
+        d_right = right_side(d2)
         w_rest = pltpu.roll(weighted - w2[0].astype(F32), 64, 1).astype(BF)
         d_top = pltpu.roll(d2[0].astype(F32), 64, 1).astype(BF)
         parts = []
         for h, mine in ((2 * p, left), (2 * p + 1, ~left)):
-            decay = jnp.exp(cum_t[h : h + 1, :] - cum[:, h : h + 1] + barred)
-            mix = halves(decay * scores_t)
-            wide = mm(mix[0], both)
-            parts.append(wide[:, :128] + wide[:, 128:] + mm(mix[1], d2[0]))
-            one = jnp.concatenate(
-                [jnp.where(mine, w2[0], w_rest), jnp.where(mine, w2[0], zero)], axis=1
-            )
-            other = jnp.concatenate(
-                [jnp.where(mine, d2[0], d_top), jnp.where(mine, d2[1], zero)], axis=1
-            )
+            decay = jnp.exp(jnp.minimum(cum_t[h : h + 1, :] - cum[:, h : h + 1], 0.0))
+            parts.append(folded(mm(beside(halves(decay * scores_t)), d_right)))
+            one = beside((jnp.where(mine, w2[0], w_rest), jnp.where(mine, w2[0], zero)))
+            other = beside((jnp.where(mine, d2[0], d_top), jnp.where(mine, d2[1], zero)))
             d_scores_t = d_scores_t + mm_nt(one, other) * decay
-        held, after = starts[0, :, lanes], later_grad[:, lanes]
-        after2 = halves(after)
+        held, after_here = starts[0, :, lanes], later_grad[:, lanes]
+        after2 = halves(after_here)
         ends = by_pair(ending, p)
-        d_weighted = jnp.where(left, parts[0], parts[1]) + ends * mm3(b2, after2)
+        d_weighted = jnp.where(left, parts[0], parts[1]) + ends * folded(
+            mm(b_left, right_side(after2))
+        )
         gain = skip[:, lanes]
-        products[:, lanes] = dy * (mixer[:, lanes] - gain * v)
-        products[:, 128 * (pairs + p) : 128 * (pairs + p) + 128] = v * d_weighted
-        d_values[:, lanes] = by_pair(step, p) * d_weighted + gain * dy
-        skip_rows.append(jnp.sum(v * dy, axis=0, keepdims=True))
-        final_rows.append(jnp.sum(after * later_state[:, lanes], axis=0, keepdims=True))
+        reached = reached + mm(beside(halves(dy * (mixer[:, lanes] - gain * v))), pick)
+        pulled = pulled + mm(beside(halves(v * d_weighted)), pick)
+        ended = jnp.sum(after_here * later_state[:, lanes], axis=0, keepdims=True)
+        at_end = at_end + mm(beside(halves(jnp.broadcast_to(ended, (8, 128)))), pick)
         faded = halves(by_pair(grown, p) * dy)
-        d_c = d_c + mm3_nt(faded, halves(held))
-        d_b = d_b + mm3_nt(halves(weighted * ends), after2)
-        later_grad[:, lanes] = after * by_pair(whole, p) + mm3(ct2, faded)
+        d_c = d_c + folded(mm_nt(beside(faded), right_side_nt(halves(held))))
+        d_b = d_b + folded(mm_nt(beside(halves(weighted * ends)), right_side_nt(after2)))
+        later_grad[:, lanes] = after_here * by_pair(whole, p) + folded(
+            mm(ct_left, right_side(faded))
+        )
+        d_total = (steps * d_weighted + gain * dy) * (sigmoid * (1.0 + total * (1.0 - sigmoid)))
+        d_x, rows = taps_back(d_total, vhead[:, lanes], vpre[:, lanes], vtaps[:, lanes])
+        values_low[:, lanes] = d_x.astype(BF)
+        rows += [jnp.sum(v * dy, axis=0, keepdims=True), jnp.zeros((2, 128), F32)]
+        value_sums[:, lanes] += jnp.concatenate(rows, axis=0)
+        vhead[:, lanes] = d_total[:8]
     later_state[...] = starts[0]
-    d2 = halves(d_scores_t)
-    dt2 = halves(d_scores_t.T)
-    d_b = d_b + mm3(d2, c2)
-    d_c = d_c + mm3(dt2, b2)
-    width = 128 * pairs
-    pick = chooser[...]
-
-    def by_head(x):
-        top, rest = halves(x)
-        return mm(top, pick) + mm(rest, pick)
-
-    reached = by_head(products[:, :width])
-    pulled = by_head(products[:, width:])
-    at_end = by_head(jnp.broadcast_to(jnp.concatenate(final_rows, axis=1), (8, width)))[:1]
-    rows128 = lax.broadcasted_iota(jnp.int32, (CHUNK, 128), 0)
-    d_cum = reached - step * pulled + jnp.where(rows128 == CHUNK - 1, at_end, 0.0)
-    upper = jnp.where(cols >= rows, 1.0, 0.0).astype(F32)
+    d_scores_t = jnp.where(causal, d_scores_t, 0.0)
+    d_b = d_b + folded(mm(beside(halves(d_scores_t)), right_side(c2)))
+    d_c = d_c + folded(mm(beside(halves(d_scores_t.T)), right_side(b2)))
+    last = lax.broadcasted_iota(jnp.int32, (CHUNK, 128), 0) == CHUNK - 1
+    d_cum = reached - step * pulled + jnp.where(last, at_end[:1], 0.0)
+    upper = jnp.where(causal, 1.0, 0.0).astype(F32)
     d_rate = jnp.dot(upper, d_cum, precision=HIGH, preferred_element_type=F32)
-    d_step = pulled - rates * d_rate
-    d_shifted = d_step * jax.nn.sigmoid(shifted_pre)
+    d_shifted = (pulled - rates * d_rate) * jax.nn.sigmoid(shifted_pre)
     step_low[...] = d_shifted.astype(BF)
     step_sums[0:1, :] += jnp.sum(d_shifted, axis=0, keepdims=True)
     step_sums[1:2, :] -= jnp.sum(d_rate * step, axis=0, keepdims=True) * rates
-    d_vtotal = d_values[...] * silu_slope(vtotal)
-    values_low[...] = taps_back(d_vtotal, vhead[...], vtaps[...]).astype(BF)
-    value_sums[...] += jnp.concatenate(
-        taps_grads(d_vtotal, vext)
-        + [jnp.concatenate(skip_rows, axis=1), jnp.zeros((2, width), F32)],
-        axis=0,
-    )
-    vhead[...] = d_vtotal[:8]
-    d_stotal = jnp.concatenate([d_b, d_c], axis=1) * silu_slope(stotal)
-    d_spre[...] = taps_back(d_stotal, shead[...], staps[...])
-    state_sums[...] += jnp.concatenate(
-        taps_grads(d_stotal, sext) + [jnp.zeros((3, 2 * STATE), F32)], axis=0
-    )
-    shead[...] = d_stotal[:8]
+    d_total = beside((d_b, d_c)) * (s_sigmoid * (1.0 + stot * (1.0 - s_sigmoid)))
+    d_x, rows = taps_back(d_total, shead[...], spre[...], staps[...])
+    d_spre[...] = d_x
+    state_sums[...] += jnp.concatenate(rows + [jnp.zeros((3, 2 * STATE), F32)], axis=0)
+    shead[...] = d_total[:8]
 
 
 def backward_scan(
-    vpre, spre, step_pre, vtaps, staps, bias, log_decay, skip, mixer, d_mixer, starts
+    vpre, vtotal, spre, stotal, step_pre, vtaps, staps, bias, log_decay, skip, mixer, d_mixer, starts
 ):
     tokens, width = vpre.shape
     chunks = tokens // CHUNK
-    heads = jnp.arange(width)[:, None] // 64
-    chooser = (heads == jnp.arange(128)[None, :]).astype(BF)
+    lane = jnp.arange(2 * width)
+    heads = 2 * (lane // 256) + lane % 128 // 64
+    chooser = (heads[:, None] == jnp.arange(128)[None, :]).astype(BF)
     row = lambda n: pl.BlockSpec((CHUNK, n), lambda i: (chunks - 1 - i, 0))
-    before = lambda n: pl.BlockSpec(
-        (8, n), lambda i: (jnp.maximum((chunks - 1 - i) * (CHUNK // 8) - 1, 0), 0)
-    )
     fixed = lambda x: pl.BlockSpec(x.shape, lambda i: (0, 0))
     summed = lambda n: pl.BlockSpec((8, n), lambda i: (0, 0))
     return pl.pallas_call(
         backward_kernel,
         grid=(chunks,),
-        in_specs=[row(width), before(width), row(2 * STATE), before(2 * STATE), row(128)]
+        in_specs=[row(width), row(width), row(2 * STATE), row(2 * STATE), row(128)]
         + [fixed(x) for x in (vtaps, staps, bias, log_decay, skip, chooser)]
         + [row(width), row(width), pl.BlockSpec((1, STATE, width), lambda i: (chunks - 1 - i, 0, 0))],
         out_specs=[
@@ -625,17 +611,18 @@
             pltpu.VMEM((STATE, width), F32),
             pltpu.VMEM((8, width), F32),
             pltpu.VMEM((8, 2 * STATE), F32),
-            pltpu.VMEM((CHUNK, 2 * width), F32),
-            pltpu.VMEM((CHUNK, width), F32),
         ],
         compiler_params=pltpu.CompilerParams(vmem_limit_bytes=VMEM),
         cost_estimate=pl.CostEstimate(
-            flops=chunks * 12 * 8 * CHUNK * CHUNK * 256,
-            bytes_accessed=tokens * width * 16,
-            transcendentals=chunks * 12 * CHUNK * CHUNK,
+            flops=tokens * width * 40 * 256,
+            bytes_accessed=tokens * width * 24,
+            transcendentals=tokens * width * 3,
         ),
         name="scan_backward",
-    )(vpre, vpre, spre, spre, step_pre, vtaps, staps, bias, log_decay, skip, chooser, mixer, d_mixer, starts)
+    )(
+        vpre, vtotal, spre, stotal, step_pre, vtaps, staps, bias, log_decay, skip, chooser,
+        mixer, d_mixer, starts,
+    )
 
 
 def place(arrays, piece, targets, rows):
@@ -687,6 +674,10 @@
     return lax.ppermute(x, axis, [(i, (i + distance) % n) for i in range(n)])
 
 
+def after(x, *earlier):
+    return lax.optimization_barrier((x, *earlier))[0]
+
+
 def at(x, index, axis):
     return lax.dynamic_index_in_dim(x, index, axis, keepdims=False)
 
@@ -699,6 +690,52 @@
     first = jnp.where(flag == 0, mine, other)
     second = jnp.where(flag == 0, other, mine)
     return jnp.concatenate([first, second], axis=axis)
+
+
+def paired_kernel(count, core, *refs):
+    lows, weights, outs = refs[:count], refs[count : 3 * count], refs[3 * count :]
+    step, tiles = pl.program_id(0), pl.num_programs(0) // 2
+    for j in range(2):
+
+        @pl.when(step // tiles == j)
+        def _(j=j):
+            for out, which in zip(outs, (1 - core[0], core[0]), strict=True):
+                total = 0.0
+                for k, low in enumerate(lows):
+                    block = low[:, which]
+                    total = total + mm_nt(
+                        block.reshape(-1, block.shape[-1]), weights[2 * k + j][...]
+                    )
+                out[...] = total
+
+
+def paired_products(lows, weights, core, sub):
+    tokens, n = lows[0].shape[0], weights[0][0].shape[0]
+    groups = tokens // (4 * sub)
+    split = [x.reshape(groups, 2, 2 * sub, x.shape[1]) for x in lows]
+    tile = 256
+    tiles = n // tile
+    out = jax.ShapeDtypeStruct((tokens // 2, 2 * n), F32)
+    first = lambda i, core: (jnp.minimum(i, tiles - 1), 0)
+    second = lambda i, core: (jnp.maximum(i - tiles, 0), 0)
+    return pl.pallas_call(
+        functools.partial(paired_kernel, len(lows)),
+        grid_spec=pltpu.PrefetchScalarGridSpec(
+            num_scalar_prefetch=1,
+            grid=(2 * tiles,),
+            in_specs=[pl.BlockSpec(x.shape, lambda i, core: (0, 0, 0, 0)) for x in split]
+            + [
+                pl.BlockSpec((tile, w.shape[1]), where)
+                for pair in weights
+                for w, where in zip(pair, (first, second), strict=True)
+            ],
+            out_specs=[pl.BlockSpec((tokens // 2, tile), lambda i, core: (0, i))] * 2,
+        ),
+        out_shape=[out, out],
+        compiler_params=pltpu.CompilerParams(vmem_limit_bytes=VMEM),
+        cost_estimate=pl.CostEstimate(flops=1, bytes_accessed=1, transcendentals=0),
+        name="paired_products",
+    )(core[None], *split, *[w for pair in weights for w in pair])
 
 
 def whole_sequences(
@@ -709,109 +746,111 @@
     nz = lax.axis_size("seq")
     nx = lax.axis_size("x")
     d_model = block_input.shape[-1]
+    half = d_model // 2
     group = block_input.shape[2]
-    sub = group // 4
+    sub = group // 2
     tokens = group * nz
-    own = sub * nz
+    own = sub * nz // 2
     rows = gate_weight.shape[0]
     cols = gate_weight.shape[1] // 2
     heads = step_weight.shape[1] // 2
-    slot = 2 * (zi // 2) + ci
-
-    def tokens_in(x):
+
+    def turned_halves(x):
+        return jnp.where(xi == 0, x, jnp.concatenate([x[:, half:], x[:, :half]], axis=1))
+
+    def route(r):
+        return [
+            (c * nz + z, (z % 2) * nz + 2 * ((z // 2) ^ r) + c) for c in range(2) for z in range(nz)
+        ]
+
+    def tokens_in(x, *earlier):
         rounds = []
-        for r in range(nz):
-            j = zi ^ r
-            start = yi * (2 * sub) + (j % 2) * sub
-            piece = lax.dynamic_slice(x, (j // 2, 0, start, 0), (1, 1, sub, d_model))
-            route = [
-                (c * nz + z, ((z ^ r) % 2) * nz + 2 * ((z ^ r) // 2) + c)
-                for c in range(2)
-                for z in range(nz)
-            ]
-            rounds.append(lax.ppermute(piece.reshape(sub, d_model), ("core", "seq"), route))
-        return place(rounds, sub, [(slot ^ r) * sub for r in range(nz)], own)
+        for r in range(2):
+            piece = lax.dynamic_slice(x, ((zi // 2) ^ r, 0, yi * sub, 0), (1, 1, sub, d_model))
+            rounds.append(lax.ppermute(piece.reshape(sub, d_model), ("core", "seq"), route(r)))
+        return ordered(zi // 2, after(rounds[0], *earlier), after(rounds[1], *earlier), 0)
 
     def tokens_back(x):
-        mine, other = [], []
-        for r in range(nz):
-            piece = part(x, slot ^ r, sub, 0)
-            route = [
-                (((z ^ r) % 2) * nz + 2 * ((z ^ r) // 2) + c, c * nz + z)
-                for c in range(2)
-                for z in range(nz)
-            ]
-            mine.append(lax.ppermute(piece, ("core", "seq"), route))
-            other.append(swap(mine[-1], "heads"))
-        targets = [
-            (((zi ^ r) // 2) * 4 + 2 * y + (zi ^ r) % 2) * sub
-            for y in (yi, 1 - yi)
-            for r in range(nz)
+        pieces = [part(x, (zi // 2) ^ r, sub, 0) for r in range(2)]
+        return [
+            lax.ppermute(piece, ("core", "seq"), [(b, a) for a, b in route(r)])
+            for r, piece in enumerate(pieces)
         ]
-        return place(mine + other, sub, targets, 2 * group).reshape(block_input.shape)
+
+    def tokens_home(mine):
+        targets = [(2 * ((zi // 2) ^ r) + y) * sub for y in (yi, 1 - yi) for r in range(2)]
+        blocks = mine + [swap(x, "heads") for x in mine]
+        return place(blocks, sub, targets, 2 * group).reshape(block_input.shape)
 
     def spread(x):
         by_y = swap(x, "heads")
         by_core = swap(x, "core")
         by_both = swap(by_y, "core")
         targets = [
-            (4 * k + 2 * y + c) * sub
+            ((2 * k + c) * 2 + y) * sub
             for y, c in ((yi, ci), (1 - yi, ci), (yi, 1 - ci), (1 - yi, 1 - ci))
-            for k in range(nz)
+            for k in range(nz // 2)
         ]
-        return place([x, by_y, by_core, by_both], sub, targets, tokens), by_core
-
-    def reduced(x, link=BF):
-        split = x.reshape(nz, 2, 2, sub, x.shape[-1])
-        summed = at(split, ci, 2) + swap(at(split, 1 - ci, 2), "core")
-        sent = swap(at(summed, 1 - yi, 1).astype(link), "heads").astype(F32)
-        return (at(summed, yi, 1) + sent).reshape(own, x.shape[-1])
-
-    def gathered(weight):
+        return place([x, by_y, by_core, by_both], sub, targets, tokens)
+
+    def of_core(x, core):
+        return at(x.reshape(nz // 2, 2, 2 * sub, -1), core, 1).reshape(tokens // 2, -1)
+
+    def over_core(send, keep, link=BF):
+        return core_sum(swap(send, "core"), keep, link)
+
+    def core_sum(received, keep, link=BF):
+        received = received.reshape(nz // 2, 2, sub, keep.shape[1])
+        keep = keep.reshape(received.shape)
+        goes = (at(keep, 1 - yi, 1) + at(received, 1 - yi, 1)).astype(link)
+        return at(keep, yi, 1) + at(received, yi, 1), goes
+
+    def over_y(stays, received):
+        return (stays + received.astype(F32)).reshape(own, -1)
+
+    def block_of(weight):
         width = weight.shape[1] // 2
         received = swap(part(weight, 1 - ci, width, 1), "core")
-        block = ordered(ci, part(weight, ci, width, 1), received, 0)
+        return ordered(ci, part(weight, ci, width, 1), received, 0)
+
+    def ring(block, *earlier):
         right = turned(block, "seq", 1)
         left = turned(block, "seq", -1)
-        across = swap(block, "x")
-        far = turned(right, "seq", 1)
-        blocks = [block, right, left, far, across]
-        blocks += [swap(right, "x"), swap(left, "x"), swap(far, "x")]
+        return [block, right, left, turned(after(right, left, *earlier), "seq", 1)]
+
+    def stacked(blocks):
         targets = [
-            ((x * 2 + c) * nz + z % nz) * rows
-            for x in (xi, 1 - xi)
-            for z in (zi, zi + nz - 1, zi + 1, zi + 2)
-            for c in range(2)
+            (c * nz + z % nz) * rows for z in (zi, zi + nz - 1, zi + 1, zi + 2) for c in range(2)
         ]
-        return place(blocks, rows, targets, d_model)
-
-    def scattered(grad):
-        half = d_model // 2
-        summed = part(grad, xi, half, 0) + swap(
-            part(grad, 1 - xi, half, 0).astype(BF), "x"
-        ).astype(F32)
-        summed = summed.reshape(2, nz, rows, grad.shape[1])
-        total = at(summed, zi, 1)
-        for d in range(1, nz):
-            sent = at(summed, (zi + d) % nz, 1).astype(BF)
-            total = total + turned(sent, "seq", d).astype(F32)
-        return total
+        return place(blocks, rows, targets, half)
+
+    def products(low, features):
+        return transposed(features[:, half:], low).astype(BF), transposed(features[:, :half], low)
+
+    def over_x(kept, received):
+        return (kept + received.astype(F32)).reshape(2, nz, rows, -1)
+
+    def far_pieces(summed):
+        return part(summed, 1 - zi // 2, 2, summed.ndim - 3).astype(BF)
+
+    def near_sum(summed, received):
+        return part(summed, zi // 2, 2, summed.ndim - 3) + received.astype(F32)
+
+    def near_pieces(summed):
+        return at(summed, 1 - zi % 2, -3).astype(BF)
+
+    def over_z(summed, received):
+        return at(summed, zi % 2, -3) + received.astype(F32)
 
     def to_core(total):
         received = swap(at(total, 1 - ci, 0), "core")
         return at(total, ci, 0), received
 
-    gain = ordered(ci, input_gain[None], swap(input_gain[None], "core"), 0)
-    near = [gain] + [turned(gain, "seq", d) for d in range(1, nz)]
-    by_z = jnp.stack(near)[(zi - jnp.arange(nz)) % nz]
-    gain = ordered(xi, by_z[None], swap(by_z[None], "x"), 0)
-    gain = jnp.transpose(gain, (0, 2, 1, 3)).reshape(1, d_model).astype(F32)
-
-    kept = tokens_in(block_input)
-    x_own = kept.astype(F32)
-    scaling = lax.rsqrt(jnp.mean(x_own * x_own, axis=-1, keepdims=True) + EPS)
-    normed_own = (x_own * scaling * gain).astype(BF)
-    normed, normed_core = spread(normed_own)
+    project = lambda a, b: jnp.dot(a, b, preferred_element_type=F32)
+    transposed = lambda a, b: lax.dot_general(
+        a, b, (((0,), (0,)), ((), ())), preferred_element_type=F32
+    )
+    back = lambda a, b: lax.dot_general(a, b, (((1,), (1,)), ((), ())), preferred_element_type=F32)
 
     pad = 128 - heads
     first = jnp.concatenate(
@@ -821,7 +860,7 @@
                     value_weight[:, cols * k : cols * k + cols],
                     state_weight[:, STATE * k : STATE * k + STATE],
                     step_weight[:, heads * k : heads * k + heads],
-                    jnp.zeros((rows, pad), BF),
+                    jnp.broadcast_to(input_gain[:, None], (rows, pad)),
                 ],
                 axis=1,
             )
@@ -829,29 +868,71 @@
         ],
         axis=1,
     )
-    first_full = gathered(first)
-    gate_full = gathered(gate_weight)
-    og_own = tokens_in(output_grad)
-    og, og_core = spread(og_own)
-    out_full = gathered(out_weight.T)
-
-    project = lambda a, b: jnp.dot(a, b, preferred_element_type=F32)
-    weights_in = (first_full[:, :cols], first_full[:, cols : cols + STATE], first_full[:, cols + STATE :])
-    values_pre = project(normed, weights_in[0])
-    states_half = project(normed, weights_in[1])
-    step_pre = project(normed, weights_in[2])
+    first_block = block_of(first)
+    first_across = [swap(first_block, "x")]
+    first_ring = ring(first_block, *first_across)
+    first_across += [swap(x, "x") for x in first_ring[1:]]
+
+    x_own = turned_halves(tokens_in(after(block_input, first_block)))
+
+    pair_weight = after(
+        jnp.concatenate(
+            [gate_weight[:, :cols], out_weight[:cols].T, gate_weight[:, cols:], out_weight[cols:].T],
+            axis=1,
+        ),
+        first_block,
+    )
+    pair_block = block_of(pair_weight)
+    pair_across = [swap(after(pair_block, first_across[0]), "x")]
+    x_all = spread(after(x_own, *pair_across))
+    pair_ring = ring(after(pair_block, first_ring[3], first_across[1], first_across[2]))
+    pair_across += [swap(after(x, first_across[3]), "x") for x in pair_ring[1:]]
+
+    first_own = stacked(first_ring)
+    first_other = stacked(first_across)
+    def both_halves(a, w_own, w_other):
+        return project(a[:, :half], w_own) + project(a[:, half:], w_other)
+
+    split = lambda w: (w[:, :cols], w[:, cols : cols + STATE], w[:, cols + STATE :])
+    value_own, state_own, step_own = split(first_own)
+    value_other, state_other, step_other = split(first_other)
+    gain = jnp.concatenate([step_own[:, -1], step_other[:, -1]])[None].astype(F32)
+    blank = jnp.arange(128)[None, :] < heads
+    step_own, step_other = jnp.where(blank, step_own, 0), jnp.where(blank, step_other, 0)
+
+    x_wide = x_all.astype(F32)
+    normed = (
+        x_wide * lax.rsqrt(jnp.mean(x_wide * x_wide, axis=-1, keepdims=True) + EPS) * gain
+    ).astype(BF)
+    x_own = x_own.astype(F32)
+    scaling = lax.rsqrt(jnp.mean(x_own * x_own, axis=-1, keepdims=True) + EPS)
+
+    states_weights = jnp.concatenate([state_own, state_other], axis=0)
+    states_received = swap(states_weights, "core")
+    states_half = both_halves(normed, state_own, state_other)
     states_pre = ordered(ci, states_half, swap(states_half, "core"), 1)
+    values_pre = both_halves(normed, value_own, value_other)
+    step_pre = both_halves(normed, step_own, step_other)
 
     vtaps = part(value_taps, ci, cols, 1)
     lanes = lambda v: jnp.pad(part(v, ci, heads, 0), (0, pad))[None]
     bias, decays = lanes(step_bias), lanes(log_decay)
     skip = jnp.repeat(part(skip_gain, ci, heads, 0), cols // heads)[None]
     gain_mixer = part(mixer_gain, ci, cols, 0)[None]
-    mixer, starts = forward_scan(
+    values_pre, states_received, *pair_across[1:3], pair_ring[3] = lax.optimization_barrier(
+        (values_pre, states_received, *pair_across[1:3], pair_ring[3])
+    )
+    mixer, starts, values_total, states_total = forward_scan(
         values_pre, states_pre, step_pre, vtaps, state_taps, bias, decays, skip
     )
-    gate_lin = project(normed, gate_full)
-    d_out = project(og, out_full)
+    og_own = turned_halves(tokens_in(after(output_grad, pair_ring[1], pair_ring[2]), mixer))
+    og = spread(og_own)
+    pair_own = stacked(pair_ring)
+    pair_other = stacked(pair_across)
+    gate_own, out_own = pair_own[:, :cols], pair_own[:, cols:]
+    gate_other, out_other = pair_other[:, :cols], pair_other[:, cols:]
+    gate_lin = both_halves(normed, gate_own, gate_other)
+    d_out = both_halves(og, out_own, out_other)
     sigmoid_gate = jax.nn.sigmoid(gate_lin)
     silu_gate = gate_lin * sigmoid_gate
     gated = mixer * silu_gate
@@ -866,77 +947,130 @@
     gate_low = (d_gated * mixer * sigmoid_gate * (1.0 + gate_lin * (1.0 - sigmoid_gate))).astype(BF)
     g_mixer_gain = jnp.sum(d_out * gated * inverse, axis=0)
 
-    transposed = lambda a, b: lax.dot_general(
-        a, b, (((0,), (0,)), ((), ())), preferred_element_type=F32
-    )
-    back = lambda a, b: lax.dot_general(a, b, (((1,), (1,)), ((), ())), preferred_element_type=F32)
-    g_out = scattered(transposed(og, out_normed))
-    g_gate = scattered(transposed(normed, gate_low))
-    branch = reduced(back(out_normed, out_full))
-    block_output = tokens_back((x_own + branch).astype(BF))
-
-    values_low, d_states, step_low, value_sums, state_sums, step_sums = backward_scan(
-        values_pre, states_pre, step_pre, vtaps, state_taps, bias, decays, skip, mixer, d_mixer, starts
-    )
-    states_own = reduced(d_states, F32).astype(BF)
-    g_value = scattered(transposed(normed, values_low))
-    d_normed = reduced(
-        back(gate_low, gate_full) + back(values_low, weights_in[0]) + back(step_low, weights_in[2])
-    )
-    states_weights = ordered(ci, weights_in[1], swap(weights_in[1], "core"), 1)
-    d_normed = d_normed + back(states_own, states_weights)
-    states_both = jnp.concatenate([states_own, swap(states_own, "core")], axis=0)
-    normed_both = jnp.concatenate([normed_own, normed_core], axis=0)
-    g_small = scattered(
-        jnp.concatenate(
-            [
-                transposed(normed_both, part(states_both, ci, STATE, 1)),
-                transposed(normed, step_low),
-            ],
-            axis=1,
-        )
-    )
-
+    branch_sends, branch_keeps = paired_products([out_normed], [(out_own, out_other)], ci, sub)
+    then = after(out_normed, branch_sends)
+    out_sum = jnp.stack([transposed(og[:, :half], then), transposed(og[:, half:], then)])
+    out_sum = out_sum.reshape(2, 2, nz, rows, cols)
+    out_pieces = far_pieces(out_sum)
+    gate_sends, gate_keeps = products(after(gate_low, out_pieces), normed)
+    branch_stays, branch_goes = over_core(branch_sends, branch_keeps)
+    d_mixer = after(d_mixer, out_pieces, gate_sends, branch_goes)
+    scanned = backward_scan(
+        values_pre, values_total, states_pre, states_total, step_pre, vtaps, state_taps, bias, decays, skip,
+        mixer, d_mixer, starts,
+    )
+    sent = (swap(out_pieces, "seq", 2), swap(gate_sends, "x"), swap(branch_goes, "heads"))
+    sent, scanned = lax.optimization_barrier((sent, scanned))
+    out_received, gate_received, branch_received = sent
+    values_low, d_states, step_low, value_sums, state_sums, step_sums = scanned
+
+    value_sends, value_keeps = products(values_low, normed)
+    gate_sum = over_x(after(gate_keeps, value_sends), gate_received)
+    gate_pieces = far_pieces(gate_sum)
+    d_states = after(d_states, gate_pieces)
+    states_stay, states_go = over_core(of_core(d_states, 1 - ci), of_core(d_states, ci), F32)
+    dn_sends, dn_keeps = paired_products(
+        [after(gate_low, value_sends, states_go), values_low, step_low],
+        [(gate_own, gate_other), (value_own, value_other), (step_own, step_other)],
+        ci,
+        sub,
+    )
+    out_sum = near_sum(out_sum, after(out_received, dn_sends))
+    out_pieces = near_pieces(out_sum)
+    branch = over_y(branch_stays, after(branch_received, dn_sends))
+    output_rows = turned_halves((x_own + branch).astype(BF))
+    (
+        value_received, gate_received, states_received_y, dn_received, dn_keeps, out_pieces, output_rows
+    ) = lax.optimization_barrier(
+        (
+            swap(value_sends, "x"), swap(gate_pieces, "seq", 2), swap(states_go, "heads"),
+            swap(dn_sends, "core"), dn_keeps, out_pieces, output_rows,
+        )
+    )
+
+    dn_stays, dn_goes = core_sum(dn_received, dn_keeps)
+    output_sent = tokens_back(output_rows)
+    gate_sum = near_sum(gate_sum, gate_received)
+    gate_pieces = near_pieces(gate_sum)
+    states_low = over_y(states_stay, states_received_y).astype(BF)
+    states_weights = ordered(ci, states_weights, states_received, 1)
+    states_both = swap(states_low, "core").reshape(nz // 2, sub, -1), states_low.reshape(nz // 2, sub, -1)
+    states_both = [part(x, ci, STATE, 2) for x in states_both]
+    of_y = at(after(normed, dn_goes).reshape(nz // 2, 2, 2, sub, d_model), yi, 2)
+    states_both = jnp.stack(
+        [jnp.where(ci == k, states_both[1], states_both[0]) for k in range(2)], axis=1
+    ).reshape(tokens // 2, STATE)
+    parts = [
+        products(states_both, of_y.reshape(tokens // 2, d_model)),
+        products(after(step_low, dn_goes), normed),
+    ]
+    small_sends, small_keeps = (jnp.concatenate(p, axis=1) for p in zip(*parts, strict=True))
+    value_sum = over_x(value_keeps, value_received)
+    (
+        dn_received, output_sent, gate_received, small_received, out_pieces, value_sum
+    ) = lax.optimization_barrier(
+        (
+            swap(dn_goes, "heads"), output_sent, swap(gate_pieces, "seq", 1), swap(small_sends, "x"),
+            out_pieces, value_sum,
+        )
+    )
+
+    value_sum = jnp.concatenate([value_sum, over_x(small_keeps, small_received)], axis=-1)
+    value_pieces = far_pieces(value_sum)
+    d_normed = over_y(dn_stays, after(dn_received, value_pieces)) + back(states_low, states_weights)
     pushed = d_normed * gain
     d_tokens = scaling * pushed - x_own * (scaling * scaling * scaling) * jnp.mean(
         pushed * x_own, axis=-1, keepdims=True
     )
-    grad_input = tokens_back((og_own.astype(F32) + d_tokens).astype(BF))
-    g_input_gain = jnp.sum(d_normed * x_own * scaling, axis=0)
+    input_rows = turned_halves((og_own.astype(F32) + d_tokens).astype(BF))
+    block_output = tokens_home(output_sent)
+    g_gate = over_z(gate_sum, gate_received)
+    out_sum = over_z(out_sum, swap(out_pieces, "seq", 1))
+    out_sum, input_sent = lax.optimization_barrier((out_sum, tokens_back(input_rows)))
+
+    grad_input = tokens_home(input_sent)
+    g_out = out_sum[0] + swap(out_sum[1].astype(BF), "x").astype(F32)
+    value_sum = near_sum(value_sum, after(swap(value_pieces, "seq", 2), *input_sent))
+    g_value = over_z(value_sum, swap(near_pieces(value_sum), "seq", 1))
+    g_input_gain = turned_halves(jnp.sum(d_normed * x_own * scaling, axis=0)[None])
 
     per_core = jnp.concatenate(
         [value_sums[:6], g_mixer_gain[None], jnp.pad(step_sums[:2].reshape(1, -1), ((0, 0), (0, cols - 256)))],
         axis=0,
     ).reshape(-1, 256)
     shared = jnp.concatenate([state_sums, g_input_gain.reshape(-1, 256)], axis=0)
+    shared = after(shared, *input_sent)
+    shared = shared + swap(shared, "heads")
+    received = swap(jnp.concatenate([per_core, shared], axis=0), "core")
     n_core = per_core.shape[0]
-    pack = jnp.concatenate([per_core, shared], axis=0)
+    pack = jnp.concatenate(
+        [ordered(ci, per_core, received[:n_core], 0), shared + received[n_core:]], axis=0
+    )
     pack = pack + swap(pack, "x")
     pack = pack + swap(pack, "seq", 1)
     pack = pack + swap(pack, "seq", 2)
-    other = swap(pack, "core")
-    shared = pack[n_core:] + other[n_core:]
-    shared = shared + swap(shared, "heads")
-    both = ordered(ci, pack[:n_core].reshape(1, 8, cols), other[:n_core].reshape(1, 8, cols), 0)
+    both, shared = pack[: 2 * n_core].reshape(2, 8, cols), pack[2 * n_core :]
     by_channel = jnp.transpose(both, (1, 0, 2)).reshape(8, 2 * cols)
     per_head = both[:, 7, :256].reshape(2, 2, 128)[:, :, :heads]
     input_gain_all = shared[8:].reshape(nx, 2, nz, rows)
     my_gain = at(at(at(input_gain_all, xi, 0), ci, 0), zi, 0)
 
-    widths = lambda total: ordered(ci, *to_core(total), 1)
-    small_mine, small_other = to_core(g_small)
-    g_state = ordered(ci, small_mine[:, :STATE], small_other[:, :STATE], 1)
+    def widths(mine, received):
+        return ordered(ci, mine, received, 1)
+
+    value_mine, value_received = to_core(g_value)
+    states_at, steps_at = slice(cols, cols + STATE), slice(cols + STATE, cols + STATE + heads)
+    g_state = widths(value_mine[:, states_at], value_received[:, states_at])
     g_state = g_state + swap(g_state, "heads")
-    g_step = ordered(ci, small_mine[:, STATE : STATE + heads], small_other[:, STATE : STATE + heads], 1)
     return (
         block_output,
         grad_input,
         my_gain,
-        widths(g_gate),
-        widths(g_value),
+        widths(*to_core(g_gate)),
+        widths(value_mine[:, :cols], value_received[:, :cols]),
         g_state,
-        g_step,
-        widths(g_out).T,
+        widths(value_mine[:, steps_at], value_received[:, steps_at]),
+        widths(*to_core(g_out)).T,
         by_channel[:5],
         shared[:5],
         per_head[:, 0].reshape(-1),

time: 598 us -> 435 us (0.73)
  waiting for transfers between devices: 257 us -> 156 us
  local copies, waits for them, and re-layouts: 66.2 us -> 42.2 us
  starting transfers between devices: 103 us -> 83.3 us
  matrix products: 49.3 us -> 29.6 us
    ppermute x24 -> x6, waiting for transfers between devices: 74.4 us -> 26.7 us  [turned(): return lax.ppermute(x, axis, [(i, (i + distance) % n) for i in range(n)])]
    ppermute x56 -> x50, waiting for transfers between devices: 134 us -> 99.4 us  [swap(): lax.ppermute(x, axis, [(i, i ^ bit) for i in range(lax.axis_size(axis))])]
    ppermute x24 -> x6, starting transfers between devices: 37.5 us -> 15 us  [turned(): return lax.ppermute(x, axis, [(i, (i + distance) % n) for i in range(n)])]
    ppermute x16 -> x8, waiting for transfers between devices: 48.2 us -> 29.5 us  [the longest x4 15.2 us: tokens_in(): lax.ppermute(piece.reshape(sub, d_model), ('core', 'seq'), route(r))]
    dot_general x5 -> x1, matrix products: 18.4 us -> 0.75 us  [whole_sequences(): lax.dot_general(a, b, (((1,), (1,)), ((), ())), preferred_element_type=F32)]
    pallas_call x9 -> x8, Pallas kernels: 31.7 us -> 17.2 us  [place(): pl.pallas_call(kernel, grid_spec=pltpu.PrefetchScalarGridSpec(num_scalar_...]
    ppermute x56 -> x50, starting transfers between devices: 38.9 us -> 52.2 us  [swap(): lax.ppermute(x, axis, [(i, i ^ bit) for i in range(lax.axis_size(axis))])]
    ppermute x16 -> x8, starting transfers between devices: 26.6 us -> 16.1 us  [the longest x4 8.44 us: tokens_in(): lax.ppermute(piece.reshape(sub, d_model), ('core', 'seq'), route(r))]
  transfers between devices with their start and end apart: 96 -> 64, of which waited for: 42 -> 26; matrix products, arithmetic and copies ran while one was open for 15% -> 16% of each run, Pallas kernels for 7% -> 14%
where the time goes in v2:
time: 435 us; the launch traced here: 428 us
  waiting for transfers between devices  156 us (36%)
  starting transfers between devices  83.3 us (19%)
  Pallas kernels  74.1 us (17%)
  local copies, waits for them, and re-layouts  42.2 us (10%)
  other arithmetic  40.6 us (9%)
  matrix products  29.6 us (7%)
    ppermute x50, waiting for transfers between devices, swap(): lax.ppermute(x, axis, [(i, i ^ bit) for i in range(lax.axis_size(axis))])  99.4 us
    ppermute x50, starting transfers between devices, swap(): lax.ppermute(x, axis, [(i, i ^ bit) for i in range(lax.axis_size(axis))])  52.2 us
    pallas_call x1, Pallas kernels, backward_scan(): pl.pallas_call(backward_kernel, grid=(chunks,), in_specs=[row(width), row...  28.4 us
    ppermute x6, waiting for transfers between devices, turned(): return lax.ppermute(x, axis, [(i, (i + distance) % n) for i in range(n)])  26.7 us
    unnamed x176, local copies, waits for them, and re-layouts  21.3 us
    pallas_call x8, Pallas kernels, place(): pl.pallas_call(kernel, grid_spec=pltpu.PrefetchScalarGridSpec(num_scalar_...  17.2 us
    dot_general x10, matrix products, whole_sequences(): lax.dot_general(a, b, (((0,), (0,)), ((), ())), preferred_element_type=F32)  15.7 us
    pallas_call x1, Pallas kernels, forward_scan(): pl.pallas_call(forward_kernel, grid=(chunks,), in_specs=[row(width), row(...  15.5 us
  transfers between devices with their start and end apart: 64, of which 26 were waited for; matrix products, arithmetic and copies ran while one was open for 16% of the time, Pallas kernels for 14%

profile of v2, /device:TPU:8, one launch (start us, length us, event | category | flops | bytes accessed | tf_op | source)
XLA Modules:
  0.0 428.0 jit_solution(16681707075933609475)
XLA Ops:
  7.8 1.6 collective-permute-start.9
  11.8 5.0 %collective-permute-start.1 = (bf16[128,1536]{1,0:T(8,128)(2,1)S(1)}, bf16[128,1536]{1,0:T(8,128)(2,1)S(1)}, u32[]{:S(2)}, u32[]{:S(2)}) collective-permute-start(bf16[128,1536]{1,0:T(8,128)(2,1)S(1)} %get-tuple-element.224), channel_id=1, source_target_pairs={{0,0},{2,8},{4,4},{6,12},{8,2},{10,10},{12,6},{14,14},{1,1},{3,9},... | collective-permute-start | bytes 1179656 | tf_op jit(solution)/shard_map/ppermute | solution.py:770
  19.2 16.1 %collective-permute-done.9.refs_1_ = bf16[192,1024]{1,0:T(8,128)(2,1)S(1)} collective-permute-done((bf16[192,1024]{1,0:T(8,128)(2,1)S(1)}, bf16[192,1024]{1,0:T(8,128)(2,1)S(1)}, u32[]{:S(2)}, u32[]{:S(2)}) %collective-permute-start.9) | collective-permute-done | bytes 393248 | tf_op jit(solution)/shard_map/ppermute | solution.py:674
  35.3 2.9 collective-permute-start.11
  38.2 15.1 %collective-permute-done.2 = bf16[128,1536]{1,0:T(8,128)(2,1)S(1)} collective-permute-done((bf16[128,1536]{1,0:T(8,128)(2,1)S(1)}, bf16[128,1536]{1,0:T(8,128)(2,1)S(1)}, u32[]{:S(2)}, u32[]{:S(2)}) %collective-permute-start.2) | collective-permute-done | bytes 393248 | tf_op jit(solution)/shard_map/ppermute | solution.py:770
  54.7 1.5 collective-permute-start.6
  59.4 5.1 %collective-permute-done.12.refs_1_ = bf16[192,1024]{1,0:T(8,128)(2,1)S(1)} collective-permute-done((bf16[192,1024]{1,0:T(8,128)(2,1)S(1)}, bf16[192,1024]{1,0:T(8,128)(2,1)S(1)}, u32[]{:S(2)}, u32[]{:S(2)}) %collective-permute-start.12) | collective-permute-done | bytes 393248 | tf_op jit(solution)/shard_map/ppermute | solution.py:669
  64.5 4.3 %collective-permute-done.13.refs_2_ = bf16[192,1024]{1,0:T(8,128)(2,1)} collective-permute-done((bf16[192,1024]{1,0:T(8,128)(2,1)S(1)}, bf16[192,1024]{1,0:T(8,128)(2,1)}, u32[]{:S(2)}, u32[]{:S(2)}) %collective-permute-start.13) | collective-permute-done | bytes 393248 | tf_op jit(solution)/shard_map/ppermute | solution.py:669
  68.9 7.5 %collective-permute-start.15 = (bf16[192,1536]{1,0:T(8,128)(2,1)S(1)}, bf16[192,1536]{1,0:T(8,128)(2,1)S(1)}, u32[]{:S(2)}, u32[]{:S(2)}) collective-permute-start(bf16[192,1536]{1,0:T(8,128)(2,1)S(1)} %pad_maximum_fusion.6.refs_0_), channel_id=1, source_target_pairs={{0,2},{2,4},{4,6},{6,0},{1,3},{3,5},{5,7},{7,1},{8,10},{10,12},{12... | collective-permute-start | bytes 1769480 | tf_op jit(solution)/shard_map/ppermute | solution.py:674
  76.4 2.7 place.9
  80.7 2.8 place.10
  84.6 10.6 %collective-permute-done.15.refs_1_ = bf16[192,1536]{1,0:T(8,128)(2,1)S(1)} collective-permute-done((bf16[192,1536]{1,0:T(8,128)(2,1)S(1)}, bf16[192,1536]{1,0:T(8,128)(2,1)S(1)}, u32[]{:S(2)}, u32[]{:S(2)}) %collective-permute-start.15) | collective-permute-done | bytes 589856 | tf_op jit(solution)/shard_map/ppermute | solution.py:674
  97.3 2.5 collective-permute-start.21
  99.8 2.1 collective-permute-start.17
  101.9 2.1 place.8
  107.6 3.2 convolution_add_fusion.3.vpre
  111.4 10.0 %collective-permute-done.20.refs_2_ = bf16[192,1536]{1,0:T(8,128)(2,1)S(1)} collective-permute-done((bf16[192,1536]{1,0:T(8,128)(2,1)S(1)}, bf16[192,1536]{1,0:T(8,128)(2,1)S(1)}, u32[]{:S(2)}, u32[]{:S(2)}) %collective-permute-start.20) | collective-permute-done | bytes 589856 | tf_op jit(solution)/shard_map/ppermute | solution.py:669
  124.7 15.5 %scan_forward.1 = (f32[1024,768]{1,0:T(8,128)S(1)}, f32[8,128,768]{2,1,0:T(8,128)S(1)}, f32[1024,768]{1,0:T(8,128)S(1)}, f32[1024,256]{1,0:T(8,128)S(1)}) custom-call(f32[1024,768]{1,0:T(8,128)} %convolution_add_fusion.3.vpre, f32[1024,256]{1,0:T(8,128)S(1)} %pad_maximum_fusion.spre, f32[1024,128]{1,0:T(8,128)S(1)} %fusion.60.spre_step, ...), custom_call_target="tpu_custom_call" | custom-call | flops 3221225472 | bytes 15728640 | tf_op jit(solution)/shard_map/scan_forward/pallas_call | solution.py:450
  140.3 1.6 copy-done.34
  141.9 1.7 copy-done.35
  147.4 13.2 %collective-permute-done.27.refs_3_ = bf16[192,1536]{1,0:T(8,128)(2,1)S(1)} collective-permute-done((bf16[192,1536]{1,0:T(8,128)(2,1)S(1)}, bf16[192,1536]{1,0:T(8,128)(2,1)S(1)}, u32[]{:S(2)}, u32[]{:S(2)}) %collective-permute-start.27) | collective-permute-done | bytes 589856 | tf_op jit(solution)/shard_map/ppermute | solution.py:669
  161.8 2.8 collective-permute-done.24.refs_1_
  167.4 2.3 place.11
  171.4 2.1 multiply_reduce_fusion.2
  177.0 1.9 collective-permute-done.29
  179.0 4.1 fusion.27
  183.1 5.0 %paired_products.2 = (f32[512,1536]{1,0:T(8,128)}, f32[512,1536]{1,0:T(8,128)S(1)}) custom-call(s32[1]{0:T(128)} %bitcast.31.core, bf16[2,2,256,768]{3,2,1,0:T(8,128)(2,1)S(1)} %bitcast.188, bf16[768,768]{1,0:T(8,128)(2,1)S(1)} %get-tuple-element.216.refs_1_, bf16[768,768]{1,0:T(8,128)(2,1)S(1)} %get-tuple-element.214.refs_2_), custom_call_target="tpu_custom_call" | custom-call | flops 1 | bytes 1 | tf_op jit(solution)/shard_map/paired_products/pallas_call | solution.py:721
  188.1 1.7 copy-done.12
  190.1 3.5 fusion.32
  196.9 2.9 collective-permute-start.30
  199.9 2.5 convolution_convert_fusion.1
  202.9 2.6 fusion.37
  208.2 28.4 %scan_backward.1 = (bf16[1024,768]{1,0:T(8,128)(2,1)S(1)}, f32[1024,256]{1,0:T(8,128)S(1)}, bf16[1024,128]{1,0:T(8,128)(2,1)S(1)}, f32[8,768]{1,0:T(8,128)S(1)},...) custom-call(f32[1024,768]{1,0:T(8,128)S(1)} %copy-done.9, f32[1024,768]{1,0:T(8,128)S(1)} %copy-done.36, ...), custom_call_target="tpu_custom_call" | custom-call | flops 8053063680 | bytes 18874368 | tf_op jit(solution)/shard_map/scan_backward/pallas_call | solution.py:592
  236.6 14.8 %collective-permute-done.30 = bf16[2,2,2,96,768]{4,3,2,1,0:T(8,128)(2,1)S(1)} collective-permute-done((bf16[2,2,2,96,768]{4,3,2,1,0:T(8,128)(2,1)}, bf16[2,2,2,96,768]{4,3,2,1,0:T(8,128)(2,1)S(1)}, u32[]{:S(2)}, u32[]{:S(2)}) %collective-permute-start.30) | collective-permute-done | bytes 1179680 | tf_op jit(solution)/shard_map/ppermute | solution.py:669
  251.4 2.5 convolution_convert_fusion
  259.8 8.1 %paired_products.3 = (f32[512,1536]{1,0:T(8,128)}, f32[512,1536]{1,0:T(8,128)}) custom-call(s32[1]{0:T(128)} %bitcast.31.core, bf16[2,2,256,768]{3,2,1,0:T(8,128)(2,1)S(1)} %bitcast.187, bf16[2,2,256,768]{3,2,1,0:T(8,128)(2,1)S(1)} %bitcast.191, bf16[2,2,256,128]{3,2,1,0:T(8,128)(2,1)S(1)} %bitcast.193, bf16[768,768]{1,0:T(8,128)(2,1)S(1)} %copy-done.7, ...), custom_call_target="tpu_custom_call" | custom-call | flops 1 | bytes 1 | tf_op jit(solution)/shard_map/paired_products/pallas_call | solution.py:721
  270.1 3.3 collective-permute-start.35
  273.8 2.5 fusion.25
  280.3 16.9 %collective-permute-done.35 = bf16[2,2,96,768]{3,2,1,0:T(8,128)(2,1)S(1)} collective-permute-done((bf16[2,2,96,768]{3,2,1,0:T(8,128)(2,1)}, bf16[2,2,96,768]{3,2,1,0:T(8,128)(2,1)S(1)}, u32[]{:S(2)}, u32[]{:S(2)}) %collective-permute-start.35) | collective-permute-done | bytes 589856 | tf_op jit(solution)/shard_map/ppermute | solution.py:669
  297.8 1.8 fusion.38
  300.2 4.0 collective-permute-start.40
  304.2 1.7 collective-permute-start.41
  308.8 2.9 convert_add_fusion.1
  314.3 9.7 %collective-permute-done.42 = bf16[2,96,768]{2,1,0:T(8,128)(2,1)S(1)} collective-permute-done((bf16[2,96,768]{2,1,0:T(8,128)(2,1)S(1)}, bf16[2,96,768]{2,1,0:T(8,128)(2,1)S(1)}, u32[]{:S(2)}, u32[]{:S(2)}) %collective-permute-start.42) | collective-permute-done | bytes 294944 | tf_op jit(solution)/shard_map/ppermute | solution.py:669
  324.1 2.6 collective-permute-start.47
  329.1 2.7 fusion.20
  332.0 1.8 fusion.23
  335.5 1.9 collective-permute-start.48
  337.6 2.1 collective-permute-done.47
  339.7 2.6 bitcast_add_fusion.4
  342.3 5.7 %collective-permute-done.48.refs_0_ = bf16[128,1536]{1,0:T(8,128)(2,1)S(1)} collective-permute-done((bf16[128,1536]{1,0:T(8,128)(2,1)S(1)}, bf16[128,1536]{1,0:T(8,128)(2,1)S(1)}, u32[]{:S(2)}, u32[]{:S(2)}) %collective-permute-start.48) | collective-permute-done | bytes 393248 | tf_op jit(solution)/shard_map/ppermute | solution.py:776
  348.0 8.6 %collective-permute-done.49.refs_1_ = bf16[128,1536]{1,0:T(8,128)(2,1)S(1)} collective-permute-done((bf16[128,1536]{1,0:T(8,128)(2,1)S(1)}, bf16[128,1536]{1,0:T(8,128)(2,1)S(1)}, u32[]{:S(2)}, u32[]{:S(2)}) %collective-permute-start.49) | collective-permute-done | bytes 393248 | tf_op jit(solution)/shard_map/ppermute | solution.py:776
  356.6 1.5 collective-permute-start.52
  358.8 1.5 collective-permute-start.46
  361.9 9.7 %collective-permute-start.54 = (f32[62,256]{1,0:T(8,128)S(1)}, f32[62,256]{1,0:T(8,128)S(1)}, u32[]{:S(2)}, u32[]{:S(2)}) collective-permute-start(f32[62,256]{1,0:T(8,128)S(1)} %pad_maximum_fusion.12), channel_id=1, source_target_pairs={{0,16},{16,0},{1,17},{17,1},{2,18},{18,2},{3,19},{19,3},{4,20},{20... | collective-permute-start | bytes 190472 | tf_op jit(solution)/shard_map/ppermute | solution.py:669
  372.9 2.9 collective-permute-done.46.refs_3_
  375.8 2.5 place.14
  378.9 1.5 collective-permute-start.51
  380.4 2.7 collective-permute-start.55
  384.2 7.4 %collective-permute-done.55 = f32[62,256]{1,0:T(8,128)S(1)} collective-permute-done((f32[62,256]{1,0:T(8,128)S(1)}, f32[62,256]{1,0:T(8,128)S(1)}, u32[]{:S(2)}, u32[]{:S(2)}) %collective-permute-start.55) | collective-permute-done | bytes 63520 | tf_op jit(solution)/shard_map/ppermute | solution.py:669
  392.8 3.7 collective-permute-start.56
  407.6 2.5 place.15
  410.1 2.2 bitcast_select_fusion.1
  423.5 3.6 collective-permute-done.61
  (424 shorter events, 100.4 us)
Async XLA Ops:
  4.4 1.5 collective-permute-start
  6.1 5.7 %collective-permute-start.3 = (bf16[96,1536]{1,0:T(8,128)(2,1)S(1)}, bf16[96,1536]{1,0:T(8,128)(2,1)S(1)}, u32[]{:S(2)}, u32[]{:S(2)}) collective-permute-start(bf16[96,1536]{1,0:T(8,128)(2,1)S(1)} %constant_dynamic-slice_fusion.15), channel_id=1, source_target_pairs={{0,8},{8,0},{1,9},{9,1},{2,10},{10,2},{3,11},{11,3},{4,12},{12,4},... | collective-permute-start | bytes 884744 | tf_op jit(solution)/shard_map/ppermute | solution.py:669
  6.3 11.4 %collective-permute-start.4 = (bf16[192,1024]{1,0:T(8,128)(2,1)S(1)}, bf16[192,1024]{1,0:T(8,128)(2,1)S(1)}, u32[]{:S(2)}, u32[]{:S(2)}) collective-permute-start(bf16[192,1024]{1,0:T(8,128)(2,1)S(1)} %pad_maximum_fusion.7.refs_0_), channel_id=1, source_target_pairs={{0,16},{16,0},{1,17},{17,1},{2,18},{18,2},{3,19},{19,3},{4,20},{20... | collective-permute-start | bytes 1179656 | tf_op jit(solution)/shard_map/ppermute | solution.py:669
  7.8 27.5 %collective-permute-start.9 = (bf16[192,1024]{1,0:T(8,128)(2,1)S(1)}, bf16[192,1024]{1,0:T(8,128)(2,1)S(1)}, u32[]{:S(2)}, u32[]{:S(2)}) collective-permute-start(bf16[192,1024]{1,0:T(8,128)(2,1)S(1)} %pad_maximum_fusion.7.refs_0_), channel_id=1, source_target_pairs={{0,2},{2,4},{4,6},{6,0},{1,3},{3,5},{5,7},{7,1},{8,10},{10,12},{12... | collective-permute-start | bytes 1179656 | tf_op jit(solution)/shard_map/ppermute | solution.py:674
  9.4 25.9 %collective-permute-start.10 = (bf16[192,1024]{1,0:T(8,128)(2,1)S(1)}, bf16[192,1024]{1,0:T(8,128)(2,1)S(1)}, u32[]{:S(2)}, u32[]{:S(2)}) collective-permute-start(bf16[192,1024]{1,0:T(8,128)(2,1)S(1)} %pad_maximum_fusion.7.refs_0_), channel_id=1, source_target_pairs={{0,6},{2,0},{4,2},{6,4},{1,7},{3,1},{5,3},{7,5},{8,14},{10,8},{12,... | collective-permute-start | bytes 1179656 | tf_op jit(solution)/shard_map/ppermute | solution.py:674
  11.0 42.4 %collective-permute-start.2 = (bf16[128,1536]{1,0:T(8,128)(2,1)S(1)}, bf16[128,1536]{1,0:T(8,128)(2,1)S(1)}, u32[]{:S(2)}, u32[]{:S(2)}) collective-permute-start(bf16[128,1536]{1,0:T(8,128)(2,1)S(1)} %get-tuple-element.223), channel_id=1, source_target_pairs={{0,4},{2,12},{4,0},{6,8},{8,6},{10,14},{12,2},{14,10},{1,5},{3,13}... | collective-permute-start | bytes 1179656 | tf_op jit(solution)/shard_map/ppermute | solution.py:770
  11.8 41.6 %collective-permute-start.1 = (bf16[128,1536]{1,0:T(8,128)(2,1)S(1)}, bf16[128,1536]{1,0:T(8,128)(2,1)S(1)}, u32[]{:S(2)}, u32[]{:S(2)}) collective-permute-start(bf16[128,1536]{1,0:T(8,128)(2,1)S(1)} %get-tuple-element.224), channel_id=1, source_target_pairs={{0,0},{2,8},{4,4},{6,12},{8,2},{10,10},{12,6},{14,14},{1,1},{3,9},... | collective-permute-start | bytes 1179656 | tf_op jit(solution)/shard_map/ppermute | solution.py:770
  17.7 36.2 %collective-permute-start.5 = (bf16[192,1536]{1,0:T(8,128)(2,1)S(1)}, bf16[192,1536]{1,0:T(8,128)(2,1)S(1)}, u32[]{:S(2)}, u32[]{:S(2)}) collective-permute-start(bf16[192,1536]{1,0:T(8,128)(2,1)S(1)} %pad_maximum_fusion.6.refs_0_), channel_id=1, source_target_pairs={{0,16},{16,0},{1,17},{17,1},{2,18},{18,2},{3,19},{19,3},{4,20},{20... | collective-permute-start | bytes 1769480 | tf_op jit(solution)/shard_map/ppermute | solution.py:669
  35.3 23.1 %collective-permute-start.11 = (bf16[192,1024]{1,0:T(8,128)(2,1)S(1)}, bf16[192,1024]{1,0:T(8,128)(2,1)S(1)}, u32[]{:S(2)}, u32[]{:S(2)}) collective-permute-start(bf16[192,1024]{1,0:T(8,128)(2,1)S(1)} %collective-permute-done.9.refs_1_), channel_id=1, source_target_pairs={{0,2},{2,4},{4,6},{6,0},{1,3},{3,5},{5,7},{7,1},{8,10},{10,12},{12... | collective-permute-start | bytes 1179656 | tf_op jit(solution)/shard_map/ppermute | solution.py:674
  54.7 28.8 %collective-permute-start.6 = (bf16[256,1536]{1,0:T(8,128)(2,1)S(1)}, bf16[256,1536]{1,0:T(8,128)(2,1)}, u32[]{:S(2)}, u32[]{:S(2)}) collective-permute-start(bf16[256,1536]{1,0:T(8,128)(2,1)S(1)} %get-tuple-element.88.refs_0_), channel_id=1, source_target_pairs={{0,1},{1,0},{2,3},{3,2},{4,5},{5,4},{6,7},{7,6},{8,9},{9,8},{10,11... | collective-permute-start | bytes 2359304 | tf_op jit(solution)/shard_map/ppermute | solution.py:669
  56.2 8.3 %collective-permute-start.12 = (bf16[192,1024]{1,0:T(8,128)(2,1)S(1)}, bf16[192,1024]{1,0:T(8,128)(2,1)S(1)}, u32[]{:S(2)}, u32[]{:S(2)}) collective-permute-start(bf16[192,1024]{1,0:T(8,128)(2,1)S(1)} %collective-permute-done.9.refs_1_), channel_id=1, source_target_pairs={{0,16},{16,0},{1,17},{17,1},{2,18},{18,2},{3,19},{19,3},{4,20},{20... | collective-permute-start | bytes 1179656 | tf_op jit(solution)/shard_map/ppermute | solution.py:669
  56.8 12.1 %collective-permute-start.13 = (bf16[192,1024]{1,0:T(8,128)(2,1)S(1)}, bf16[192,1024]{1,0:T(8,128)(2,1)}, u32[]{:S(2)}, u32[]{:S(2)}) collective-permute-start(bf16[192,1024]{1,0:T(8,128)(2,1)S(1)} %collective-permute-done.10.refs_2_), channel_id=1, source_target_pairs={{0,16},{16,0},{1,17},{17,1},{2,18},{18,2},{3,19},{19,3},{4,20},{20... | collective-permute-start | bytes 1179656 | tf_op jit(solution)/shard_map/ppermute | solution.py:669
  58.3 21.1 %collective-permute-start.14 = (bf16[192,1024]{1,0:T(8,128)(2,1)S(1)}, bf16[192,1024]{1,0:T(8,128)(2,1)}, u32[]{:S(2)}, u32[]{:S(2)}) collective-permute-start(bf16[192,1024]{1,0:T(8,128)(2,1)S(1)} %collective-permute-done.11.refs_3_), channel_id=1, source_target_pairs={{0,16},{16,0},{1,17},{17,1},{2,18},{18,2},{3,19},{19,3},{4,20},{20... | collective-permute-start | bytes 1179656 | tf_op jit(solution)/shard_map/ppermute | solution.py:669
  68.9 26.3 %collective-permute-start.15 = (bf16[192,1536]{1,0:T(8,128)(2,1)S(1)}, bf16[192,1536]{1,0:T(8,128)(2,1)S(1)}, u32[]{:S(2)}, u32[]{:S(2)}) collective-permute-start(bf16[192,1536]{1,0:T(8,128)(2,1)S(1)} %pad_maximum_fusion.6.refs_0_), channel_id=1, source_target_pairs={{0,2},{2,4},{4,6},{6,0},{1,3},{3,5},{5,7},{7,1},{8,10},{10,12},{12... | collective-permute-start | bytes 1769480 | tf_op jit(solution)/shard_map/ppermute | solution.py:674
  76.4 19.3 %collective-permute-start.16 = (bf16[192,1536]{1,0:T(8,128)(2,1)S(1)}, bf16[192,1536]{1,0:T(8,128)(2,1)S(1)}, u32[]{:S(2)}, u32[]{:S(2)}) collective-permute-start(bf16[192,1536]{1,0:T(8,128)(2,1)S(1)} %pad_maximum_fusion.6.refs_0_), channel_id=1, source_target_pairs={{0,6},{2,0},{4,2},{6,4},{1,7},{3,1},{5,3},{7,5},{8,14},{10,8},{12,... | collective-permute-start | bytes 1769480 | tf_op jit(solution)/shard_map/ppermute | solution.py:674
  79.3 17.9 %collective-permute-start.7 = (bf16[256,1536]{1,0:T(8,128)(2,1)S(1)}, bf16[256,1536]{1,0:T(8,128)(2,1)S(1)}, u32[]{:S(2)}, u32[]{:S(2)}) collective-permute-start(bf16[256,1536]{1,0:T(8,128)(2,1)S(1)} %get-tuple-element.88.refs_0_), channel_id=1, source_target_pairs={{0,8},{8,0},{1,9},{9,1},{2,10},{10,2},{3,11},{11,3},{4,12},{12,4},... | collective-permute-start | bytes 2359304 | tf_op jit(solution)/shard_map/ppermute | solution.py:669
  83.5 16.3 %collective-permute-start.8 = (bf16[256,1536]{1,0:T(8,128)(2,1)}, bf16[256,1536]{1,0:T(8,128)(2,1)S(1)}, u32[]{:S(2)}, u32[]{:S(2)}) collective-permute-start(bf16[256,1536]{1,0:T(8,128)(2,1)} %collective-permute-done.6.refs_1_), channel_id=1, source_target_pairs={{0,8},{8,0},{1,9},{9,1},{2,10},{10,2},{3,11},{11,3},{4,12},{12,4},... | collective-permute-start | bytes 2359304 | tf_op jit(solution)/shard_map/ppermute | solution.py:669
  84.0 26.7 %collective-permute-start.18 = (bf16[1536,128]{1,0:T(8,128)(2,1)S(1)}, bf16[1536,128]{1,0:T(8,128)(2,1)S(1)}, u32[]{:S(2)}, u32[]{:S(2)}) collective-permute-start(bf16[1536,128]{1,0:T(8,128)(2,1)S(1)} %pad_maximum_fusion.8), channel_id=1, source_target_pairs={{0,8},{8,0},{1,9},{9,1},{2,10},{10,2},{3,11},{11,3},{4,12},{12,4},... | collective-permute-start | bytes 1179656 | tf_op jit(solution)/shard_map/ppermute | solution.py:669
  95.2 16.3 %collective-permute-start.19 = (bf16[192,1536]{1,0:T(8,128)(2,1)S(1)}, bf16[192,1536]{1,0:T(8,128)(2,1)S(1)}, u32[]{:S(2)}, u32[]{:S(2)}) collective-permute-start(bf16[192,1536]{1,0:T(8,128)(2,1)S(1)} %collective-permute-done.15.refs_1_), channel_id=1, source_target_pairs={{0,16},{16,0},{1,17},{17,1},{2,18},{18,2},{3,19},{19,3},{4,20},{20... | collective-permute-start | bytes 1769480 | tf_op jit(solution)/shard_map/ppermute | solution.py:669
  95.7 25.7 %collective-permute-start.20 = (bf16[192,1536]{1,0:T(8,128)(2,1)S(1)}, bf16[192,1536]{1,0:T(8,128)(2,1)S(1)}, u32[]{:S(2)}, u32[]{:S(2)}) collective-permute-start(bf16[192,1536]{1,0:T(8,128)(2,1)S(1)} %collective-permute-done.16.refs_2_), channel_id=1, source_target_pairs={{0,16},{16,0},{1,17},{17,1},{2,18},{18,2},{3,19},{19,3},{4,20},{20... | collective-permute-start | bytes 1769480 | tf_op jit(solution)/shard_map/ppermute | solution.py:669
  97.3 24.1 %collective-permute-start.21 = (bf16[192,1536]{1,0:T(8,128)(2,1)S(1)}, bf16[192,1536]{1,0:T(8,128)(2,1)S(1)}, u32[]{:S(2)}, u32[]{:S(2)}) collective-permute-start(bf16[192,1536]{1,0:T(8,128)(2,1)S(1)} %collective-permute-done.15.refs_1_), channel_id=1, source_target_pairs={{0,2},{2,4},{4,6},{6,0},{1,3},{3,5},{5,7},{7,1},{8,10},{10,12},{12... | collective-permute-start | bytes 1769480 | tf_op jit(solution)/shard_map/ppermute | solution.py:674
  99.8 44.8 %collective-permute-start.17 = (bf16[128,1536]{1,0:T(8,128)(2,1)S(1)}, bf16[128,1536]{1,0:T(8,128)(2,1)S(1)}, u32[]{:S(2)}, u32[]{:S(2)}) collective-permute-start(bf16[128,1536]{1,0:T(8,128)(2,1)S(1)} %get-tuple-element.217), channel_id=1, source_target_pairs={{0,0},{2,8},{4,4},{6,12},{8,2},{10,10},{12,6},{14,14},{1,1},{3,9},... | collective-permute-start | bytes 1179656 | tf_op jit(solution)/shard_map/ppermute | solution.py:770
  110.7 33.9 %collective-permute-start.23 = (bf16[128,1536]{1,0:T(8,128)(2,1)S(1)}, bf16[128,1536]{1,0:T(8,128)(2,1)S(1)}, u32[]{:S(2)}, u32[]{:S(2)}) collective-permute-start(bf16[128,1536]{1,0:T(8,128)(2,1)S(1)} %get-tuple-element.218), channel_id=1, source_target_pairs={{0,4},{2,12},{4,0},{6,8},{8,6},{10,14},{12,2},{14,10},{1,5},{3,13}... | collective-permute-start | bytes 1179656 | tf_op jit(solution)/shard_map/ppermute | solution.py:770
  122.0 2.0 collective-permute-start.22
  144.9 19.6 %collective-permute-start.24 = (bf16[256,1536]{1,0:T(8,128)(2,1)S(1)}, bf16[256,1536]{1,0:T(8,128)(2,1)S(1)}, u32[]{:S(2)}, u32[]{:S(2)}) collective-permute-start(bf16[256,1536]{1,0:T(8,128)(2,1)S(1)} %fusion.35.refs_0_), channel_id=1, source_target_pairs={{0,1},{1,0},{2,3},{3,2},{4,5},{5,4},{6,7},{7,6},{8,9},{9,8},{10,11... | collective-permute-start | bytes 2359304 | tf_op jit(solution)/shard_map/ppermute | solution.py:669
  145.5 15.1 %collective-permute-start.27 = (bf16[192,1536]{1,0:T(8,128)(2,1)S(1)}, bf16[192,1536]{1,0:T(8,128)(2,1)S(1)}, u32[]{:S(2)}, u32[]{:S(2)}) collective-permute-start(bf16[192,1536]{1,0:T(8,128)(2,1)S(1)} %collective-permute-done.21.refs_3_), channel_id=1, source_target_pairs={{0,16},{16,0},{1,17},{17,1},{2,18},{18,2},{3,19},{19,3},{4,20},{20... | collective-permute-start | bytes 1769480 | tf_op jit(solution)/shard_map/ppermute | solution.py:669
  161.7 5.7 %collective-permute-start.25 = (bf16[256,1536]{1,0:T(8,128)(2,1)S(1)}, bf16[256,1536]{1,0:T(8,128)(2,1)S(1)}, u32[]{:S(2)}, u32[]{:S(2)}) collective-permute-start(bf16[256,1536]{1,0:T(8,128)(2,1)S(1)} %fusion.35.refs_0_), channel_id=1, source_target_pairs={{0,8},{8,0},{1,9},{9,1},{2,10},{10,2},{3,11},{11,3},{4,12},{12,4},... | collective-permute-start | bytes 2359304 | tf_op jit(solution)/shard_map/ppermute | solution.py:669
  164.6 2.8 collective-permute-start.26
  173.5 1.7 collective-permute-start.28
  175.2 3.7 collective-permute-start.29
  189.8 13.1 %collective-permute-start.32 = (f32[512,1536]{1,0:T(8,128)}, f32[512,1536]{1,0:T(8,128)}, u32[]{:S(2)}, u32[]{:S(2)}) collective-permute-start(f32[512,1536]{1,0:T(8,128)} %get-tuple-element.103), channel_id=1, source_target_pairs={{0,8},{8,0},{1,9},{9,1},{2,10},{10,2},{3,11},{11,3},{4,12},{12,4},... | collective-permute-start | bytes 9437192 | tf_op jit(solution)/shard_map/ppermute | solution.py:669
  196.9 54.4 %collective-permute-start.30 = (bf16[2,2,2,96,768]{4,3,2,1,0:T(8,128)(2,1)}, bf16[2,2,2,96,768]{4,3,2,1,0:T(8,128)(2,1)S(1)}, u32[]{:S(2)}, u32[]{:S(2)}) collective-permute-start(bf16[2,2,2,96,768]{4,3,2,1,0:T(8,128)(2,1)} %fusion.7), channel_id=1, source_target_pairs={{0,4},{2,6},{4,0},{6,2},{1,5},{3,7},{5,1},{7,3},{8,12},{10,14},{12... | collective-permute-start | bytes 3538952 | tf_op jit(solution)/shard_map/ppermute | solution.py:669
  202.3 49.0 %collective-permute-start.31 = (bf16[768,768]{1,0:T(8,128)(2,1)}, bf16[768,768]{1,0:T(8,128)(2,1)}, u32[]{:S(2)}, u32[]{:S(2)}) collective-permute-start(bf16[768,768]{1,0:T(8,128)(2,1)} %convolution_convert_fusion.1), channel_id=1, source_target_pairs={{0,16},{16,0},{1,17},{17,1},{2,18},{18,2},{3,19},{19,3},{4,20},{20... | collective-permute-start | bytes 3538952 | tf_op jit(solution)/shard_map/ppermute | solution.py:669
  205.5 45.8 %collective-permute-start.33 = (bf16[2,128,1536]{2,1,0:T(8,128)(2,1)}, bf16[2,128,1536]{2,1,0:T(8,128)(2,1)}, u32[]{:S(2)}, u32[]{:S(2)}) collective-permute-start(bf16[2,128,1536]{2,1,0:T(8,128)(2,1)} %fusion.37), channel_id=1, source_target_pairs={{0,1},{1,0},{2,3},{3,2},{4,5},{5,4},{6,7},{7,6},{8,9},{9,8},{10,11... | collective-permute-start | bytes 2359304 | tf_op jit(solution)/shard_map/ppermute | solution.py:669
  257.0 1.9 collective-permute-start.36
  267.9 29.8 %collective-permute-start.38 = (f32[512,1536]{1,0:T(8,128)}, f32[512,1536]{1,0:T(8,128)}, u32[]{:S(2)}, u32[]{:S(2)}) collective-permute-start(f32[512,1536]{1,0:T(8,128)} %get-tuple-element.124), channel_id=1, source_target_pairs={{0,8},{8,0},{1,9},{9,1},{2,10},{10,2},{3,11},{11,3},{4,12},{12,4},... | collective-permute-start | bytes 9437192 | tf_op jit(solution)/shard_map/ppermute | solution.py:669
  269.5 28.2 %collective-permute-start.34 = (bf16[768,768]{1,0:T(8,128)(2,1)S(1)}, bf16[768,768]{1,0:T(8,128)(2,1)S(1)}, u32[]{:S(2)}, u32[]{:S(2)}) collective-permute-start(bf16[768,768]{1,0:T(8,128)(2,1)S(1)} %copy-done.82), channel_id=1, source_target_pairs={{0,16},{16,0},{1,17},{17,1},{2,18},{18,2},{3,19},{19,3},{4,20},{20... | collective-permute-start | bytes 3538952 | tf_op jit(solution)/shard_map/ppermute | solution.py:669
  270.1 27.1 %collective-permute-start.35 = (bf16[2,2,96,768]{3,2,1,0:T(8,128)(2,1)}, bf16[2,2,96,768]{3,2,1,0:T(8,128)(2,1)S(1)}, u32[]{:S(2)}, u32[]{:S(2)}) collective-permute-start(bf16[2,2,96,768]{3,2,1,0:T(8,128)(2,1)} %dynamic-slice_convert_fusion.1), channel_id=1, source_target_pairs={{0,4},{2,6},{4,0},{6,2},{1,5},{3,7},{5,1},{7,3},{8,12},{10,14},{12... | collective-permute-start | bytes 1769480 | tf_op jit(solution)/shard_map/ppermute | solution.py:669
  273.4 23.9 %collective-permute-start.37 = (f32[2,128,256]{2,1,0:T(8,128)}, f32[2,128,256]{2,1,0:T(8,128)S(1)}, u32[]{:S(2)}, u32[]{:S(2)}) collective-permute-start(f32[2,128,256]{2,1,0:T(8,128)} %fusion.79), channel_id=1, source_target_pairs={{0,1},{1,0},{2,3},{3,2},{4,5},{5,4},{6,7},{7,6},{8,9},{9,8},{10,11... | collective-permute-start | bytes 786440 | tf_op jit(solution)/shard_map/ppermute | solution.py:669
  299.5 24.5 %collective-permute-start.39 = (bf16[2,128,1536]{2,1,0:T(8,128)(2,1)S(1)}, bf16[2,128,1536]{2,1,0:T(8,128)(2,1)S(1)}, u32[]{:S(2)}, u32[]{:S(2)}) collective-permute-start(bf16[2,128,1536]{2,1,0:T(8,128)(2,1)S(1)} %fusion.38), channel_id=1, source_target_pairs={{0,1},{1,0},{2,3},{3,2},{4,5},{5,4},{6,7},{7,6},{8,9},{9,8},{10,11... | collective-permute-start | bytes 2359304 | tf_op jit(solution)/shard_map/ppermute | solution.py:669
  300.2 23.9 %collective-permute-start.40 = (bf16[128,1536]{1,0:T(8,128)(2,1)S(1)}, bf16[128,1536]{1,0:T(8,128)(2,1)S(1)}, u32[]{:S(2)}, u32[]{:S(2)}) collective-permute-start(bf16[128,1536]{1,0:T(8,128)(2,1)S(1)} %get-tuple-element.250), channel_id=1, source_target_pairs={{0,0},{8,2},{4,4},{12,6},{2,8},{10,10},{6,12},{14,14},{1,1},{9,3},... | collective-permute-start | bytes 1179656 | tf_op jit(solution)/shard_map/ppermute | solution.py:776
  304.2 19.8 %collective-permute-start.41 = (bf16[128,1536]{1,0:T(8,128)(2,1)S(1)}, bf16[128,1536]{1,0:T(8,128)(2,1)S(1)}, u32[]{:S(2)}, u32[]{:S(2)}) collective-permute-start(bf16[128,1536]{1,0:T(8,128)(2,1)S(1)} %get-tuple-element.249), channel_id=1, source_target_pairs={{4,0},{12,2},{0,4},{8,6},{6,8},{14,10},{2,12},{10,14},{5,1},{13,3}... | collective-permute-start | bytes 1179656 | tf_op jit(solution)/shard_map/ppermute | solution.py:776
  306.1 17.9 %collective-permute-start.42 = (bf16[2,96,768]{2,1,0:T(8,128)(2,1)S(1)}, bf16[2,96,768]{2,1,0:T(8,128)(2,1)S(1)}, u32[]{:S(2)}, u32[]{:S(2)}) collective-permute-start(bf16[2,96,768]{2,1,0:T(8,128)(2,1)S(1)} %fusion.77), channel_id=1, source_target_pairs={{0,2},{2,0},{4,6},{6,4},{1,3},{3,1},{5,7},{7,5},{8,10},{10,8},{12,... | collective-permute-start | bytes 884744 | tf_op jit(solution)/shard_map/ppermute | solution.py:669
  306.3 5.8 %collective-permute-start.43 = (bf16[256,256]{1,0:T(8,128)(2,1)S(1)}, bf16[256,256]{1,0:T(8,128)(2,1)S(1)}, u32[]{:S(2)}, u32[]{:S(2)}) collective-permute-start(bf16[256,256]{1,0:T(8,128)(2,1)S(1)} %bitcast.218), channel_id=1, source_target_pairs={{0,8},{8,0},{1,9},{9,1},{2,10},{10,2},{3,11},{11,3},{4,12},{12,4},... | collective-permute-start | bytes 393224 | tf_op jit(solution)/shard_map/ppermute | solution.py:669
  312.6 11.5 %collective-permute-start.44 = (bf16[768,256]{0,1:T(8,128)(2,1)S(1)}, bf16[768,256]{0,1:T(8,128)(2,1)S(1)}, u32[]{:S(2)}, u32[]{:S(2)}) collective-permute-start(bf16[768,256]{0,1:T(8,128)(2,1)S(1)} %pad_maximum_fusion.9), channel_id=1, source_target_pairs={{0,16},{16,0},{1,17},{17,1},{2,18},{18,2},{3,19},{19,3},{4,20},{20... | collective-permute-start | bytes 1179656 | tf_op jit(solution)/shard_map/ppermute | solution.py:669
  324.1 15.6 %collective-permute-start.47 = (bf16[2,2,96,768]{3,2,1,0:T(8,128)(2,1)}, bf16[2,2,96,768]{3,2,1,0:T(8,128)(2,1)}, u32[]{:S(2)}, u32[]{:S(2)}) collective-permute-start(bf16[2,2,96,768]{3,2,1,0:T(8,128)(2,1)} %fusion.46), channel_id=1, source_target_pairs={{0,2},{2,0},{4,6},{6,4},{1,3},{3,1},{5,7},{7,5},{8,10},{10,8},{12,... | collective-permute-start | bytes 1769480 | tf_op jit(solution)/shard_map/ppermute | solution.py:669
  335.5 12.5 %collective-permute-start.48 = (bf16[128,1536]{1,0:T(8,128)(2,1)S(1)}, bf16[128,1536]{1,0:T(8,128)(2,1)S(1)}, u32[]{:S(2)}, u32[]{:S(2)}) collective-permute-start(bf16[128,1536]{1,0:T(8,128)(2,1)S(1)} %get-tuple-element.244), channel_id=1, source_target_pairs={{0,0},{8,2},{4,4},{12,6},{2,8},{10,10},{6,12},{14,14},{1,1},{9,3},... | collective-permute-start | bytes 1179656 | tf_op jit(solution)/shard_map/ppermute | solution.py:776
  337.4 19.2 %collective-permute-start.49 = (bf16[128,1536]{1,0:T(8,128)(2,1)S(1)}, bf16[128,1536]{1,0:T(8,128)(2,1)S(1)}, u32[]{:S(2)}, u32[]{:S(2)}) collective-permute-start(bf16[128,1536]{1,0:T(8,128)(2,1)S(1)} %get-tuple-element.243), channel_id=1, source_target_pairs={{4,0},{12,2},{0,4},{8,6},{6,8},{14,10},{2,12},{10,14},{5,1},{13,3}... | collective-permute-start | bytes 1179656 | tf_op jit(solution)/shard_map/ppermute | solution.py:776
  356.6 4.0 collective-permute-start.52
  358.2 34.6 %collective-permute-start.58 = (bf16[2,2,96,1024]{3,2,1,0:T(8,128)(2,1)}, bf16[2,2,96,1024]{3,2,1,0:T(8,128)(2,1)}, u32[]{:S(2)}, u32[]{:S(2)}) collective-permute-start(bf16[2,2,96,1024]{3,2,1,0:T(8,128)(2,1)} %fusion.20), channel_id=1, source_target_pairs={{0,4},{2,6},{4,0},{6,2},{1,5},{3,7},{5,1},{7,3},{8,12},{10,14},{12... | collective-permute-start | bytes 2359304 | tf_op jit(solution)/shard_map/ppermute | solution.py:669
  358.3 14.6 %collective-permute-start.45 = (bf16[128,1536]{1,0:T(8,128)(2,1)S(1)}, bf16[128,1536]{1,0:T(8,128)(2,1)S(1)}, u32[]{:S(2)}, u32[]{:S(2)}) collective-permute-start(bf16[128,1536]{1,0:T(8,128)(2,1)S(1)} %collective-permute-done.40.refs_0_), channel_id=1, source_target_pairs={{0,1},{1,0},{2,3},{3,2},{4,5},{5,4},{6,7},{7,6},{8,9},{9,8},{10,11... | collective-permute-start | bytes 1179656 | tf_op jit(solution)/shard_map/ppermute | solution.py:669
  358.8 17.0 %collective-permute-start.46 = (bf16[128,1536]{1,0:T(8,128)(2,1)S(1)}, bf16[128,1536]{1,0:T(8,128)(2,1)S(1)}, u32[]{:S(2)}, u32[]{:S(2)}) collective-permute-start(bf16[128,1536]{1,0:T(8,128)(2,1)S(1)} %collective-permute-done.41.refs_1_), channel_id=1, source_target_pairs={{0,1},{1,0},{2,3},{3,2},{4,5},{5,4},{6,7},{7,6},{8,9},{9,8},{10,11... | collective-permute-start | bytes 1179656 | tf_op jit(solution)/shard_map/ppermute | solution.py:669
  360.6 1.3 collective-permute-start.53
  361.9 18.5 %collective-permute-start.54 = (f32[62,256]{1,0:T(8,128)S(1)}, f32[62,256]{1,0:T(8,128)S(1)}, u32[]{:S(2)}, u32[]{:S(2)}) collective-permute-start(f32[62,256]{1,0:T(8,128)S(1)} %pad_maximum_fusion.12), channel_id=1, source_target_pairs={{0,16},{16,0},{1,17},{17,1},{2,18},{18,2},{3,19},{19,3},{4,20},{20... | collective-permute-start | bytes 190472 | tf_op jit(solution)/shard_map/ppermute | solution.py:669
  372.5 37.5 %collective-permute-start.57 = (f32[96,768]{0,1:T(8,128)}, f32[96,768]{0,1:T(8,128)}, u32[]{:S(2)}, u32[]{:S(2)}) collective-permute-start(f32[96,768]{0,1:T(8,128)} %bitcast.76), channel_id=1, source_target_pairs={{0,8},{8,0},{1,9},{9,1},{2,10},{10,2},{3,11},{11,3},{4,12},{12,4},... | collective-permute-start | bytes 884744 | tf_op jit(solution)/shard_map/ppermute | solution.py:669
  378.3 29.2 %collective-permute-start.50 = (bf16[128,1536]{1,0:T(8,128)(2,1)S(1)}, bf16[128,1536]{1,0:T(8,128)(2,1)S(1)}, u32[]{:S(2)}, u32[]{:S(2)}) collective-permute-start(bf16[128,1536]{1,0:T(8,128)(2,1)S(1)} %collective-permute-done.48.refs_0_), channel_id=1, source_target_pairs={{0,1},{1,0},{2,3},{3,2},{4,5},{5,4},{6,7},{7,6},{8,9},{9,8},{10,11... | collective-permute-start | bytes 1179656 | tf_op jit(solution)/shard_map/ppermute | solution.py:669
  378.9 28.7 %collective-permute-start.51 = (bf16[128,1536]{1,0:T(8,128)(2,1)S(1)}, bf16[128,1536]{1,0:T(8,128)(2,1)S(1)}, u32[]{:S(2)}, u32[]{:S(2)}) collective-permute-start(bf16[128,1536]{1,0:T(8,128)(2,1)S(1)} %collective-permute-done.49.refs_1_), channel_id=1, source_target_pairs={{0,1},{1,0},{2,3},{3,2},{4,5},{5,4},{6,7},{7,6},{8,9},{9,8},{10,11... | collective-permute-start | bytes 1179656 | tf_op jit(solution)/shard_map/ppermute | solution.py:669
  380.4 11.2 %collective-permute-start.55 = (f32[62,256]{1,0:T(8,128)S(1)}, f32[62,256]{1,0:T(8,128)S(1)}, u32[]{:S(2)}, u32[]{:S(2)}) collective-permute-start(f32[62,256]{1,0:T(8,128)S(1)} %fusion.101), channel_id=1, source_target_pairs={{0,2},{2,0},{4,6},{6,4},{1,3},{3,1},{5,7},{7,5},{8,10},{10,8},{12,... | collective-permute-start | bytes 190472 | tf_op jit(solution)/shard_map/ppermute | solution.py:669
  391.7 10.5 %collective-permute-start.62 = (bf16[2,96,768]{2,1,0:T(8,128)(2,1)S(1)}, bf16[2,96,768]{2,1,0:T(8,128)(2,1)S(1)}, u32[]{:S(2)}, u32[]{:S(2)}) collective-permute-start(bf16[2,96,768]{2,1,0:T(8,128)(2,1)S(1)} %fusion.78), channel_id=1, source_target_pairs={{0,16},{16,0},{1,17},{17,1},{2,18},{18,2},{3,19},{19,3},{4,20},{20... | collective-permute-start | bytes 884744 | tf_op jit(solution)/shard_map/ppermute | solution.py:669
  392.8 7.1 %collective-permute-start.56 = (f32[62,256]{1,0:T(8,128)S(1)}, f32[62,256]{1,0:T(8,128)S(1)}, u32[]{:S(2)}, u32[]{:S(2)}) collective-permute-start(f32[62,256]{1,0:T(8,128)S(1)} %add.557), channel_id=1, source_target_pairs={{0,4},{2,6},{4,0},{6,2},{1,5},{3,7},{5,1},{7,3},{8,12},{10,14},{12... | collective-permute-start | bytes 190472 | tf_op jit(solution)/shard_map/ppermute | solution.py:669
  399.8 12.5 %collective-permute-start.59 = (bf16[2,96,1024]{2,1,0:T(8,128)(2,1)}, bf16[2,96,1024]{2,1,0:T(8,128)(2,1)}, u32[]{:S(2)}, u32[]{:S(2)}) collective-permute-start(bf16[2,96,1024]{2,1,0:T(8,128)(2,1)} %fusion.72), channel_id=1, source_target_pairs={{0,2},{2,0},{4,6},{6,4},{1,3},{3,1},{5,7},{7,5},{8,10},{10,8},{12,... | collective-permute-start | bytes 1179656 | tf_op jit(solution)/shard_map/ppermute | solution.py:669
  403.5 6.6 %collective-permute-start.63 = (f32[96,768]{0,1:T(8,128)S(1)}, f32[96,768]{0,1:T(8,128)}, u32[]{:S(2)}, u32[]{:S(2)}) collective-permute-start(f32[96,768]{0,1:T(8,128)S(1)} %bitcast.225), channel_id=1, source_target_pairs={{0,8},{8,0},{1,9},{9,1},{2,10},{10,2},{3,11},{11,3},{4,12},{12,4},... | collective-permute-start | bytes 884744 | tf_op jit(solution)/shard_map/ppermute | solution.py:669
  414.6 4.0 collective-permute-start.60
  421.6 5.5 %collective-permute-start.61 = (f32[96,256]{0,1:T(8,128)S(1)}, f32[96,256]{0,1:T(8,128)S(1)}, u32[]{:S(2)}, u32[]{:S(2)}) collective-permute-start(f32[96,256]{0,1:T(8,128)S(1)} %pad_maximum_fusion.11), channel_id=1, source_target_pairs={{0,1},{1,0},{2,3},{3,2},{4,5},{5,4},{6,7},{7,6},{8,9},{9,8},{10,11... | collective-permute-start | bytes 294920 | tf_op jit(solution)/shard_map/ppermute | solution.py:669
  (86 other events, 785.1 us)

commit v3 on v2

--- a/solution.py
+++ b/solution.py
@@ -332,7 +332,8 @@
 
 BF = jnp.bfloat16
 F32 = jnp.float32
-CHUNK = 128
+CHUNK = 256
+HALF = 128
 VMEM = 40 * 1024 * 1024
 
 
@@ -372,11 +373,19 @@
     return jnp.maximum(x, 0.0) + jnp.log1p(jnp.exp(-jnp.abs(x)))
 
 
-def taps_applied(extended, taps):
+def taps_applied(x, before, taps, moved):
+    moved[:8, :] = before
+    moved[8:, :] = x
     total = taps[CONV : CONV + 1, :]
-    for k in range(CONV):
-        total = total + extended[5 + k : 5 + k + CHUNK] * taps[k : k + 1, :]
-    return total
+    for k in range(CONV - 1):
+        total = total + moved[5 + k : 5 + k + CHUNK, :] * taps[k : k + 1, :]
+    return total + x * taps[CONV - 1 : CONV, :]
+
+
+def summed_by(ones, x):
+    top, rest = halves(x)
+    low = x - top.astype(F32) - rest.astype(F32)
+    return folded(mm(ones, beside((top, rest)))) + mm(ones, low.astype(BF))
 
 
 def square(which):
@@ -387,8 +396,7 @@
     shifted_pre = step_ref[...] + bias_ref[...]
     step = softplus(shifted_pre)
     rates = jnp.exp(log_decay_ref[...])
-    lower = jnp.where(square(0) >= square(1), 1.0, 0.0).astype(F32)
-    cum = jnp.dot(lower, -step * rates, precision=HIGH, preferred_element_type=F32)
+    cum = summed_by(jnp.where(square(0) >= square(1), 1.0, 0.0).astype(BF), -step * rates)
     return shifted_pre, step, rates, cum
 
 
@@ -399,7 +407,7 @@
 
 def forward_kernel(
     vpre, spre, spre_step, vtaps, staps, bias, log_decay, skip,
-    mixer, starts, vtotal, stotal, state, vtail, stail,
+    mixer, starts, values, vslope, states_ref, sslope, state, vtail, stail, vmoved, smoved,
 ):
     @pl.when(pl.program_id(0) == 0)
     def _():
@@ -408,16 +416,18 @@
         stail[...] = jnp.zeros_like(stail)
 
     sx = spre[...]
-    total = taps_applied(jnp.concatenate([stail[...], sx], axis=0), staps[...])
-    stotal[...] = total
-    states = jax.nn.silu(total)
+    total = taps_applied(sx, stail[...], staps[...], smoved)
+    sigmoid = jax.nn.sigmoid(total)
+    states = total * sigmoid
+    states_ref[...] = states
+    sslope[...] = sigmoid * (1.0 + total * (1.0 - sigmoid))
     stail[...] = sx[CHUNK - 8 :]
     b, c = states[:, :STATE], states[:, STATE:]
     shifted_pre, step, rates, cum = step_terms(spre_step, bias, log_decay)
     cum_t = cum.T
     final = cum[CHUNK - 1 :, :]
     grown, ending, whole = jnp.exp(cum), jnp.exp(final - cum), jnp.exp(final)
-    c_left, bt_left = beside(halves(c)), beside(halves(b.T))
+    c_left, bt2 = beside(halves(c)), halves(b.T)
     scores = folded(mm_nt(c_left, right_side_nt(halves(b))))
     scores = jnp.where(square(0) >= square(1), scores, 0.0)
     left = lax.broadcasted_iota(jnp.int32, (1, 128), 1) < 64
@@ -425,21 +435,37 @@
     for p in range(vpre.shape[1] // 128):
         lanes = slice(128 * p, 128 * p + 128)
         vx = vpre[:, lanes]
-        total = taps_applied(jnp.concatenate([vtail[:, lanes], vx], axis=0), vtaps[:, lanes])
-        vtotal[:, lanes] = total
+        total = taps_applied(vx, vtail[:, lanes], vtaps[:, lanes], vmoved.at[p])
         vtail[:, lanes] = vx[CHUNK - 8 :]
-        v = jax.nn.silu(total)
+        sigmoid = jax.nn.sigmoid(total)
+        v = total * sigmoid
+        values[:, lanes] = v
+        vslope[:, lanes] = sigmoid * (1.0 + total * (1.0 - sigmoid))
         weighted = v * by_pair(step, p)
-        right = right_side(halves(weighted))
-        parts = []
+        w2 = halves(weighted)
+        early, late = [], []
         for h in (2 * p, 2 * p + 1):
-            decay = jnp.exp(jnp.minimum(cum[:, h : h + 1] - cum_t[h : h + 1, :], 0.0))
-            parts.append(folded(mm(beside(halves(decay * scores)), right)))
+            gap = cum[:HALF, h : h + 1] - cum_t[h : h + 1, :HALF]
+            early.append(jnp.exp(jnp.minimum(gap, 0.0)) * scores[:HALF, :HALF])
+            gap = cum[HALF:, h : h + 1] - cum_t[h : h + 1, :]
+            late.append(jnp.exp(jnp.minimum(gap, 0.0)) * scores[HALF:, :])
+        early = beside(halves(jnp.concatenate(early, axis=0)))
+        early = folded(mm(early, right_side((w2[0][:HALF], w2[1][:HALF]))))
+        late = halves(jnp.concatenate(late, axis=0))
+        late = folded(mm(late[0], beside(w2))) + mm(late[1], w2[0])
+        within = jnp.concatenate(
+            [
+                jnp.where(left, early[:HALF], early[HALF:]),
+                jnp.where(left, late[:HALF], late[HALF:]),
+            ],
+            axis=0,
+        )
         held = state[:, lanes]
         carried = by_pair(grown, p) * folded(mm(c_left, right_side(halves(held))))
-        mixer[:, lanes] = jnp.where(left, parts[0], parts[1]) + carried + skip[:, lanes] * v
-        entering_here = right_side(halves(weighted * by_pair(ending, p)))
-        state[:, lanes] = held * by_pair(whole, p) + folded(mm(bt_left, entering_here))
+        mixer[:, lanes] = within + carried + skip[:, lanes] * v
+        ends = halves(weighted * by_pair(ending, p))
+        added = folded(mm(bt2[0], beside(ends))) + mm(bt2[1], ends[0])
+        state[:, lanes] = held * by_pair(whole, p) + added
 
 
 def forward_scan(vpre, spre, step_pre, vtaps, staps, bias, log_decay, skip):
@@ -453,18 +479,23 @@
         in_specs=[row(width), row(2 * STATE), row(128)]
         + [fixed(x) for x in (vtaps, staps, bias, log_decay, skip)],
         out_specs=[
-            row(width), pl.BlockSpec((1, STATE, width), lambda i: (i, 0, 0)), row(width), row(2 * STATE)
+            row(width), pl.BlockSpec((1, STATE, width), lambda i: (i, 0, 0)),
+            row(width), row(width), row(2 * STATE), row(2 * STATE),
         ],
         out_shape=[
             jax.ShapeDtypeStruct((tokens, width), F32),
             jax.ShapeDtypeStruct((chunks, STATE, width), F32),
             jax.ShapeDtypeStruct((tokens, width), F32),
+            jax.ShapeDtypeStruct((tokens, width), F32),
+            jax.ShapeDtypeStruct((tokens, 2 * STATE), F32),
             jax.ShapeDtypeStruct((tokens, 2 * STATE), F32),
         ],
         scratch_shapes=[
             pltpu.VMEM((STATE, width), F32),
             pltpu.VMEM((8, width), F32),
             pltpu.VMEM((8, 2 * STATE), F32),
+            pltpu.VMEM((width // 128, CHUNK + 8, 128), F32),
+            pltpu.VMEM((CHUNK + 8, 2 * STATE), F32),
         ],
         compiler_params=pltpu.CompilerParams(vmem_limit_bytes=VMEM),
         cost_estimate=pl.CostEstimate(
@@ -476,110 +507,128 @@
     )(vpre, spre, step_pre, vtaps, staps, bias, log_decay, skip)
 
 
-def taps_back(d_total, later, x, taps):
-    extended = jnp.concatenate([d_total, later], axis=0)
-    d_x, rows = 0.0, []
-    for k in range(CONV):
-        moved = extended[3 - k : 3 - k + CHUNK]
-        d_x = d_x + moved * taps[k : k + 1, :]
-        rows.append(jnp.sum(moved * x, axis=0, keepdims=True))
+def taps_back(d_total, later, x, taps, moved):
+    moved[:CHUNK, :] = d_total
+    moved[CHUNK:, :] = later
+    d_x = d_total * taps[CONV - 1 : CONV, :]
+    rows = []
+    for k in range(CONV - 1):
+        later_rows = moved[3 - k : 3 - k + CHUNK, :]
+        d_x = d_x + later_rows * taps[k : k + 1, :]
+        rows.append(jnp.sum(later_rows * x, axis=0, keepdims=True))
+    rows.append(jnp.sum(d_total * x, axis=0, keepdims=True))
     return d_x, rows + [jnp.sum(d_total, axis=0, keepdims=True)]
 
 
 def backward_kernel(
-    vpre, vtotal, spre, stotal, spre_step, vtaps, staps, bias, log_decay, skip, chooser,
+    vpre, values, vslope, spre, states_ref, sslope, spre_step, vtaps, staps, bias, log_decay, skip, chooser,
     mixer, d_mixer, starts,
     values_low, d_spre, step_low, value_sums, state_sums, step_sums,
-    later_grad, later_state, vhead, shead,
+    later_grad, later_state, vhead, shead, vmoved, smoved,
 ):
     @pl.when(pl.program_id(0) == 0)
     def _():
         for ref in (later_grad, later_state, vhead, shead, value_sums, state_sums, step_sums):
             ref[...] = jnp.zeros_like(ref)
 
-    stot = stotal[...]
-    s_sigmoid = jax.nn.sigmoid(stot)
-    states = stot * s_sigmoid
+    states = states_ref[...]
     b, c = states[:, :STATE], states[:, STATE:]
     shifted_pre, step, rates, cum = step_terms(spre_step, bias, log_decay)
     cum_t = cum.T
     final = cum[CHUNK - 1 :, :]
     grown, ending, whole = jnp.exp(cum), jnp.exp(final - cum), jnp.exp(final)
     b2, c2 = halves(b), halves(c)
-    b_left, ct_left = beside(b2), beside(halves(c.T))
+    b_left, ct2 = beside(b2), halves(c.T)
     causal = square(1) >= square(0)
     scores_t = jnp.where(causal, folded(mm_nt(b_left, right_side_nt(c2))), 0.0)
     left = lax.broadcasted_iota(jnp.int32, (1, 128), 1) < 64
     zero = jnp.zeros((CHUNK, 128), BF)
-    d_scores_t = jnp.zeros((CHUNK, CHUNK), F32)
+    d_early = jnp.zeros((HALF, CHUNK), F32)
+    d_late = jnp.zeros((HALF, HALF), F32)
     d_b = jnp.zeros((CHUNK, STATE), F32)
     d_c = jnp.zeros((CHUNK, STATE), F32)
-    reached = jnp.zeros((CHUNK, 128), F32)
-    pulled = jnp.zeros((CHUNK, 128), F32)
+    by_head = jnp.zeros((2 * CHUNK, 128), F32)
     at_end = jnp.zeros((8, 128), F32)
     for p in range(vpre.shape[1] // 128):
         lanes = slice(128 * p, 128 * p + 128)
         pick = chooser[256 * p : 256 * p + 256, :]
-        total, dy = vtotal[:, lanes], d_mixer[:, lanes]
-        sigmoid = jax.nn.sigmoid(total)
-        v = total * sigmoid
+        v, dy = values[:, lanes], d_mixer[:, lanes]
         steps = by_pair(step, p)
         weighted = v * steps
         w2, d2 = halves(weighted), halves(dy)
-        d_right = right_side(d2)
         w_rest = pltpu.roll(weighted - w2[0].astype(F32), 64, 1).astype(BF)
         d_top = pltpu.roll(d2[0].astype(F32), 64, 1).astype(BF)
-        parts = []
+        early, late = [], []
         for h, mine in ((2 * p, left), (2 * p + 1, ~left)):
-            decay = jnp.exp(jnp.minimum(cum_t[h : h + 1, :] - cum[:, h : h + 1], 0.0))
-            parts.append(folded(mm(beside(halves(decay * scores_t)), d_right)))
+            gap = cum_t[h : h + 1, :] - cum[:HALF, h : h + 1]
+            decay_early = jnp.exp(jnp.minimum(gap, 0.0))
+            gap = cum_t[h : h + 1, HALF:] - cum[HALF:, h : h + 1]
+            decay_late = jnp.exp(jnp.minimum(gap, 0.0))
+            early.append(decay_early * scores_t[:HALF, :])
+            late.append(decay_late * scores_t[HALF:, HALF:])
             one = beside((jnp.where(mine, w2[0], w_rest), jnp.where(mine, w2[0], zero)))
             other = beside((jnp.where(mine, d2[0], d_top), jnp.where(mine, d2[1], zero)))
-            d_scores_t = d_scores_t + mm_nt(one, other) * decay
+            d_mix = mm_nt(one, other)
+            d_early = d_early + d_mix[:HALF, :] * decay_early
+            d_late = d_late + d_mix[HALF:, HALF:] * decay_late
+        early = halves(jnp.concatenate(early, axis=0))
+        early = folded(mm(early[0], beside(d2))) + mm(early[1], d2[0])
+        late = beside(halves(jnp.concatenate(late, axis=0)))
+        late = folded(mm(late, right_side((d2[0][HALF:], d2[1][HALF:]))))
+        within = jnp.concatenate(
+            [
+                jnp.where(left, early[:HALF], early[HALF:]),
+                jnp.where(left, late[:HALF], late[HALF:]),
+            ],
+            axis=0,
+        )
         held, after_here = starts[0, :, lanes], later_grad[:, lanes]
         after2 = halves(after_here)
         ends = by_pair(ending, p)
-        d_weighted = jnp.where(left, parts[0], parts[1]) + ends * folded(
-            mm(b_left, right_side(after2))
-        )
+        d_weighted = within + ends * folded(mm(b_left, right_side(after2)))
         gain = skip[:, lanes]
-        reached = reached + mm(beside(halves(dy * (mixer[:, lanes] - gain * v))), pick)
-        pulled = pulled + mm(beside(halves(v * d_weighted)), pick)
+        both = jnp.concatenate([dy * (mixer[:, lanes] - gain * v), v * d_weighted], axis=0)
+        by_head = by_head + mm(beside(halves(both)), pick)
         ended = jnp.sum(after_here * later_state[:, lanes], axis=0, keepdims=True)
         at_end = at_end + mm(beside(halves(jnp.broadcast_to(ended, (8, 128)))), pick)
         faded = halves(by_pair(grown, p) * dy)
         d_c = d_c + folded(mm_nt(beside(faded), right_side_nt(halves(held))))
         d_b = d_b + folded(mm_nt(beside(halves(weighted * ends)), right_side_nt(after2)))
-        later_grad[:, lanes] = after_here * by_pair(whole, p) + folded(
-            mm(ct_left, right_side(faded))
-        )
-        d_total = (steps * d_weighted + gain * dy) * (sigmoid * (1.0 + total * (1.0 - sigmoid)))
-        d_x, rows = taps_back(d_total, vhead[:, lanes], vpre[:, lanes], vtaps[:, lanes])
+        added = folded(mm(ct2[0], beside(faded))) + mm(ct2[1], faded[0])
+        later_grad[:, lanes] = after_here * by_pair(whole, p) + added
+        d_total = (steps * d_weighted + gain * dy) * vslope[:, lanes]
+        d_x, rows = taps_back(
+            d_total, vhead[:, lanes], vpre[:, lanes], vtaps[:, lanes], vmoved.at[p]
+        )
         values_low[:, lanes] = d_x.astype(BF)
         rows += [jnp.sum(v * dy, axis=0, keepdims=True), jnp.zeros((2, 128), F32)]
         value_sums[:, lanes] += jnp.concatenate(rows, axis=0)
         vhead[:, lanes] = d_total[:8]
     later_state[...] = starts[0]
-    d_scores_t = jnp.where(causal, d_scores_t, 0.0)
-    d_b = d_b + folded(mm(beside(halves(d_scores_t)), right_side(c2)))
-    d_c = d_c + folded(mm(beside(halves(d_scores_t.T)), right_side(b2)))
+    d_late = jnp.concatenate([jnp.zeros((HALF, HALF), F32), d_late], axis=1)
+    d_scores_t = jnp.where(causal, jnp.concatenate([d_early, d_late], axis=0), 0.0)
+    top, rest = halves(d_scores_t)
+    d_b = d_b + folded(mm(top, beside(c2))) + mm(rest, c2[0])
+    top, rest = halves(d_scores_t.T)
+    d_c = d_c + folded(mm(top, beside(b2))) + mm(rest, b2[0])
+    reached, pulled = by_head[:CHUNK], by_head[CHUNK:]
     last = lax.broadcasted_iota(jnp.int32, (CHUNK, 128), 0) == CHUNK - 1
     d_cum = reached - step * pulled + jnp.where(last, at_end[:1], 0.0)
-    upper = jnp.where(causal, 1.0, 0.0).astype(F32)
-    d_rate = jnp.dot(upper, d_cum, precision=HIGH, preferred_element_type=F32)
+    d_rate = summed_by(jnp.where(causal, 1.0, 0.0).astype(BF), d_cum)
     d_shifted = (pulled - rates * d_rate) * jax.nn.sigmoid(shifted_pre)
     step_low[...] = d_shifted.astype(BF)
     step_sums[0:1, :] += jnp.sum(d_shifted, axis=0, keepdims=True)
     step_sums[1:2, :] -= jnp.sum(d_rate * step, axis=0, keepdims=True) * rates
-    d_total = beside((d_b, d_c)) * (s_sigmoid * (1.0 + stot * (1.0 - s_sigmoid)))
-    d_x, rows = taps_back(d_total, shead[...], spre[...], staps[...])
+    d_total = beside((d_b, d_c)) * sslope[...]
+    d_x, rows = taps_back(d_total, shead[...], spre[...], staps[...], smoved)
     d_spre[...] = d_x
     state_sums[...] += jnp.concatenate(rows + [jnp.zeros((3, 2 * STATE), F32)], axis=0)
     shead[...] = d_total[:8]
 
 
 def backward_scan(
-    vpre, vtotal, spre, stotal, step_pre, vtaps, staps, bias, log_decay, skip, mixer, d_mixer, starts
+    vpre, values, vslope, spre, states, sslope, step_pre, vtaps, staps, bias, log_decay, skip, mixer, d_mixer,
+    starts,
 ):
     tokens, width = vpre.shape
     chunks = tokens // CHUNK
@@ -592,7 +641,7 @@
     return pl.pallas_call(
         backward_kernel,
         grid=(chunks,),
-        in_specs=[row(width), row(width), row(2 * STATE), row(2 * STATE), row(128)]
+        in_specs=[row(width)] * 3 + [row(2 * STATE)] * 3 + [row(128)]
         + [fixed(x) for x in (vtaps, staps, bias, log_decay, skip, chooser)]
         + [row(width), row(width), pl.BlockSpec((1, STATE, width), lambda i: (chunks - 1 - i, 0, 0))],
         out_specs=[
@@ -611,6 +660,8 @@
             pltpu.VMEM((STATE, width), F32),
             pltpu.VMEM((8, width), F32),
             pltpu.VMEM((8, 2 * STATE), F32),
+            pltpu.VMEM((width // 128, CHUNK + 8, 128), F32),
+            pltpu.VMEM((CHUNK + 8, 2 * STATE), F32),
         ],
         compiler_params=pltpu.CompilerParams(vmem_limit_bytes=VMEM),
         cost_estimate=pl.CostEstimate(
@@ -620,7 +671,7 @@
         ),
         name="scan_backward",
     )(
-        vpre, vtotal, spre, stotal, step_pre, vtaps, staps, bias, log_decay, skip, chooser,
+        vpre, values, vslope, spre, states, sslope, step_pre, vtaps, staps, bias, log_decay, skip, chooser,
         mixer, d_mixer, starts,
     )
 
@@ -713,7 +764,7 @@
     tokens, n = lows[0].shape[0], weights[0][0].shape[0]
     groups = tokens // (4 * sub)
     split = [x.reshape(groups, 2, 2 * sub, x.shape[1]) for x in lows]
-    tile = 256
+    tile = n
     tiles = n // tile
     out = jax.ShapeDtypeStruct((tokens // 2, 2 * n), F32)
     first = lambda i, core: (jnp.minimum(i, tiles - 1), 0)
@@ -763,12 +814,15 @@
             (c * nz + z, (z % 2) * nz + 2 * ((z // 2) ^ r) + c) for c in range(2) for z in range(nz)
         ]
 
-    def tokens_in(x, *earlier):
+    def tokens_in(x):
         rounds = []
         for r in range(2):
             piece = lax.dynamic_slice(x, ((zi // 2) ^ r, 0, yi * sub, 0), (1, 1, sub, d_model))
             rounds.append(lax.ppermute(piece.reshape(sub, d_model), ("core", "seq"), route(r)))
-        return ordered(zi // 2, after(rounds[0], *earlier), after(rounds[1], *earlier), 0)
+        return rounds
+
+    def in_order(rounds):
+        return turned_halves(ordered(zi // 2, *rounds, 0))
 
     def tokens_back(x):
         pieces = [part(x, (zi // 2) ^ r, sub, 0) for r in range(2)]
@@ -777,21 +831,21 @@
             for r, piece in enumerate(pieces)
         ]
 
-    def tokens_home(mine):
+    def tokens_home(mine, by_y):
         targets = [(2 * ((zi // 2) ^ r) + y) * sub for y in (yi, 1 - yi) for r in range(2)]
-        blocks = mine + [swap(x, "heads") for x in mine]
-        return place(blocks, sub, targets, 2 * group).reshape(block_input.shape)
-
-    def spread(x):
-        by_y = swap(x, "heads")
+        return place([mine, by_y], sub, targets, 2 * group).reshape(block_input.shape)
+
+    spread_targets = [
+        ((2 * k + c) * 2 + y) * sub
+        for y, c in ((yi, ci), (1 - yi, ci), (yi, 1 - ci), (1 - yi, 1 - ci))
+        for k in range(nz // 2)
+    ]
+
+    def spread(x, by_y=None):
+        by_y = swap(x, "heads") if by_y is None else by_y
         by_core = swap(x, "core")
         by_both = swap(by_y, "core")
-        targets = [
-            ((2 * k + c) * 2 + y) * sub
-            for y, c in ((yi, ci), (1 - yi, ci), (yi, 1 - ci), (1 - yi, 1 - ci))
-            for k in range(nz // 2)
-        ]
-        return place([x, by_y, by_core, by_both], sub, targets, tokens)
+        return place([x, by_y, by_core, by_both], sub, spread_targets, tokens)
 
     def of_core(x, core):
         return at(x.reshape(nz // 2, 2, 2 * sub, -1), core, 1).reshape(tokens // 2, -1)
@@ -830,17 +884,22 @@
     def over_x(kept, received):
         return (kept + received.astype(F32)).reshape(2, nz, rows, -1)
 
-    def far_pieces(summed):
-        return part(summed, 1 - zi // 2, 2, summed.ndim - 3).astype(BF)
-
-    def near_sum(summed, received):
-        return part(summed, zi // 2, 2, summed.ndim - 3) + received.astype(F32)
-
-    def near_pieces(summed):
-        return at(summed, 1 - zi % 2, -3).astype(BF)
+    def by_parity(summed, which):
+        shape = summed.shape
+        split = summed.reshape(*shape[:-3], nz // 2, 2, *shape[-2:])
+        return at(split, which, split.ndim - 3)
+
+    def first_pieces(summed):
+        return by_parity(summed, 1 - zi % 2).astype(BF)
+
+    def first_sum(summed, received):
+        return by_parity(summed, zi % 2) + received.astype(F32)
+
+    def second_pieces(summed):
+        return at(summed, 1 - zi // 2, -3).astype(BF)
 
     def over_z(summed, received):
-        return at(summed, zi % 2, -3) + received.astype(F32)
+        return at(summed, zi // 2, -3) + received.astype(F32)
 
     def to_core(total):
         received = swap(at(total, 1 - ci, 0), "core")
@@ -873,7 +932,7 @@
     first_ring = ring(first_block, *first_across)
     first_across += [swap(x, "x") for x in first_ring[1:]]
 
-    x_own = turned_halves(tokens_in(after(block_input, first_block)))
+    x_own = in_order(tokens_in(block_input))
 
     pair_weight = after(
         jnp.concatenate(
@@ -885,8 +944,8 @@
     pair_block = block_of(pair_weight)
     pair_across = [swap(after(pair_block, first_across[0]), "x")]
     x_all = spread(after(x_own, *pair_across))
-    pair_ring = ring(after(pair_block, first_ring[3], first_across[1], first_across[2]))
-    pair_across += [swap(after(x, first_across[3]), "x") for x in pair_ring[1:]]
+    pair_ring = ring(after(pair_block, first_ring[3]))
+    pair_across += [swap(after(x, first_across[3]), "x") for x in pair_ring[1:3]] + [None]
 
     first_own = stacked(first_ring)
     first_other = stacked(first_across)
@@ -919,14 +978,19 @@
     bias, decays = lanes(step_bias), lanes(log_decay)
     skip = jnp.repeat(part(skip_gain, ci, heads, 0), cols // heads)[None]
     gain_mixer = part(mixer_gain, ci, cols, 0)[None]
-    values_pre, states_received, *pair_across[1:3], pair_ring[3] = lax.optimization_barrier(
-        (values_pre, states_received, *pair_across[1:3], pair_ring[3])
-    )
-    mixer, starts, values_total, states_total = forward_scan(
+    og_rounds = tokens_in(after(output_grad, pair_ring[1], pair_ring[2]))
+    values_pre, states_received, *pair_across[1:3], pair_ring[3], og_rounds = lax.optimization_barrier(
+        (values_pre, states_received, *pair_across[1:3], pair_ring[3], og_rounds)
+    )
+    og_own = in_order(og_rounds)
+    og_own, values_pre = lax.optimization_barrier((og_own, values_pre))
+    mixer, starts, *kept = forward_scan(
         values_pre, states_pre, step_pre, vtaps, state_taps, bias, decays, skip
     )
-    og_own = turned_halves(tokens_in(after(output_grad, pair_ring[1], pair_ring[2]), mixer))
-    og = spread(og_own)
+    pair_across[3], og_by_y, mixer = lax.optimization_barrier(
+        (swap(pair_ring[3], "x"), swap(og_own, "heads"), mixer)
+    )
+    og = spread(og_own, og_by_y)
     pair_own = stacked(pair_ring)
     pair_other = stacked(pair_across)
     gate_own, out_own = pair_own[:, :cols], pair_own[:, cols:]
@@ -947,26 +1011,30 @@
     gate_low = (d_gated * mixer * sigmoid_gate * (1.0 + gate_lin * (1.0 - sigmoid_gate))).astype(BF)
     g_mixer_gain = jnp.sum(d_out * gated * inverse, axis=0)
 
-    branch_sends, branch_keeps = paired_products([out_normed], [(out_own, out_other)], ci, sub)
-    then = after(out_normed, branch_sends)
-    out_sum = jnp.stack([transposed(og[:, :half], then), transposed(og[:, half:], then)])
-    out_sum = out_sum.reshape(2, 2, nz, rows, cols)
-    out_pieces = far_pieces(out_sum)
-    gate_sends, gate_keeps = products(after(gate_low, out_pieces), normed)
+    out_sum = jnp.stack(
+        [transposed(og[:, :half], out_normed), transposed(og[:, half:], out_normed)]
+    ).reshape(2, 2, nz, rows, cols)
+    out_pieces = first_pieces(out_sum)
+    branch_sends, branch_keeps = paired_products(
+        [after(out_normed, out_pieces)], [(out_own, out_other)], ci, sub
+    )
+    gate_sends, gate_keeps = products(after(gate_low, branch_sends), normed)
     branch_stays, branch_goes = over_core(branch_sends, branch_keeps)
     d_mixer = after(d_mixer, out_pieces, gate_sends, branch_goes)
     scanned = backward_scan(
-        values_pre, values_total, states_pre, states_total, step_pre, vtaps, state_taps, bias, decays, skip,
+        values_pre, *kept[:2], states_pre, *kept[2:], step_pre, vtaps, state_taps, bias, decays, skip,
         mixer, d_mixer, starts,
     )
-    sent = (swap(out_pieces, "seq", 2), swap(gate_sends, "x"), swap(branch_goes, "heads"))
+    sent = (swap(out_pieces, "seq", 1), swap(gate_sends, "x"), swap(branch_goes, "heads"))
     sent, scanned = lax.optimization_barrier((sent, scanned))
     out_received, gate_received, branch_received = sent
     values_low, d_states, step_low, value_sums, state_sums, step_sums = scanned
 
-    value_sends, value_keeps = products(values_low, normed)
-    gate_sum = over_x(after(gate_keeps, value_sends), gate_received)
-    gate_pieces = far_pieces(gate_sum)
+    out_sum = first_sum(out_sum, out_received)
+    out_pieces = second_pieces(out_sum)
+    gate_sum = over_x(gate_keeps, gate_received)
+    gate_pieces = first_pieces(gate_sum)
+    value_sends, value_keeps = products(after(values_low, out_pieces, gate_pieces), normed)
     d_states = after(d_states, gate_pieces)
     states_stay, states_go = over_core(of_core(d_states, 1 - ci), of_core(d_states, ci), F32)
     dn_sends, dn_keeps = paired_products(
@@ -975,80 +1043,96 @@
         ci,
         sub,
     )
-    out_sum = near_sum(out_sum, after(out_received, dn_sends))
-    out_pieces = near_pieces(out_sum)
+    states_low = over_y(states_stay, swap(states_go, "heads")).astype(BF)
+    dn_sends = after(dn_sends, states_low)
+    states_by_y = swap(states_low, "heads")
+    states_by_core = swap(after(states_low, states_by_y), "core")
+    states_by_both = swap(after(states_by_y, states_by_core), "core")
+    states_all = place(
+        [x.astype(F32) for x in (states_low, states_by_y, states_by_core, states_by_both)],
+        sub,
+        spread_targets,
+        tokens,
+    ).astype(BF)
+    parts = [
+        products(part(states_all, ci, STATE, 1), normed),
+        products(step_low, normed),
+    ]
+    small_sends, small_keeps = (jnp.concatenate(p, axis=1) for p in zip(*parts, strict=True))
     branch = over_y(branch_stays, after(branch_received, dn_sends))
     output_rows = turned_halves((x_own + branch).astype(BF))
     (
-        value_received, gate_received, states_received_y, dn_received, dn_keeps, out_pieces, output_rows
+        value_received, gate_received, small_sends, dn_received, dn_keeps, out_received, output_rows
     ) = lax.optimization_barrier(
         (
-            swap(value_sends, "x"), swap(gate_pieces, "seq", 2), swap(states_go, "heads"),
-            swap(dn_sends, "core"), dn_keeps, out_pieces, output_rows,
+            swap(value_sends, "x"), swap(gate_pieces, "seq", 1), small_sends,
+            swap(dn_sends, "core"), dn_keeps, swap(out_pieces, "seq", 2), output_rows,
         )
     )
 
     dn_stays, dn_goes = core_sum(dn_received, dn_keeps)
     output_sent = tokens_back(output_rows)
-    gate_sum = near_sum(gate_sum, gate_received)
-    gate_pieces = near_pieces(gate_sum)
-    states_low = over_y(states_stay, states_received_y).astype(BF)
+    gate_sum = first_sum(after(gate_sum, dn_goes), gate_received)
+    gate_pieces = second_pieces(gate_sum)
+    value_sum = over_x(after(value_keeps, dn_goes), value_received)
+    value_pieces = first_pieces(value_sum)
     states_weights = ordered(ci, states_weights, states_received, 1)
-    states_both = swap(states_low, "core").reshape(nz // 2, sub, -1), states_low.reshape(nz // 2, sub, -1)
-    states_both = [part(x, ci, STATE, 2) for x in states_both]
-    of_y = at(after(normed, dn_goes).reshape(nz // 2, 2, 2, sub, d_model), yi, 2)
-    states_both = jnp.stack(
-        [jnp.where(ci == k, states_both[1], states_both[0]) for k in range(2)], axis=1
-    ).reshape(tokens // 2, STATE)
-    parts = [
-        products(states_both, of_y.reshape(tokens // 2, d_model)),
-        products(after(step_low, dn_goes), normed),
-    ]
-    small_sends, small_keeps = (jnp.concatenate(p, axis=1) for p in zip(*parts, strict=True))
-    value_sum = over_x(value_keeps, value_received)
-    (
-        dn_received, output_sent, gate_received, small_received, out_pieces, value_sum
-    ) = lax.optimization_barrier(
+    dn_received, output_sent, value_received, small_received = lax.optimization_barrier(
         (
-            swap(dn_goes, "heads"), output_sent, swap(gate_pieces, "seq", 1), swap(small_sends, "x"),
-            out_pieces, value_sum,
-        )
-    )
-
-    value_sum = jnp.concatenate([value_sum, over_x(small_keeps, small_received)], axis=-1)
-    value_pieces = far_pieces(value_sum)
-    d_normed = over_y(dn_stays, after(dn_received, value_pieces)) + back(states_low, states_weights)
+            swap(dn_goes, "heads"), output_sent, swap(value_pieces, "seq", 1), swap(small_sends, "x"),
+        )
+    )
+
+    d_normed = over_y(dn_stays, dn_received) + back(states_low, states_weights)
     pushed = d_normed * gain
     d_tokens = scaling * pushed - x_own * (scaling * scaling * scaling) * jnp.mean(
         pushed * x_own, axis=-1, keepdims=True
     )
     input_rows = turned_halves((og_own.astype(F32) + d_tokens).astype(BF))
-    block_output = tokens_home(output_sent)
-    g_gate = over_z(gate_sum, gate_received)
-    out_sum = over_z(out_sum, swap(out_pieces, "seq", 1))
-    out_sum, input_sent = lax.optimization_barrier((out_sum, tokens_back(input_rows)))
-
-    grad_input = tokens_home(input_sent)
-    g_out = out_sum[0] + swap(out_sum[1].astype(BF), "x").astype(F32)
-    value_sum = near_sum(value_sum, after(swap(value_pieces, "seq", 2), *input_sent))
-    g_value = over_z(value_sum, swap(near_pieces(value_sum), "seq", 1))
     g_input_gain = turned_halves(jnp.sum(d_normed * x_own * scaling, axis=0)[None])
-
     per_core = jnp.concatenate(
         [value_sums[:6], g_mixer_gain[None], jnp.pad(step_sums[:2].reshape(1, -1), ((0, 0), (0, cols - 256)))],
         axis=0,
     ).reshape(-1, 256)
     shared = jnp.concatenate([state_sums, g_input_gain.reshape(-1, 256)], axis=0)
-    shared = after(shared, *input_sent)
     shared = shared + swap(shared, "heads")
     received = swap(jnp.concatenate([per_core, shared], axis=0), "core")
     n_core = per_core.shape[0]
     pack = jnp.concatenate(
         [ordered(ci, per_core, received[:n_core], 0), shared + received[n_core:]], axis=0
     )
+    output_sent = jnp.concatenate(after(output_sent, shared), axis=0)
+    small_sum = over_x(small_keeps, after(small_received, input_rows))
+    small_sum = first_sum(small_sum, swap(first_pieces(small_sum), "seq", 1))
+    small_pieces = second_pieces(small_sum)
+    input_sent, output_by_y, gate_received, small_pieces, pack = lax.optimization_barrier(
+        (
+            tokens_back(input_rows), swap(output_sent, "heads"), swap(gate_pieces, "seq", 2),
+            small_pieces, pack,
+        )
+    )
+
+    input_sent = jnp.concatenate(input_sent, axis=0)
+    value_sum = first_sum(value_sum, value_received)
+    value_pieces = second_pieces(value_sum)
+    g_out = over_z(out_sum, out_received)
     pack = pack + swap(pack, "x")
+    g_out = g_out[0] + swap(g_out[1].astype(BF), "x").astype(F32)
+    out_mine, out_received = to_core(g_out)
+    input_by_y, value_received, small_received, out_received, pack = lax.optimization_barrier(
+        (
+            swap(input_sent, "heads"), swap(value_pieces, "seq", 2), swap(small_pieces, "seq", 2),
+            out_received, pack,
+        )
+    )
     pack = pack + swap(pack, "seq", 1)
     pack = pack + swap(pack, "seq", 2)
+    g_gate = over_z(gate_sum, gate_received)
+    g_value = over_z(value_sum, value_received)
+    g_small = over_z(small_sum, small_received)
+    block_output = tokens_home(output_sent, output_by_y)
+    grad_input = tokens_home(input_sent, input_by_y)
+
     both, shared = pack[: 2 * n_core].reshape(2, 8, cols), pack[2 * n_core :]
     by_channel = jnp.transpose(both, (1, 0, 2)).reshape(8, 2 * cols)
     per_head = both[:, 7, :256].reshape(2, 2, 128)[:, :, :heads]
@@ -1058,19 +1142,17 @@
     def widths(mine, received):
         return ordered(ci, mine, received, 1)
 
-    value_mine, value_received = to_core(g_value)
-    states_at, steps_at = slice(cols, cols + STATE), slice(cols + STATE, cols + STATE + heads)
-    g_state = widths(value_mine[:, states_at], value_received[:, states_at])
-    g_state = g_state + swap(g_state, "heads")
+    small_mine, small_received = to_core(g_small)
+    steps_at = slice(STATE, STATE + heads)
     return (
         block_output,
         grad_input,
         my_gain,
         widths(*to_core(g_gate)),
-        widths(value_mine[:, :cols], value_received[:, :cols]),
-        g_state,
-        widths(value_mine[:, steps_at], value_received[:, steps_at]),
-        widths(*to_core(g_out)).T,
+        widths(*to_core(g_value)),
+        widths(small_mine[:, :STATE], small_received[:, :STATE]),
+        widths(small_mine[:, steps_at], small_received[:, steps_at]),
+        widths(out_mine, out_received).T,
         by_channel[:5],
         shared[:5],
         per_head[:, 0].reshape(-1),

time: 435 us -> 378 us (0.87)
  waiting for transfers between devices: 156 us -> 130 us
  starting transfers between devices: 83.3 us -> 73.5 us
  local copies, waits for them, and re-layouts: 42.2 us -> 32.6 us
  other arithmetic: 40.6 us -> 31.9 us
  Pallas kernels: 74.1 us -> 66.7 us
    ppermute x50 -> x52, waiting for transfers between devices: 99.4 us -> 41.8 us  [swap(): lax.ppermute(x, axis, [(i, i ^ bit) for i in range(lax.axis_size(axis))])]
    ppermute x4, waiting for transfers between devices: 15.2 us -> 32.9 us  [tokens_in(): lax.ppermute(piece.reshape(sub, d_model), ('core', 'seq'), route(r))]
    ppermute x4, waiting for transfers between devices: 14.3 us -> 26.1 us  [tokens_back(): lax.ppermute(piece, ('core', 'seq'), [(b, a) for a, b in route(r)])]
    ppermute x6, starting transfers between devices: 15 us -> 5.14 us  [turned(): return lax.ppermute(x, axis, [(i, (i + distance) % n) for i in range(n)])]
    pallas_call x1, Pallas kernels: 28.4 us -> 21.6 us  [backward_scan(): pl.pallas_call(backward_kernel, grid=(chunks,), in_specs=[row(width)] * 3...]
    unnamed x176 -> x170, local copies, waits for them, and re-layouts: 21.3 us -> 15.1 us
    ppermute x50 -> x52, starting transfers between devices: 52.2 us -> 49.9 us  [swap(): lax.ppermute(x, axis, [(i, i ^ bit) for i in range(lax.axis_size(axis))])]
    pallas_call x8 -> x9, Pallas kernels: 17.2 us -> 19.4 us  [place(): pl.pallas_call(kernel, grid_spec=pltpu.PrefetchScalarGridSpec(num_scalar_...]
  transfers between devices with their start and end apart: 64 -> 66, of which waited for: 26 -> 23; matrix products, arithmetic and copies ran while one was open for 16% -> 16% of each run, Pallas kernels for 14% -> 16%
where the time goes in v3:
time: 378 us; the launch traced here: 370 us
  waiting for transfers between devices  130 us (34%)
  starting transfers between devices  73.5 us (19%)
  Pallas kernels  66.7 us (18%)
  matrix products  32.8 us (9%)
  local copies, waits for them, and re-layouts  32.6 us (9%)
  other arithmetic  31.9 us (8%)
    ppermute x52, starting transfers between devices, swap(): lax.ppermute(x, axis, [(i, i ^ bit) for i in range(lax.axis_size(axis))])  49.9 us
    ppermute x52, waiting for transfers between devices, swap(): lax.ppermute(x, axis, [(i, i ^ bit) for i in range(lax.axis_size(axis))])  41.8 us
    ppermute x4, waiting for transfers between devices, tokens_in(): lax.ppermute(piece.reshape(sub, d_model), ('core', 'seq'), route(r))  32.9 us
    ppermute x6, waiting for transfers between devices, turned(): return lax.ppermute(x, axis, [(i, (i + distance) % n) for i in range(n)])  29.3 us
    ppermute x4, waiting for transfers between devices, tokens_back(): lax.ppermute(piece, ('core', 'seq'), [(b, a) for a, b in route(r)])  26.1 us
    pallas_call x1, Pallas kernels, backward_scan(): pl.pallas_call(backward_kernel, grid=(chunks,), in_specs=[row(width)] * 3...  21.6 us
    pallas_call x9, Pallas kernels, place(): pl.pallas_call(kernel, grid_spec=pltpu.PrefetchScalarGridSpec(num_scalar_...  19.4 us
    dot_general x10, matrix products, whole_sequences(): lax.dot_general(a, b, (((0,), (0,)), ((), ())), preferred_element_type=F32)  17.6 us
  transfers between devices with their start and end apart: 66, of which 23 were waited for; matrix products, arithmetic and copies ran while one was open for 16% of the time, Pallas kernels for 16%

profile of v3, /device:TPU:8, one launch (start us, length us, event | category | flops | bytes accessed | tf_op | source)
XLA Modules:
  0.0 370.5 jit_solution(2494418670824735321)
XLA Ops:
  8.3 1.9 collective-permute-start
  10.2 2.9 collective-permute-start.1
  13.1 2.7 collective-permute-start.10
  18.4 8.0 %collective-permute-done.4.refs_0_ = bf16[192,1024]{1,0:T(8,128)(2,1)S(1)} collective-permute-done((bf16[192,1024]{1,0:T(8,128)(2,1)S(1)}, bf16[192,1024]{1,0:T(8,128)(2,1)S(1)}, u32[]{:S(2)}, u32[]{:S(2)}) %collective-permute-start.4) | collective-permute-done | bytes 393248 | tf_op jit(solution)/shard_map/ppermute | solution.py:720
  27.9 10.2 %collective-permute-done.1 = bf16[128,1536]{1,0:T(8,128)(2,1)} collective-permute-done((bf16[128,1536]{1,0:T(8,128)(2,1)}, bf16[128,1536]{1,0:T(8,128)(2,1)}, u32[]{:S(2)}, u32[]{:S(2)}) %collective-permute-start.1) | collective-permute-done | bytes 393248 | tf_op jit(solution)/shard_map/ppermute | solution.py:821
  39.4 17.3 %collective-permute-done.10.refs_2_ = bf16[192,1024]{1,0:T(8,128)(2,1)S(1)} collective-permute-done((bf16[192,1024]{1,0:T(8,128)(2,1)S(1)}, bf16[192,1024]{1,0:T(8,128)(2,1)S(1)}, u32[]{:S(2)}, u32[]{:S(2)}) %collective-permute-start.10) | collective-permute-done | bytes 393248 | tf_op jit(solution)/shard_map/ppermute | solution.py:725
  60.7 8.2 %collective-permute-done.11.refs_3_ = bf16[192,1024]{1,0:T(8,128)(2,1)} collective-permute-done((bf16[192,1024]{1,0:T(8,128)(2,1)}, bf16[192,1024]{1,0:T(8,128)(2,1)}, u32[]{:S(2)}, u32[]{:S(2)}) %collective-permute-start.11) | collective-permute-done | bytes 393248 | tf_op jit(solution)/shard_map/ppermute | solution.py:725
  68.9 1.6 collective-permute-start.14
  71.3 2.7 place.10
  74.3 2.1 collective-permute-start.18
  76.4 3.8 %collective-permute-done.14.refs_3_ = bf16[192,1024]{1,0:T(8,128)(2,1)} collective-permute-done((bf16[192,1024]{1,0:T(8,128)(2,1)}, bf16[192,1024]{1,0:T(8,128)(2,1)}, u32[]{:S(2)}, u32[]{:S(2)}) %collective-permute-start.14) | collective-permute-done | bytes 393248 | tf_op jit(solution)/shard_map/ppermute | solution.py:720
  80.1 2.5 place.11
  83.7 3.7 %collective-permute-done.18.refs_2_ = bf16[192,1536]{1,0:T(8,128)(2,1)S(1)} collective-permute-done((bf16[192,1536]{1,0:T(8,128)(2,1)S(1)}, bf16[192,1536]{1,0:T(8,128)(2,1)S(1)}, u32[]{:S(2)}, u32[]{:S(2)}) %collective-permute-start.18) | collective-permute-done | bytes 589856 | tf_op jit(solution)/shard_map/ppermute | solution.py:725
  87.4 1.9 collective-permute-start.21
  90.2 1.6 collective-permute-start.17
  91.8 2.1 place.9
  97.5 4.2 %collective-permute-start.22 = (bf16[128,1536]{1,0:T(8,128)(2,1)S(1)}, bf16[128,1536]{1,0:T(8,128)(2,1)S(1)}, u32[]{:S(2)}, u32[]{:S(2)}) collective-permute-start(bf16[128,1536]{1,0:T(8,128)(2,1)S(1)} %get-tuple-element.261), channel_id=1, source_target_pairs={{0,4},{2,12},{4,0},{6,8},{8,6},{10,14},{12,2},{14,10},{1,5},{3,13}... | collective-permute-start | bytes 1179656 | tf_op jit(solution)/shard_map/ppermute | solution.py:821
  101.7 3.2 convolution_add_fusion.3.vpre
  104.9 22.8 %collective-permute-done.22 = bf16[128,1536]{1,0:T(8,128)(2,1)S(1)} collective-permute-done((bf16[128,1536]{1,0:T(8,128)(2,1)S(1)}, bf16[128,1536]{1,0:T(8,128)(2,1)S(1)}, u32[]{:S(2)}, u32[]{:S(2)}) %collective-permute-start.22) | collective-permute-done | bytes 393248 | tf_op jit(solution)/shard_map/ppermute | solution.py:821
  134.7 13.5 %scan_forward.1 = (f32[1024,768]{1,0:T(8,128)S(1)}, f32[4,128,768]{2,1,0:T(8,128)S(1)}, f32[1024,768]{1,0:T(8,128)S(1)}, f32[1024,768]{1,0:T(8,128)}, f32[1024,256]{1,0:T(8,128)S(1)}, /*index=5*/f32[1024,256]{1,0:T(8,128)S(1)}) custom-call(f32[1024,768]{1,0:T(8,128)} %convolution_add_fusion.3.vpre, f32[1024,256]{1,0:T(8,128)S(1)} %pad_maximum_fusion.spre, ...), custom_call_target="tpu_custom_call" | custom-call | flops 3221225472 | bytes 15728640 | tf_op jit(solution)/shard_map/scan_forward/pallas_call | solution.py:476
  148.2 1.6 copy-done.22
  151.9 1.6 place.14
  153.6 1.8 copy-done.30
  158.2 2.1 place.12
  161.8 3.3 multiply_reduce_fusion.2
  168.2 2.0 collective-permute-done.29
  170.2 4.2 %fusion.24 = (f32[1024,768]{1,0:T(8,128)}, bf16[1024,768]{1,0:T(8,128)(2,1)}, f32[768]{0:T(1024)S(1)}, bf16[1024,768]{1,0:T(8,128)(2,1)S(1)}) fusion(f32[1024]{0:T(1024)S(1)} %bitcast.260, f32[1024,768]{1,0:T(8,128)S(1)} %get-tuple-element.248, f32[1024,768]{1,0:T(8,128)S(1)} %copy-done.45, f32[1024]{0:T(1024)S(1)} %multiply_multiply_fusion, ...), kind=kLoop, calls=%fused_computation.52 | loop fusion | flops 18087168 | bytes 18892800 | tf_op jit(solution)/shard_map/mul | solution.py:1010
  179.2 4.3 %paired_products.2 = (f32[512,1536]{1,0:T(8,128)}, f32[512,1536]{1,0:T(8,128)S(1)}) custom-call(s32[1]{0:T(128)} %bitcast.35.core, bf16[2,2,256,768]{3,2,1,0:T(8,128)(2,1)S(1)} %bitcast.220, bf16[768,768]{1,0:T(8,128)(2,1)S(1)} %get-tuple-element.256.refs_1_, bf16[768,768]{1,0:T(8,128)(2,1)S(1)} %get-tuple-element.254.refs_2_), custom_call_target="tpu_custom_call" | custom-call | flops 1 | bytes 1 | tf_op jit(solution)/shard_map/paired_products/pallas_call | solution.py:772
  183.5 1.7 copy-done.7
  187.2 2.0 collective-permute-start.30
  189.3 2.5 convolution_convert_fusion.1
  191.8 1.6 collective-permute-start.31
  193.4 1.8 fusion.35
  196.9 21.6 %scan_backward.1 = (bf16[1024,768]{1,0:T(8,128)(2,1)S(1)}, f32[1024,256]{1,0:T(8,128)S(1)}, bf16[1024,128]{1,0:T(8,128)(2,1)S(1)}, f32[8,768]{1,0:T(8,128)S(1)},...) custom-call(f32[1024,768]{1,0:T(8,128)S(1)} %copy-done.6, f32[1024,768]{1,0:T(8,128)} %copy-done.22, ...), custom_call_target="tpu_custom_call" | custom-call | flops 8053063680 | bytes 18874368 | tf_op jit(solution)/shard_map/scan_backward/pallas_call | solution.py:641
  221.7 2.9 convert_add_fusion.2
  226.3 1.7 collective-permute-start.35
  230.0 2.5 convolution_convert_fusion
  232.4 1.6 collective-permute-start.34
  237.0 7.9 %paired_products.3 = (f32[512,1536]{1,0:T(8,128)}, f32[512,1536]{1,0:T(8,128)}) custom-call(s32[1]{0:T(128)} %bitcast.35.core, bf16[2,2,256,768]{3,2,1,0:T(8,128)(2,1)S(1)} %bitcast.219, bf16[2,2,256,768]{3,2,1,0:T(8,128)(2,1)S(1)} %bitcast.223, bf16[2,2,256,128]{3,2,1,0:T(8,128)(2,1)S(1)} %bitcast.225, bf16[768,768]{1,0:T(8,128)(2,1)S(1)} %copy-done.4, ...), custom_call_target="tpu_custom_call" | custom-call | flops 1 | bytes 1 | tf_op jit(solution)/shard_map/paired_products/pallas_call | solution.py:772
  245.2 3.0 fusion.57
  249.7 1.8 fusion.22
  251.7 2.3 collective-permute-done.38
  256.8 2.2 place.15
  262.0 1.6 fusion.36
  265.2 1.8 convert_add_fusion.1
  269.6 2.3 collective-permute-start.44
  271.9 2.4 collective-permute-start.45
  275.5 2.5 collective-permute-done.58
  280.0 11.9 %collective-permute-done.44 = bf16[128,1536]{1,0:T(8,128)(2,1)S(1)} collective-permute-done((bf16[128,1536]{1,0:T(8,128)(2,1)S(1)}, bf16[128,1536]{1,0:T(8,128)(2,1)S(1)}, u32[]{:S(2)}, u32[]{:S(2)}) %collective-permute-start.44) | collective-permute-done | bytes 393248 | tf_op jit(solution)/shard_map/ppermute | solution.py:830
  291.9 8.5 %collective-permute-start.52 = (bf16[2,96,768]{2,1,0:T(8,128)(2,1)}, bf16[2,96,768]{2,1,0:T(8,128)(2,1)}, u32[]{:S(2)}, u32[]{:S(2)}) collective-permute-start(bf16[2,96,768]{2,1,0:T(8,128)(2,1)} %fusion.50), channel_id=1, source_target_pairs={{0,4},{2,6},{4,0},{6,2},{1,5},{3,7},{5,1},{7,3},{8,12},{10,14},{12... | collective-permute-start | bytes 884744 | tf_op jit(solution)/shard_map/ppermute | solution.py:720
  301.4 1.8 fusion.20
  307.0 1.9 collective-permute-start.49
  313.5 6.9 %collective-permute-done.49 = bf16[128,1536]{1,0:T(8,128)(2,1)S(1)} collective-permute-done((bf16[128,1536]{1,0:T(8,128)(2,1)S(1)}, bf16[128,1536]{1,0:T(8,128)(2,1)S(1)}, u32[]{:S(2)}, u32[]{:S(2)}) %collective-permute-start.49) | collective-permute-done | bytes 393248 | tf_op jit(solution)/shard_map/ppermute | solution.py:830
  320.3 7.4 %collective-permute-done.50 = bf16[128,1536]{1,0:T(8,128)(2,1)S(1)} collective-permute-done((bf16[128,1536]{1,0:T(8,128)(2,1)S(1)}, bf16[128,1536]{1,0:T(8,128)(2,1)S(1)}, u32[]{:S(2)}, u32[]{:S(2)}) %collective-permute-start.50) | collective-permute-done | bytes 393248 | tf_op jit(solution)/shard_map/ppermute | solution.py:830
  327.7 3.1 collective-permute-done.51.refs_1_
  333.8 3.3 collective-permute-start.56
  337.1 2.5 place.16
  339.6 1.8 collective-permute-start.57
  342.4 9.1 %collective-permute-done.56 = bf16[2,96,768]{2,1,0:T(8,128)(2,1)S(1)} collective-permute-done((bf16[2,96,768]{2,1,0:T(8,128)(2,1)S(1)}, bf16[2,96,768]{2,1,0:T(8,128)(2,1)S(1)}, u32[]{:S(2)}, u32[]{:S(2)}) %collective-permute-start.56) | collective-permute-done | bytes 294944 | tf_op jit(solution)/shard_map/ppermute | solution.py:720
  351.5 2.1 collective-permute-done.57
  354.5 2.3 collective-permute-start.61
  357.6 2.5 place.17
  360.1 2.1 collective-permute-start.62
  363.6 1.8 collective-permute-done.62
  (425 shorter events, 93.1 us)
Async XLA Ops:
  4.4 1.6 collective-permute-start.2
  7.1 10.1 %collective-permute-start.3 = (bf16[96,1536]{1,0:T(8,128)(2,1)S(1)}, bf16[96,1536]{1,0:T(8,128)(2,1)}, u32[]{:S(2)}, u32[]{:S(2)}) collective-permute-start(bf16[96,1536]{1,0:T(8,128)(2,1)S(1)} %constant_dynamic-slice_fusion.8), channel_id=1, source_target_pairs={{0,8},{8,0},{1,9},{9,1},{2,10},{10,2},{3,11},{11,3},{4,12},{12,4},... | collective-permute-start | bytes 884744 | tf_op jit(solution)/shard_map/ppermute | solution.py:720
  8.3 19.7 %collective-permute-start = (bf16[128,1536]{1,0:T(8,128)(2,1)}, bf16[128,1536]{1,0:T(8,128)(2,1)}, u32[]{:S(2)}, u32[]{:S(2)}) collective-permute-start(bf16[128,1536]{1,0:T(8,128)(2,1)} %get-tuple-element.264), channel_id=1, source_target_pairs={{0,0},{2,8},{4,4},{6,12},{8,2},{10,10},{12,6},{14,14},{1,1},{3,9},... | collective-permute-start | bytes 1179656 | tf_op jit(solution)/shard_map/ppermute | solution.py:821
  10.2 27.9 %collective-permute-start.1 = (bf16[128,1536]{1,0:T(8,128)(2,1)}, bf16[128,1536]{1,0:T(8,128)(2,1)}, u32[]{:S(2)}, u32[]{:S(2)}) collective-permute-start(bf16[128,1536]{1,0:T(8,128)(2,1)} %get-tuple-element.263), channel_id=1, source_target_pairs={{0,4},{2,12},{4,0},{6,8},{8,6},{10,14},{12,2},{14,10},{1,5},{3,13}... | collective-permute-start | bytes 1179656 | tf_op jit(solution)/shard_map/ppermute | solution.py:821
  13.1 43.6 %collective-permute-start.10 = (bf16[192,1024]{1,0:T(8,128)(2,1)S(1)}, bf16[192,1024]{1,0:T(8,128)(2,1)S(1)}, u32[]{:S(2)}, u32[]{:S(2)}) collective-permute-start(bf16[192,1024]{1,0:T(8,128)(2,1)S(1)} %pad_maximum_fusion.7.refs_0_), channel_id=1, source_target_pairs={{0,6},{2,0},{4,2},{6,4},{1,7},{3,1},{5,3},{7,5},{8,14},{10,8},{12,... | collective-permute-start | bytes 1179656 | tf_op jit(solution)/shard_map/ppermute | solution.py:725
  15.8 10.7 %collective-permute-start.4 = (bf16[192,1024]{1,0:T(8,128)(2,1)S(1)}, bf16[192,1024]{1,0:T(8,128)(2,1)S(1)}, u32[]{:S(2)}, u32[]{:S(2)}) collective-permute-start(bf16[192,1024]{1,0:T(8,128)(2,1)S(1)} %pad_maximum_fusion.7.refs_0_), channel_id=1, source_target_pairs={{0,16},{16,0},{1,17},{17,1},{2,18},{18,2},{3,19},{19,3},{4,20},{20... | collective-permute-start | bytes 1179656 | tf_op jit(solution)/shard_map/ppermute | solution.py:720
  17.3 39.4 %collective-permute-start.9 = (bf16[192,1024]{1,0:T(8,128)(2,1)S(1)}, bf16[192,1024]{1,0:T(8,128)(2,1)}, u32[]{:S(2)}, u32[]{:S(2)}) collective-permute-start(bf16[192,1024]{1,0:T(8,128)(2,1)S(1)} %pad_maximum_fusion.7.refs_0_), channel_id=1, source_target_pairs={{0,2},{2,4},{4,6},{6,0},{1,3},{3,5},{5,7},{7,1},{8,10},{10,12},{12... | collective-permute-start | bytes 1179656 | tf_op jit(solution)/shard_map/ppermute | solution.py:725
  26.4 30.6 %collective-permute-start.5 = (bf16[192,1536]{1,0:T(8,128)(2,1)S(1)}, bf16[192,1536]{1,0:T(8,128)(2,1)S(1)}, u32[]{:S(2)}, u32[]{:S(2)}) collective-permute-start(bf16[192,1536]{1,0:T(8,128)(2,1)S(1)} %pad_maximum_fusion.4.refs_0_), channel_id=1, source_target_pairs={{0,16},{16,0},{1,17},{17,1},{2,18},{18,2},{3,19},{19,3},{4,20},{20... | collective-permute-start | bytes 1769480 | tf_op jit(solution)/shard_map/ppermute | solution.py:720
  56.7 12.2 %collective-permute-start.11 = (bf16[192,1024]{1,0:T(8,128)(2,1)}, bf16[192,1024]{1,0:T(8,128)(2,1)}, u32[]{:S(2)}, u32[]{:S(2)}) collective-permute-start(bf16[192,1024]{1,0:T(8,128)(2,1)} %collective-permute-done.9.refs_1_), channel_id=1, source_target_pairs={{0,2},{2,4},{4,6},{6,0},{1,3},{3,5},{5,7},{7,1},{8,10},{10,12},{12... | collective-permute-start | bytes 1179656 | tf_op jit(solution)/shard_map/ppermute | solution.py:725
  57.1 25.5 %collective-permute-start.6 = (bf16[256,1536]{1,0:T(8,128)(2,1)S(1)}, bf16[256,1536]{1,0:T(8,128)(2,1)}, u32[]{:S(2)}, u32[]{:S(2)}) collective-permute-start(bf16[256,1536]{1,0:T(8,128)(2,1)S(1)} %get-tuple-element.100.refs_0_), channel_id=1, source_target_pairs={{0,1},{1,0},{2,3},{3,2},{4,5},{5,4},{6,7},{7,6},{8,9},{9,8},{10,11... | collective-permute-start | bytes 2359304 | tf_op jit(solution)/shard_map/ppermute | solution.py:720
  58.7 15.6 %collective-permute-start.12 = (bf16[192,1024]{1,0:T(8,128)(2,1)}, bf16[192,1024]{1,0:T(8,128)(2,1)}, u32[]{:S(2)}, u32[]{:S(2)}) collective-permute-start(bf16[192,1024]{1,0:T(8,128)(2,1)} %collective-permute-done.9.refs_1_), channel_id=1, source_target_pairs={{0,16},{16,0},{1,17},{17,1},{2,18},{18,2},{3,19},{19,3},{4,20},{20... | collective-permute-start | bytes 1179656 | tf_op jit(solution)/shard_map/ppermute | solution.py:720
  60.2 16.2 %collective-permute-start.13 = (bf16[192,1024]{1,0:T(8,128)(2,1)S(1)}, bf16[192,1024]{1,0:T(8,128)(2,1)}, u32[]{:S(2)}, u32[]{:S(2)}) collective-permute-start(bf16[192,1024]{1,0:T(8,128)(2,1)S(1)} %collective-permute-done.10.refs_2_), channel_id=1, source_target_pairs={{0,16},{16,0},{1,17},{17,1},{2,18},{18,2},{3,19},{19,3},{4,20},{20... | collective-permute-start | bytes 1179656 | tf_op jit(solution)/shard_map/ppermute | solution.py:720
  68.9 11.2 %collective-permute-start.14 = (bf16[192,1024]{1,0:T(8,128)(2,1)}, bf16[192,1024]{1,0:T(8,128)(2,1)}, u32[]{:S(2)}, u32[]{:S(2)}) collective-permute-start(bf16[192,1024]{1,0:T(8,128)(2,1)} %collective-permute-done.11.refs_3_), channel_id=1, source_target_pairs={{0,16},{16,0},{1,17},{17,1},{2,18},{18,2},{3,19},{19,3},{4,20},{20... | collective-permute-start | bytes 1179656 | tf_op jit(solution)/shard_map/ppermute | solution.py:720
  71.2 12.4 %collective-permute-start.16 = (bf16[192,1536]{1,0:T(8,128)(2,1)S(1)}, bf16[192,1536]{1,0:T(8,128)(2,1)S(1)}, u32[]{:S(2)}, u32[]{:S(2)}) collective-permute-start(bf16[192,1536]{1,0:T(8,128)(2,1)S(1)} %pad_maximum_fusion.4.refs_0_), channel_id=1, source_target_pairs={{0,2},{2,4},{4,6},{6,0},{1,3},{3,5},{5,7},{7,1},{8,10},{10,12},{12... | collective-permute-start | bytes 1769480 | tf_op jit(solution)/shard_map/ppermute | solution.py:725
  74.3 13.1 %collective-permute-start.18 = (bf16[192,1536]{1,0:T(8,128)(2,1)S(1)}, bf16[192,1536]{1,0:T(8,128)(2,1)S(1)}, u32[]{:S(2)}, u32[]{:S(2)}) collective-permute-start(bf16[192,1536]{1,0:T(8,128)(2,1)S(1)} %pad_maximum_fusion.4.refs_0_), channel_id=1, source_target_pairs={{0,6},{2,0},{4,2},{6,4},{1,7},{3,1},{5,3},{7,5},{8,14},{10,8},{12,... | collective-permute-start | bytes 1769480 | tf_op jit(solution)/shard_map/ppermute | solution.py:725
  76.4 13.4 %collective-permute-start.7 = (bf16[256,1536]{1,0:T(8,128)(2,1)S(1)}, bf16[256,1536]{1,0:T(8,128)(2,1)S(1)}, u32[]{:S(2)}, u32[]{:S(2)}) collective-permute-start(bf16[256,1536]{1,0:T(8,128)(2,1)S(1)} %get-tuple-element.100.refs_0_), channel_id=1, source_target_pairs={{0,8},{8,0},{1,9},{9,1},{2,10},{10,2},{3,11},{11,3},{4,12},{12,4},... | collective-permute-start | bytes 2359304 | tf_op jit(solution)/shard_map/ppermute | solution.py:720
  82.6 7.6 %collective-permute-start.8 = (bf16[256,1536]{1,0:T(8,128)(2,1)}, bf16[256,1536]{1,0:T(8,128)(2,1)S(1)}, u32[]{:S(2)}, u32[]{:S(2)}) collective-permute-start(bf16[256,1536]{1,0:T(8,128)(2,1)} %collective-permute-done.6.refs_1_), channel_id=1, source_target_pairs={{0,8},{8,0},{1,9},{9,1},{2,10},{10,2},{3,11},{11,3},{4,12},{12,4},... | collective-permute-start | bytes 2359304 | tf_op jit(solution)/shard_map/ppermute | solution.py:720
  82.9 14.6 %collective-permute-start.15 = (bf16[1536,128]{1,0:T(8,128)(2,1)S(1)}, bf16[1536,128]{1,0:T(8,128)(2,1)S(1)}, u32[]{:S(2)}, u32[]{:S(2)}) collective-permute-start(bf16[1536,128]{1,0:T(8,128)(2,1)S(1)} %pad_maximum_fusion.8), channel_id=1, source_target_pairs={{0,8},{8,0},{1,9},{9,1},{2,10},{10,2},{3,11},{11,3},{4,12},{12,4},... | collective-permute-start | bytes 1179656 | tf_op jit(solution)/shard_map/ppermute | solution.py:720
  87.4 17.5 %collective-permute-start.21 = (bf16[128,1536]{1,0:T(8,128)(2,1)S(1)}, bf16[128,1536]{1,0:T(8,128)(2,1)S(1)}, u32[]{:S(2)}, u32[]{:S(2)}) collective-permute-start(bf16[128,1536]{1,0:T(8,128)(2,1)S(1)} %get-tuple-element.262), channel_id=1, source_target_pairs={{0,0},{2,8},{4,4},{6,12},{8,2},{10,10},{12,6},{14,14},{1,1},{3,9},... | collective-permute-start | bytes 1179656 | tf_op jit(solution)/shard_map/ppermute | solution.py:821
  89.4 38.3 %collective-permute-start.20 = (bf16[192,1536]{1,0:T(8,128)(2,1)S(1)}, bf16[192,1536]{1,0:T(8,128)(2,1)S(1)}, u32[]{:S(2)}, u32[]{:S(2)}) collective-permute-start(bf16[192,1536]{1,0:T(8,128)(2,1)S(1)} %collective-permute-done.16.refs_1_), channel_id=1, source_target_pairs={{0,2},{2,4},{4,6},{6,0},{1,3},{3,5},{5,7},{7,1},{8,10},{10,12},{12... | collective-permute-start | bytes 1769480 | tf_op jit(solution)/shard_map/ppermute | solution.py:725
  89.7 37.9 %collective-permute-start.19 = (bf16[192,1536]{1,0:T(8,128)(2,1)S(1)}, bf16[192,1536]{1,0:T(8,128)(2,1)S(1)}, u32[]{:S(2)}, u32[]{:S(2)}) collective-permute-start(bf16[192,1536]{1,0:T(8,128)(2,1)S(1)} %collective-permute-done.18.refs_2_), channel_id=1, source_target_pairs={{0,16},{16,0},{1,17},{17,1},{2,18},{18,2},{3,19},{19,3},{4,20},{20... | collective-permute-start | bytes 1769480 | tf_op jit(solution)/shard_map/ppermute | solution.py:720
  90.2 37.5 %collective-permute-start.17 = (bf16[192,1536]{1,0:T(8,128)(2,1)S(1)}, bf16[192,1536]{1,0:T(8,128)(2,1)S(1)}, u32[]{:S(2)}, u32[]{:S(2)}) collective-permute-start(bf16[192,1536]{1,0:T(8,128)(2,1)S(1)} %collective-permute-done.16.refs_1_), channel_id=1, source_target_pairs={{0,16},{16,0},{1,17},{17,1},{2,18},{18,2},{3,19},{19,3},{4,20},{20... | collective-permute-start | bytes 1769480 | tf_op jit(solution)/shard_map/ppermute | solution.py:720
  97.5 30.2 %collective-permute-start.22 = (bf16[128,1536]{1,0:T(8,128)(2,1)S(1)}, bf16[128,1536]{1,0:T(8,128)(2,1)S(1)}, u32[]{:S(2)}, u32[]{:S(2)}) collective-permute-start(bf16[128,1536]{1,0:T(8,128)(2,1)S(1)} %get-tuple-element.261), channel_id=1, source_target_pairs={{0,4},{2,12},{4,0},{6,8},{8,6},{10,14},{12,2},{14,10},{1,5},{3,13}... | collective-permute-start | bytes 1179656 | tf_op jit(solution)/shard_map/ppermute | solution.py:821
  128.0 23.8 %collective-permute-start.24 = (bf16[256,1536]{1,0:T(8,128)(2,1)S(1)}, bf16[256,1536]{1,0:T(8,128)(2,1)S(1)}, u32[]{:S(2)}, u32[]{:S(2)}) collective-permute-start(bf16[256,1536]{1,0:T(8,128)(2,1)S(1)} %fusion.33.refs_0_), channel_id=1, source_target_pairs={{0,1},{1,0},{2,3},{3,2},{4,5},{5,4},{6,7},{7,6},{8,9},{9,8},{10,11... | collective-permute-start | bytes 2359304 | tf_op jit(solution)/shard_map/ppermute | solution.py:720
  129.6 28.6 %collective-permute-start.26 = (bf16[256,1536]{1,0:T(8,128)(2,1)S(1)}, bf16[256,1536]{1,0:T(8,128)(2,1)S(1)}, u32[]{:S(2)}, u32[]{:S(2)}) collective-permute-start(bf16[256,1536]{1,0:T(8,128)(2,1)S(1)} %fusion.33.refs_0_), channel_id=1, source_target_pairs={{0,8},{8,0},{1,9},{9,1},{2,10},{10,2},{3,11},{11,3},{4,12},{12,4},... | collective-permute-start | bytes 2359304 | tf_op jit(solution)/shard_map/ppermute | solution.py:720
  130.2 3.7 %collective-permute-start.25 = (f32[1024,128]{1,0:T(8,128)S(1)}, f32[1024,128]{1,0:T(8,128)S(1)}, u32[]{:S(2)}, u32[]{:S(2)}) collective-permute-start(f32[1024,128]{1,0:T(8,128)S(1)} %convolution_add_fusion.4), channel_id=1, source_target_pairs={{0,8},{8,0},{1,9},{9,1},{2,10},{10,2},{3,11},{11,3},{4,12},{12,4},... | collective-permute-start | bytes 1572872 | tf_op jit(solution)/shard_map/ppermute | solution.py:720
  130.7 21.1 %collective-permute-start.23 = (bf16[192,1536]{1,0:T(8,128)(2,1)S(1)}, bf16[192,1536]{1,0:T(8,128)(2,1)S(1)}, u32[]{:S(2)}, u32[]{:S(2)}) collective-permute-start(bf16[192,1536]{1,0:T(8,128)(2,1)S(1)} %collective-permute-done.20.refs_3_), channel_id=1, source_target_pairs={{0,16},{16,0},{1,17},{17,1},{2,18},{18,2},{3,19},{19,3},{4,20},{20... | collective-permute-start | bytes 1769480 | tf_op jit(solution)/shard_map/ppermute | solution.py:720
  151.8 6.4 %collective-permute-start.27 = (bf16[256,1536]{1,0:T(8,128)(2,1)S(1)}, bf16[256,1536]{1,0:T(8,128)(2,1)S(1)}, u32[]{:S(2)}, u32[]{:S(2)}) collective-permute-start(bf16[256,1536]{1,0:T(8,128)(2,1)S(1)} %collective-permute-done.24.refs_1_), channel_id=1, source_target_pairs={{0,8},{8,0},{1,9},{9,1},{2,10},{10,2},{3,11},{11,3},{4,12},{12,4},... | collective-permute-start | bytes 2359304 | tf_op jit(solution)/shard_map/ppermute | solution.py:720
  166.4 3.7 %collective-permute-start.29 = (f32[2,1024]{1,0:T(2,128)S(1)}, f32[2,1024]{1,0:T(2,128)S(1)}, u32[]{:S(2)}, u32[]{:S(2)}) collective-permute-start(f32[2,1024]{1,0:T(2,128)S(1)} %fusion.110), channel_id=1, source_target_pairs={{0,1},{1,0},{2,3},{3,2},{4,5},{5,4},{6,7},{7,6},{8,9},{9,8},{10,11... | collective-permute-start | bytes 24584 | tf_op jit(solution)/shard_map/ppermute | solution.py:720
  185.2 8.2 %collective-permute-start.32 = (f32[512,1536]{1,0:T(8,128)}, f32[512,1536]{1,0:T(8,128)}, u32[]{:S(2)}, u32[]{:S(2)}) collective-permute-start(f32[512,1536]{1,0:T(8,128)} %get-tuple-element.120), channel_id=1, source_target_pairs={{0,8},{8,0},{1,9},{9,1},{2,10},{10,2},{3,11},{11,3},{4,12},{12,4},... | collective-permute-start | bytes 9437192 | tf_op jit(solution)/shard_map/ppermute | solution.py:720
  187.2 32.8 %collective-permute-start.30 = (bf16[2,2,2,96,768]{4,3,2,1,0:T(8,128)(2,1)}, bf16[2,2,2,96,768]{4,3,2,1,0:T(8,128)(2,1)S(1)}, u32[]{:S(2)}, u32[]{:S(2)}) collective-permute-start(bf16[2,2,2,96,768]{4,3,2,1,0:T(8,128)(2,1)} %fusion.32), channel_id=1, source_target_pairs={{0,2},{2,0},{4,6},{6,4},{1,3},{3,1},{5,7},{7,5},{8,10},{10,8},{12,... | collective-permute-start | bytes 3538952 | tf_op jit(solution)/shard_map/ppermute | solution.py:720
  191.8 28.3 %collective-permute-start.31 = (bf16[768,768]{1,0:T(8,128)(2,1)}, bf16[768,768]{1,0:T(8,128)(2,1)S(1)}, u32[]{:S(2)}, u32[]{:S(2)}) collective-permute-start(bf16[768,768]{1,0:T(8,128)(2,1)} %convolution_convert_fusion.1), channel_id=1, source_target_pairs={{0,16},{16,0},{1,17},{17,1},{2,18},{18,2},{3,19},{19,3},{4,20},{20... | collective-permute-start | bytes 3538952 | tf_op jit(solution)/shard_map/ppermute | solution.py:720
  195.2 24.9 %collective-permute-start.33 = (bf16[2,128,1536]{2,1,0:T(8,128)(2,1)S(1)}, bf16[2,128,1536]{2,1,0:T(8,128)(2,1)S(1)}, u32[]{:S(2)}, u32[]{:S(2)}) collective-permute-start(bf16[2,128,1536]{2,1,0:T(8,128)(2,1)S(1)} %fusion.35), channel_id=1, source_target_pairs={{0,1},{1,0},{2,3},{3,2},{4,5},{5,4},{6,7},{7,6},{8,9},{9,8},{10,11... | collective-permute-start | bytes 2359304 | tf_op jit(solution)/shard_map/ppermute | solution.py:720
  226.3 34.9 %collective-permute-start.35 = (bf16[2,2,96,768]{3,2,1,0:T(8,128)(2,1)}, bf16[2,2,96,768]{3,2,1,0:T(8,128)(2,1)}, u32[]{:S(2)}, u32[]{:S(2)}) collective-permute-start(bf16[2,2,96,768]{3,2,1,0:T(8,128)(2,1)} %fusion.42), channel_id=1, source_target_pairs={{0,2},{2,0},{4,6},{6,4},{1,3},{3,1},{5,7},{7,5},{8,10},{10,8},{12,... | collective-permute-start | bytes 1769480 | tf_op jit(solution)/shard_map/ppermute | solution.py:720
  229.3 31.9 %collective-permute-start.42 = (bf16[2,2,96,768]{3,2,1,0:T(8,128)(2,1)}, bf16[2,2,96,768]{3,2,1,0:T(8,128)(2,1)}, u32[]{:S(2)}, u32[]{:S(2)}) collective-permute-start(bf16[2,2,96,768]{3,2,1,0:T(8,128)(2,1)} %fusion.41), channel_id=1, source_target_pairs={{0,4},{2,6},{4,0},{6,2},{1,5},{3,7},{5,1},{7,3},{8,12},{10,14},{12... | collective-permute-start | bytes 1769480 | tf_op jit(solution)/shard_map/ppermute | solution.py:720
  230.0 5.3 %collective-permute-start.36 = (f32[512,256]{1,0:T(8,128)S(1)}, f32[512,256]{1,0:T(8,128)S(1)}, u32[]{:S(2)}, u32[]{:S(2)}) collective-permute-start(f32[512,256]{1,0:T(8,128)S(1)} %bitcast.249), channel_id=1, source_target_pairs={{0,8},{8,0},{1,9},{9,1},{2,10},{10,2},{3,11},{11,3},{4,12},{12,4},... | collective-permute-start | bytes 1572872 | tf_op jit(solution)/shard_map/ppermute | solution.py:720
  232.4 28.8 %collective-permute-start.34 = (bf16[768,768]{1,0:T(8,128)(2,1)}, bf16[768,768]{1,0:T(8,128)(2,1)}, u32[]{:S(2)}, u32[]{:S(2)}) collective-permute-start(bf16[768,768]{1,0:T(8,128)(2,1)} %convolution_convert_fusion), channel_id=1, source_target_pairs={{0,16},{16,0},{1,17},{17,1},{2,18},{18,2},{3,19},{19,3},{4,20},{20... | collective-permute-start | bytes 3538952 | tf_op jit(solution)/shard_map/ppermute | solution.py:720
  235.3 9.6 %collective-permute-start.37 = (f32[2,128,256]{2,1,0:T(8,128)S(1)}, f32[2,128,256]{2,1,0:T(8,128)S(1)}, u32[]{:S(2)}, u32[]{:S(2)}) collective-permute-start(f32[2,128,256]{2,1,0:T(8,128)S(1)} %add_bitcast_fusion), channel_id=1, source_target_pairs={{0,1},{1,0},{2,3},{3,2},{4,5},{5,4},{6,7},{7,6},{8,9},{9,8},{10,11... | collective-permute-start | bytes 786440 | tf_op jit(solution)/shard_map/ppermute | solution.py:720
  244.9 16.3 %collective-permute-start.41 = (f32[512,1536]{1,0:T(8,128)}, f32[512,1536]{1,0:T(8,128)}, u32[]{:S(2)}, u32[]{:S(2)}) collective-permute-start(f32[512,1536]{1,0:T(8,128)} %get-tuple-element.146), channel_id=1, source_target_pairs={{0,8},{8,0},{1,9},{9,1},{2,10},{10,2},{3,11},{11,3},{4,12},{12,4},... | collective-permute-start | bytes 9437192 | tf_op jit(solution)/shard_map/ppermute | solution.py:720
  248.2 5.9 %collective-permute-start.38 = (bf16[256,256]{1,0:T(8,128)(2,1)S(1)}, bf16[256,256]{1,0:T(8,128)(2,1)S(1)}, u32[]{:S(2)}, u32[]{:S(2)}) collective-permute-start(bf16[256,256]{1,0:T(8,128)(2,1)S(1)} %bitcast.244), channel_id=1, source_target_pairs={{0,1},{1,0},{2,3},{3,2},{4,5},{5,4},{6,7},{7,6},{8,9},{9,8},{10,11... | collective-permute-start | bytes 393224 | tf_op jit(solution)/shard_map/ppermute | solution.py:720
  254.1 1.3 collective-permute-start.39
  255.4 1.3 collective-permute-start.40
  263.6 37.7 %collective-permute-start.43 = (bf16[2,128,1536]{2,1,0:T(8,128)(2,1)S(1)}, bf16[2,128,1536]{2,1,0:T(8,128)(2,1)S(1)}, u32[]{:S(2)}, u32[]{:S(2)}) collective-permute-start(bf16[2,128,1536]{2,1,0:T(8,128)(2,1)S(1)} %fusion.36), channel_id=1, source_target_pairs={{0,1},{1,0},{2,3},{3,2},{4,5},{5,4},{6,7},{7,6},{8,9},{9,8},{10,11... | collective-permute-start | bytes 2359304 | tf_op jit(solution)/shard_map/ppermute | solution.py:720
  267.1 33.4 %collective-permute-start.46 = (bf16[2,2,96,768]{3,2,1,0:T(8,128)(2,1)S(1)}, bf16[2,2,96,768]{3,2,1,0:T(8,128)(2,1)S(1)}, u32[]{:S(2)}, u32[]{:S(2)}) collective-permute-start(bf16[2,2,96,768]{3,2,1,0:T(8,128)(2,1)S(1)} %fusion.43), channel_id=1, source_target_pairs={{0,2},{2,0},{4,6},{6,4},{1,3},{3,1},{5,7},{7,5},{8,10},{10,8},{12,... | collective-permute-start | bytes 1769480 | tf_op jit(solution)/shard_map/ppermute | solution.py:720
  269.1 8.9 %collective-permute-start.58 = (bf16[2,96,768]{2,1,0:T(8,128)(2,1)S(1)}, bf16[2,96,768]{2,1,0:T(8,128)(2,1)S(1)}, u32[]{:S(2)}, u32[]{:S(2)}) collective-permute-start(bf16[2,96,768]{2,1,0:T(8,128)(2,1)S(1)} %fusion.52), channel_id=1, source_target_pairs={{0,16},{16,0},{1,17},{17,1},{2,18},{18,2},{3,19},{19,3},{4,20},{20... | collective-permute-start | bytes 884744 | tf_op jit(solution)/shard_map/ppermute | solution.py:720
  269.6 22.3 %collective-permute-start.44 = (bf16[128,1536]{1,0:T(8,128)(2,1)S(1)}, bf16[128,1536]{1,0:T(8,128)(2,1)S(1)}, u32[]{:S(2)}, u32[]{:S(2)}) collective-permute-start(bf16[128,1536]{1,0:T(8,128)(2,1)S(1)} %get-tuple-element.284), channel_id=1, source_target_pairs={{0,0},{8,2},{4,4},{12,6},{2,8},{10,10},{6,12},{14,14},{1,1},{9,3},... | collective-permute-start | bytes 1179656 | tf_op jit(solution)/shard_map/ppermute | solution.py:830
  271.9 28.5 %collective-permute-start.45 = (bf16[128,1536]{1,0:T(8,128)(2,1)S(1)}, bf16[128,1536]{1,0:T(8,128)(2,1)S(1)}, u32[]{:S(2)}, u32[]{:S(2)}) collective-permute-start(bf16[128,1536]{1,0:T(8,128)(2,1)S(1)} %get-tuple-element.283), channel_id=1, source_target_pairs={{4,0},{12,2},{0,4},{8,6},{6,8},{14,10},{2,12},{10,14},{5,1},{13,3}... | collective-permute-start | bytes 1179656 | tf_op jit(solution)/shard_map/ppermute | solution.py:830
  278.0 22.5 %collective-permute-start.47 = (bf16[768,256]{0,1:T(8,128)(2,1)S(1)}, bf16[768,256]{0,1:T(8,128)(2,1)S(1)}, u32[]{:S(2)}, u32[]{:S(2)}) collective-permute-start(bf16[768,256]{0,1:T(8,128)(2,1)S(1)} %pad_maximum_fusion.9), channel_id=1, source_target_pairs={{0,16},{16,0},{1,17},{17,1},{2,18},{18,2},{3,19},{19,3},{4,20},{20... | collective-permute-start | bytes 1179656 | tf_op jit(solution)/shard_map/ppermute | solution.py:720
  291.9 21.5 %collective-permute-start.52 = (bf16[2,96,768]{2,1,0:T(8,128)(2,1)}, bf16[2,96,768]{2,1,0:T(8,128)(2,1)}, u32[]{:S(2)}, u32[]{:S(2)}) collective-permute-start(bf16[2,96,768]{2,1,0:T(8,128)(2,1)} %fusion.50), channel_id=1, source_target_pairs={{0,4},{2,6},{4,0},{6,2},{1,5},{3,7},{5,1},{7,3},{8,12},{10,14},{12... | collective-permute-start | bytes 884744 | tf_op jit(solution)/shard_map/ppermute | solution.py:720
  304.1 5.8 %collective-permute-start.48 = (f32[14,256]{1,0:T(8,128)S(1)}, f32[14,256]{1,0:T(8,128)S(1)}, u32[]{:S(2)}, u32[]{:S(2)}) collective-permute-start(f32[14,256]{1,0:T(8,128)S(1)} %pad_maximum_fusion.13), channel_id=1, source_target_pairs={{0,1},{1,0},{2,3},{3,2},{4,5},{5,4},{6,7},{7,6},{8,9},{9,8},{10,11... | collective-permute-start | bytes 43016 | tf_op jit(solution)/shard_map/ppermute | solution.py:720
  306.9 6.5 %collective-permute-start.53 = (bf16[2,2,96,256]{3,2,1,0:T(8,128)(2,1)S(1)}, bf16[2,2,96,256]{3,2,1,0:T(8,128)(2,1)S(1)}, u32[]{:S(2)}, u32[]{:S(2)}) collective-permute-start(bf16[2,2,96,256]{3,2,1,0:T(8,128)(2,1)S(1)} %fusion.86), channel_id=1, source_target_pairs={{0,2},{2,0},{4,6},{6,4},{1,3},{3,1},{5,7},{7,5},{8,10},{10,8},{12,... | collective-permute-start | bytes 589832 | tf_op jit(solution)/shard_map/ppermute | solution.py:720
  307.0 13.3 %collective-permute-start.49 = (bf16[128,1536]{1,0:T(8,128)(2,1)S(1)}, bf16[128,1536]{1,0:T(8,128)(2,1)S(1)}, u32[]{:S(2)}, u32[]{:S(2)}) collective-permute-start(bf16[128,1536]{1,0:T(8,128)(2,1)S(1)} %get-tuple-element.278), channel_id=1, source_target_pairs={{0,0},{8,2},{4,4},{12,6},{2,8},{10,10},{6,12},{14,14},{1,1},{9,3},... | collective-permute-start | bytes 1179656 | tf_op jit(solution)/shard_map/ppermute | solution.py:830
  308.9 18.8 %collective-permute-start.50 = (bf16[128,1536]{1,0:T(8,128)(2,1)S(1)}, bf16[128,1536]{1,0:T(8,128)(2,1)S(1)}, u32[]{:S(2)}, u32[]{:S(2)}) collective-permute-start(bf16[128,1536]{1,0:T(8,128)(2,1)S(1)} %get-tuple-element.277), channel_id=1, source_target_pairs={{4,0},{12,2},{0,4},{8,6},{6,8},{14,10},{2,12},{10,14},{5,1},{13,3}... | collective-permute-start | bytes 1179656 | tf_op jit(solution)/shard_map/ppermute | solution.py:830
  311.2 19.6 %collective-permute-start.51 = (bf16[256,1536]{1,0:T(8,128)(2,1)S(1)}, bf16[256,1536]{1,0:T(8,128)(2,1)S(1)}, u32[]{:S(2)}, u32[]{:S(2)}) collective-permute-start(bf16[256,1536]{1,0:T(8,128)(2,1)S(1)} %constant_dynamic-update-slice_fusion.refs_0_), channel_id=1, source_target_pairs={{0,1},{1,0},{2,3},{3,2},{4,5},{5,4},{6,7},{7,6},{8,9},{9,8},{10,11... | collective-permute-start | bytes 2359304 | tf_op jit(solution)/shard_map/ppermute | solution.py:720
  313.4 29.0 %collective-permute-start.59 = (f32[96,768]{1,0:T(8,128)S(1)}, f32[96,768]{1,0:T(8,128)S(1)}, u32[]{:S(2)}, u32[]{:S(2)}) collective-permute-start(f32[96,768]{1,0:T(8,128)S(1)} %copy-done.76), channel_id=1, source_target_pairs={{0,8},{8,0},{1,9},{9,1},{2,10},{10,2},{3,11},{11,3},{4,12},{12,4},... | collective-permute-start | bytes 884744 | tf_op jit(solution)/shard_map/ppermute | solution.py:720
  330.9 22.8 %collective-permute-start.55 = (bf16[256,1536]{1,0:T(8,128)(2,1)S(1)}, bf16[256,1536]{1,0:T(8,128)(2,1)S(1)}, u32[]{:S(2)}, u32[]{:S(2)}) collective-permute-start(bf16[256,1536]{1,0:T(8,128)(2,1)S(1)} %constant_dynamic-update-slice_fusion.2.refs_0_), channel_id=1, source_target_pairs={{0,1},{1,0},{2,3},{3,2},{4,5},{5,4},{6,7},{7,6},{8,9},{9,8},{10,11... | collective-permute-start | bytes 2359304 | tf_op jit(solution)/shard_map/ppermute | solution.py:720
  333.5 8.0 %collective-permute-start.63 = (f32[96,768]{1,0:T(8,128)S(1)}, f32[96,768]{1,0:T(8,128)S(1)}, u32[]{:S(2)}, u32[]{:S(2)}) collective-permute-start(f32[96,768]{1,0:T(8,128)S(1)} %dynamic-slice_bitcast_fusion.5), channel_id=1, source_target_pairs={{0,8},{8,0},{1,9},{9,1},{2,10},{10,2},{3,11},{11,3},{4,12},{12,4},... | collective-permute-start | bytes 884744 | tf_op jit(solution)/shard_map/ppermute | solution.py:720
  333.7 5.9 %collective-permute-start.60 = (f32[62,256]{1,0:T(8,128)S(1)}, f32[62,256]{1,0:T(8,128)S(1)}, u32[]{:S(2)}, u32[]{:S(2)}) collective-permute-start(f32[62,256]{1,0:T(8,128)S(1)} %pad_maximum_fusion.11), channel_id=1, source_target_pairs={{0,16},{16,0},{1,17},{17,1},{2,18},{18,2},{3,19},{19,3},{4,20},{20... | collective-permute-start | bytes 190472 | tf_op jit(solution)/shard_map/ppermute | solution.py:720
  333.8 17.7 %collective-permute-start.56 = (bf16[2,96,768]{2,1,0:T(8,128)(2,1)S(1)}, bf16[2,96,768]{2,1,0:T(8,128)(2,1)S(1)}, u32[]{:S(2)}, u32[]{:S(2)}) collective-permute-start(bf16[2,96,768]{2,1,0:T(8,128)(2,1)S(1)} %fusion.51), channel_id=1, source_target_pairs={{0,4},{2,6},{4,0},{6,2},{1,5},{3,7},{5,1},{7,3},{8,12},{10,14},{12... | collective-permute-start | bytes 884744 | tf_op jit(solution)/shard_map/ppermute | solution.py:720
  339.6 14.0 %collective-permute-start.57 = (bf16[2,96,256]{2,1,0:T(8,128)(2,1)S(1)}, bf16[2,96,256]{2,1,0:T(8,128)(2,1)S(1)}, u32[]{:S(2)}, u32[]{:S(2)}) collective-permute-start(bf16[2,96,256]{2,1,0:T(8,128)(2,1)S(1)} %fusion.87), channel_id=1, source_target_pairs={{0,4},{2,6},{4,0},{6,2},{1,5},{3,7},{5,1},{7,3},{8,12},{10,14},{12... | collective-permute-start | bytes 294920 | tf_op jit(solution)/shard_map/ppermute | solution.py:720
  353.7 8.4 %collective-permute-start.65 = (f32[96,256]{1,0:T(8,128)S(1)}, f32[96,256]{1,0:T(8,128)S(1)}, u32[]{:S(2)}, u32[]{:S(2)}) collective-permute-start(f32[96,256]{1,0:T(8,128)S(1)} %get-tuple-element.308), channel_id=1, source_target_pairs={{0,8},{8,0},{1,9},{9,1},{2,10},{10,2},{3,11},{11,3},{4,12},{12,4},... | collective-permute-start | bytes 294920 | tf_op jit(solution)/shard_map/ppermute | solution.py:720
  353.9 15.4 %collective-permute-start.64 = (f32[96,768]{1,0:T(8,128)S(1)}, f32[96,768]{1,0:T(8,128)S(1)}, u32[]{:S(2)}, u32[]{:S(2)}) collective-permute-start(f32[96,768]{1,0:T(8,128)S(1)} %dynamic-slice_bitcast_fusion.4), channel_id=1, source_target_pairs={{0,8},{8,0},{1,9},{9,1},{2,10},{10,2},{3,11},{11,3},{4,12},{12,4},... | collective-permute-start | bytes 884744 | tf_op jit(solution)/shard_map/ppermute | solution.py:720
  354.5 5.6 %collective-permute-start.61 = (f32[62,256]{1,0:T(8,128)S(1)}, f32[62,256]{1,0:T(8,128)S(1)}, u32[]{:S(2)}, u32[]{:S(2)}) collective-permute-start(f32[62,256]{1,0:T(8,128)S(1)} %add.556), channel_id=1, source_target_pairs={{0,2},{2,0},{4,6},{6,4},{1,3},{3,1},{5,7},{7,5},{8,10},{10,8},{12,... | collective-permute-start | bytes 190472 | tf_op jit(solution)/shard_map/ppermute | solution.py:720
  360.1 5.3 %collective-permute-start.62 = (f32[62,256]{1,0:T(8,128)S(1)}, f32[62,256]{1,0:T(8,128)S(1)}, u32[]{:S(2)}, u32[]{:S(2)}) collective-permute-start(f32[62,256]{1,0:T(8,128)S(1)} %add.557), channel_id=1, source_target_pairs={{0,4},{2,6},{4,0},{6,2},{1,5},{3,7},{5,1},{7,3},{8,12},{10,14},{12... | collective-permute-start | bytes 190472 | tf_op jit(solution)/shard_map/ppermute | solution.py:720
  (86 other events, 797.2 us)
